TPU v7x, 32 devices: a whole 2x2x4 slice. The times are simulated.
32 devices in a mesh: row: 4 (over y, x), col: 8 (over z, core).
Axes of the slice: x: 2, y: 2, z: 4, core: 2. Of those that a mesh axis runs over, the one named last changes fastest.
Arguments:
- activations: bfloat16 [8, 256, 8192], P('row')
- out_grads: bfloat16 [8, 256, 28672], P('row', None, 'col')
- valid_len: int32 [8], P('row'), may hold values from 1 to 256, 1024 in all
- weight: bfloat16 [8192, 28672], P('row', 'col'), may hold values from -0.0625 to 0.0625
- sketch: bfloat16 [28672, 512], P('col'), may hold values from -6 to 6
Outputs:
- basis: float32 [8192, 512], P(('row', 'col'))
- coeffs: float32 [512, 28672], P('row', 'col')
Inputs may be any that keep to these rules, and one draw needn't show every extreme that they name: `valid_len`: valid tokens of each sequence; at least one sequence fills all 256 slots.
All inputs are finite; a program needn't handle non-finite values. No bound on the sum of `valid_len` on one device may be relied on, other than what follows from the above.
Results may differ from a plain program's by a relative error of at most 0.01.
Values may be sent and summed in bfloat16 or wider, within the bound.
No kernel may reach another device: no remote copies, remote signals or barrier semaphores. Data moves between devices by JAX's collectives and lax.ppermute only.
A program may use at most 128 MiB of HBM per device.

v0:
```python
import functools
import math

import jax
import jax.numpy as jnp
from jax import lax
from jax.experimental import pallas as pl
from jax.experimental.pallas import tpu as pltpu
from jax.sharding import PartitionSpec as P

AXES = ("row", "col")
F32 = jnp.float32
BF16 = jnp.bfloat16


def swap(block, row_bit, col_bit):
    rows, cols = lax.axis_size("row"), lax.axis_size("col")
    pairs = []
    for row in range(rows):
        for col in range(cols):
            other = (row ^ row_bit(col & 1)) * cols + (col ^ col_bit(col & 1))
            pairs.append((row * cols + col, other))
    return lax.ppermute(block, AXES, pairs)


class Halving:
    def __init__(self, axis):
        self.axis = axis
        self.size = lax.axis_size(axis)
        bits = list(range(self.size.bit_length() - 1))
        if axis == "col":
            self.orders = (bits, bits[:1] + bits[:0:-1])
        else:
            self.orders = (bits, bits[::-1])
        self.me = lax.axis_index(axis)
        self.odd = lax.axis_index("col") & 1
        steps = len(bits)
        self.masks = tuple(
            [
                sum(1 << order[t] for t in range(steps) if v >> (steps - 1 - t) & 1)
                for v in range(self.size)
            ]
            for order in self.orders
        )
        if axis == "col":
            half = self.size // 2
            even, odd = (masks[:half] for masks in self.masks)
            self.masks = (even + [1 ^ mask for mask in odd], odd + [1 ^ mask for mask in even])

    def block(self, v):
        even, odd = (masks[v] for masks in self.masks)
        return self.me ^ (even if even == odd else jnp.where(self.odd == 0, even, odd))

    def step(self, t, block):
        even, odd = (1 << order[t] for order in self.orders)
        pick = lambda parity: odd if parity else even
        none = lambda parity: 0
        return swap(block, *((none, pick) if self.axis == "col" else (pick, none)))

    def sending_first(self):
        half = self.size // 2
        places = [*range(half, self.size), *range(half)]
        return jnp.stack([self.block(v) for v in places]).astype(jnp.int32)

    def scatter_sum(self, send, keep):
        for t in range(len(self.orders[0])):
            now = keep.astype(F32) + self.step(t, send).astype(F32)
            half = now.shape[0] // 2
            send, keep = now[half:].astype(BF16), now[:half]
        return keep[0] if keep.shape[0] else now[0]

    def gather(self, own):
        now = own[None]
        for t in reversed(range(len(self.orders[0]))):
            came = self.step(t, now)
            if t:
                now = jnp.concatenate([now, came])
        return now, came

    def in_order(self, halves, axis):
        virtual = jnp.concatenate(halves)
        places = []
        for masks in self.masks:
            inverse = [0] * self.size
            for v, mask in enumerate(masks):
                inverse[mask] = v
            places.append(jnp.array(inverse, jnp.int32))
        place = jnp.where(self.odd == 0, places[0], places[1])
        take = lambda j: lax.dynamic_index_in_dim(
            virtual, place[self.me ^ j], 0, keepdims=False
        )
        return jnp.concatenate([take(j) for j in range(self.size)], axis)


def sum_everywhere(value, row=True, col=True):
    none = lambda parity: 0
    if col:
        for bit in range(lax.axis_size("col").bit_length() - 1):
            value = value + swap(value, none, lambda parity: 1 << bit)
    if row:
        steps = lax.axis_size("row").bit_length() - 1
        for t in range(steps):
            pick = lambda parity: 1 << (steps - 1 - t if parity else t)
            value = value + swap(value, pick, none)
    return value


def token_gram_kernel(valid_ref, grads_ref, gram_ref, scale_ref):
    seq = pl.program_id(0)
    length = grads_ref.shape[1]
    tokens = lax.broadcasted_iota(jnp.int32, (length, 1), 0)
    grads = grads_ref[0].astype(F32)
    grads = jnp.where(tokens < valid_ref[seq], grads, 0.0)
    largest = jnp.max(jnp.abs(grads), axis=1, keepdims=True)
    scale = jnp.ones_like(largest)
    shrink = jnp.ones_like(largest)
    for power in (16, 48, 80):
        step = 2.0 ** (power + 16)
        high, low = largest >= 2.0**power, largest < 2.0**-power
        scale = jnp.where(high, step, jnp.where(low, 1.0 / step, scale))
        shrink = jnp.where(high, 1.0 / step, jnp.where(low, step, shrink))
    near = (grads * shrink).astype(BF16)
    gram = lax.dot_general(near, near, (((1,), (1,)), ((), ())), preferred_element_type=F32)
    high = gram.astype(BF16)
    gram_ref[0, :length] = high
    gram_ref[0, length:] = (gram - high.astype(F32)).astype(BF16)
    scale_ref[0] = jnp.broadcast_to(scale, (length, 128))


def row_mass_kernel(acts_ref, gram_ref, scale_ref, mass_ref):
    length = acts_ref.shape[1]
    total = jnp.zeros((1, acts_ref.shape[2]), F32)
    for seq in range(acts_ref.shape[0]):
        acts = acts_ref[seq].astype(F32) * scale_ref[seq][:, :1]
        spread = jnp.dot(gram_ref[seq], acts.astype(BF16), preferred_element_type=F32)
        spread = spread[:length] + spread[length:]
        total = total + jnp.sum(spread * acts, axis=0, keepdims=True)
    mass_ref[...] = total


def local_mass(activations, out_grads, valid_len):
    seqs, length, width = activations.shape
    cols = out_grads.shape[2]
    whole = lambda seq, valid: (seq, 0, 0)
    gram, scale = pl.pallas_call(
        token_gram_kernel,
        out_shape=(
            jax.ShapeDtypeStruct((seqs, 2 * length, length), BF16),
            jax.ShapeDtypeStruct((seqs, length, 128), F32),
        ),
        grid_spec=pltpu.PrefetchScalarGridSpec(
            num_scalar_prefetch=1,
            grid=(seqs,),
            in_specs=[pl.BlockSpec((1, length, cols), whole)],
            out_specs=(
                pl.BlockSpec((1, 2 * length, length), whole),
                pl.BlockSpec((1, length, 128), whole),
            ),
        ),
        compiler_params=pltpu.CompilerParams(vmem_limit_bytes=48 << 20),
        cost_estimate=pl.CostEstimate(
            flops=2 * seqs * length * length * cols,
            bytes_accessed=2 * out_grads.size,
            transcendentals=0,
        ),
        name="token_gram",
    )(valid_len, out_grads)
    tile = math.gcd(width, 1024)
    fixed = lambda i: (0, 0, 0)
    mass = pl.pallas_call(
        row_mass_kernel,
        out_shape=jax.ShapeDtypeStruct((1, width), F32),
        grid=(width // tile,),
        in_specs=[
            pl.BlockSpec((seqs, length, tile), lambda i: (0, 0, i)),
            pl.BlockSpec((seqs, 2 * length, length), fixed),
            pl.BlockSpec((seqs, length, 128), fixed),
        ],
        out_specs=pl.BlockSpec((1, tile), lambda i: (0, i)),
        compiler_params=pltpu.CompilerParams(vmem_limit_bytes=48 << 20),
        cost_estimate=pl.CostEstimate(
            flops=4 * seqs * length * length * width,
            bytes_accessed=2 * activations.size,
            transcendentals=0,
        ),
        name="row_mass",
    )(activations, gram, scale)
    return mass.reshape(width)


def invert_block(tile):
    size = tile.shape[0]
    groups = [tile[i : i + 8] for i in range(0, size, 8)]
    lane = lax.broadcasted_iota(jnp.int32, (8, size), 1)
    sub = lax.broadcasted_iota(jnp.int32, (8, size), 0)
    done = []
    for g in range(size // 8):
        base = 8 * g
        inside = (lane >= base) & (lane < base + 8)
        now = groups[g]
        column = [jnp.broadcast_to(now[:, base + j : base + j + 1], (8, size)) for j in range(8)]
        now = jnp.where(inside, jnp.where(lane - base == sub, 1.0, 0.0), now)
        out = jnp.zeros((8, size), F32)
        for k in range(8):
            here = sub == k
            pivot = jnp.broadcast_to(column[k][k : k + 1], (8, size))
            row = jnp.broadcast_to(now[k : k + 1], (8, size))
            out = jnp.where(here, row * lax.rsqrt(pivot), out)
            inverse = 1.0 / pivot
            row = row * inverse
            now = jnp.where(here, row, now - column[k] * row)
            for j in range(k + 1, 8):
                part = jnp.broadcast_to(column[j][k : k + 1], (8, size)) * inverse
                column[j] = jnp.where(here, part, column[j] - column[k] * part)
        done.append(jnp.where(lane < base + 8, out, 0.0))
        rows = [jnp.broadcast_to(now[s : s + 1], (8, size)) for s in range(8)]
        for i in range(g + 1, size // 8):
            left = groups[i]
            kept = jnp.where(inside, 0.0, left)
            for s in range(8):
                weight = jnp.broadcast_to(left[:, base + s : base + s + 1], (8, size))
                kept = kept - weight * rows[s]
            groups[i] = kept
    return jnp.concatenate(done)


def inverse_factor_kernel(gram_ref, out_ref, work_ref):
    size = gram_ref.shape[0]
    block = 128
    count = size // block
    work_ref[...] = gram_ref[...]
    lane = lax.broadcasted_iota(jnp.int32, (block, size), 1)

    def step(k, carry):
        base = pl.multiple_of(k * block, block)
        here = pl.ds(base, block)
        small = invert_block(work_ref[here, here])
        inside = (lane >= base) & (lane < base + block)
        eye = lax.broadcasted_iota(jnp.int32, (block, size), 0) == lane - base
        rows = jnp.where(inside, jnp.where(eye, 1.0, 0.0), work_ref[here, :])
        rows = jnp.dot(small, rows, precision=lax.Precision.HIGHEST, preferred_element_type=F32)
        out_ref[here, :] = jnp.where(lane < base + block, rows, 0.0)
        work_ref[here, :] = rows

        def update(i, carry):
            there = pl.ds(pl.multiple_of(i * block, block), block)
            left = work_ref[here, there]
            old = jnp.where(inside, 0.0, work_ref[there, :])
            work_ref[there, :] = old - lax.dot_general(
                left,
                rows,
                (((0,), (0,)), ((), ())),
                precision=lax.Precision.HIGHEST,
                preferred_element_type=F32,
            )
            return carry

        return lax.fori_loop(k + 1, count, update, carry)

    lax.fori_loop(0, count, step, 0)


def inverse_factor(gram):
    size = gram.shape[0]
    return pl.pallas_call(
        inverse_factor_kernel,
        out_shape=jax.ShapeDtypeStruct((size, size), F32),
        in_specs=[pl.BlockSpec(memory_space=pltpu.VMEM)],
        out_specs=pl.BlockSpec(memory_space=pltpu.VMEM),
        scratch_shapes=[pltpu.VMEM((size, size), F32)],
        compiler_params=pltpu.CompilerParams(vmem_limit_bytes=32 << 20),
        cost_estimate=pl.CostEstimate(
            flops=40 * size**3, bytes_accessed=8 * size * size, transcendentals=size
        ),
        name="inverse_factor",
    )(gram)


LIMIT = 56 << 20


def dot(left, right, dims=((1,), (0,))):
    return lax.dot_general(left, right, (dims, ((), ())), preferred_element_type=F32)


NT = ((1,), (1,))


def gather_rows(order_ref, sum_ref, send_ref, keep_ref, turned):
    half = send_ref.shape[0]
    block = sum_ref.shape[0] // (2 * half)
    for i in range(2 * half):
        here = pl.ds(pl.multiple_of(order_ref[i] * block, block), block)
        value = sum_ref[here, :]
        target = send_ref if i < half else keep_ref
        target[i % half] = value.T if turned else value


def add_up(step, term, sum_ref):
    @pl.when(step == 0)
    def _():
        sum_ref[...] = term

    @pl.when(step > 0)
    def _():
        sum_ref[...] += term


def rows_plain_kernel(turned, order_ref, weight_ref, right_ref, send_ref, keep_ref, sum_ref):
    step = pl.program_id(0)
    add_up(step, dot(weight_ref[...], right_ref[...]), sum_ref)

    @pl.when(step == pl.num_programs(0) - 1)
    def _():
        gather_rows(order_ref, sum_ref, send_ref, keep_ref, turned)


def two_halves(size, shape, send_type):
    dims = (size // 2,) + shape
    shapes = (jax.ShapeDtypeStruct(dims, send_type), jax.ShapeDtypeStruct(dims, F32))
    return shapes, (pl.BlockSpec(dims, lambda *_: (0, 0, 0)),) * 2


def rows_times(weight, right, part, width, rows, turned):
    height, depth = weight.shape
    block = height // rows.size
    chunk = 512 if depth % 512 == 0 else depth
    shapes, specs = two_halves(rows.size, (width, block) if turned else (block, width), F32)
    return pl.pallas_call(
        functools.partial(rows_plain_kernel, turned),
        out_shape=shapes,
        grid_spec=pltpu.PrefetchScalarGridSpec(
            num_scalar_prefetch=1,
            grid=(depth // chunk,),
            in_specs=[
                pl.BlockSpec((height, chunk), lambda i, order: (0, i)),
                pl.BlockSpec((chunk, width), lambda i, order: (i, part)),
            ],
            out_specs=specs,
            scratch_shapes=[pltpu.VMEM((height, width), F32)],
        ),
        compiler_params=pltpu.CompilerParams(vmem_limit_bytes=LIMIT),
        cost_estimate=pl.CostEstimate(
            flops=2 * height * depth * width,
            bytes_accessed=2 * (height + width) * depth,
            transcendentals=0,
        ),
        name="rows_times",
    )(rows.sending_first(), weight, right)


def rows_joined_kernel(rows_ref, cols_ref, weight_ref, first_ref, second_ref, send_ref, keep_ref, sum_ref):
    step, steps = pl.program_id(0), pl.num_programs(0)
    right = jnp.where(step < steps // 2, first_ref[0], second_ref[0])
    add_up(step, dot(weight_ref[...], right, NT), sum_ref)

    @pl.when(step == steps - 1)
    def _():
        gather_rows(rows_ref, sum_ref, send_ref, keep_ref, False)


def rows_times_joined(weight, halves, rows, cols):
    height, depth = weight.shape
    block = height // rows.size
    half, width, own = halves[0].shape
    if own % 128:
        return rows_times(weight, cols.in_order(halves, 1).T, 0, width, rows, False)
    shapes, specs = two_halves(rows.size, (block, width), F32)
    return pl.pallas_call(
        rows_joined_kernel,
        out_shape=shapes,
        grid_spec=pltpu.PrefetchScalarGridSpec(
            num_scalar_prefetch=2,
            grid=(cols.size,),
            in_specs=[
                pl.BlockSpec(
                    (height, own), lambda i, _, order: (0, order[(i + half) % (2 * half)])
                ),
                pl.BlockSpec((1, width, own), lambda i, *_: (jnp.minimum(i, half - 1), 0, 0)),
                pl.BlockSpec((1, width, own), lambda i, *_: (jnp.maximum(i - half, 0), 0, 0)),
            ],
            out_specs=specs,
            scratch_shapes=[pltpu.VMEM((height, width), F32)],
        ),
        compiler_params=pltpu.CompilerParams(vmem_limit_bytes=LIMIT),
        cost_estimate=pl.CostEstimate(
            flops=2 * height * depth * width,
            bytes_accessed=2 * (height + width) * depth,
            transcendentals=0,
        ),
        name="rows_times_joined",
    )(rows.sending_first(), cols.sending_first(), weight, *halves)


def put(value, send_ref, keep_ref):
    step, half = pl.program_id(0), pl.num_programs(0) // 2

    @pl.when(step < half)
    def _():
        send_ref[0] = value.astype(send_ref.dtype)

    @pl.when(step >= half)
    def _():
        keep_ref[0] = value.astype(keep_ref.dtype)


def halves_out(size, shape, send_type):
    half = size // 2
    dims = (half,) + shape
    shapes = (jax.ShapeDtypeStruct(dims, send_type), jax.ShapeDtypeStruct(dims, F32))
    specs = (
        pl.BlockSpec((1,) + shape, lambda i, *_: (jnp.minimum(i, half - 1), 0, 0)),
        pl.BlockSpec((1,) + shape, lambda i, *_: (jnp.maximum(i - half, 0), 0, 0)),
    )
    return shapes, specs


def join(order_ref, halves, whole_ref, width):
    @pl.when(pl.program_id(0) == 0)
    def _():
        count = halves[0].shape[0]
        for v in range(2 * count):
            block = order_ref[(v + count) % (2 * count)]
            there = pl.ds(pl.multiple_of(block * width, 128), width)
            whole_ref[:, there] = halves[v // count][v % count]


def cols_kernel(cols_ref, rows_ref, weight_ref, first_ref, second_ref, send_ref, keep_ref, whole_ref):
    join(rows_ref, (first_ref, second_ref), whole_ref, first_ref.shape[2])
    put(dot(whole_ref[...], weight_ref[...]), send_ref, keep_ref)


def cols_times_joined(weight, halves, rows, cols):
    height, depth = weight.shape
    block = depth // cols.size
    width, own = halves[0].shape[1:]
    if own % 128 or block % 128:
        full = dot(rows.in_order(halves, 1), weight).reshape(width, cols.size, block)
        order = cols.sending_first()
        full = jnp.stack([full[:, order[i]] for i in range(cols.size)])
        return full[: cols.size // 2].astype(BF16), full[cols.size // 2 :]
    shapes, specs = halves_out(cols.size, (width, block), BF16)
    fixed = pl.BlockSpec(halves[0].shape, lambda i, *_: (0, 0, 0))
    return pl.pallas_call(
        cols_kernel,
        out_shape=shapes,
        grid_spec=pltpu.PrefetchScalarGridSpec(
            num_scalar_prefetch=2,
            grid=(cols.size,),
            in_specs=[pl.BlockSpec((height, block), lambda i, order, _: (0, order[i])), fixed, fixed],
            out_specs=specs,
            scratch_shapes=[pltpu.VMEM((width, height), BF16)],
        ),
        compiler_params=pltpu.CompilerParams(vmem_limit_bytes=LIMIT),
        cost_estimate=pl.CostEstimate(
            flops=2 * height * depth * width,
            bytes_accessed=2 * (height + width) * depth,
            transcendentals=0,
        ),
        name="cols_times_joined",
    )(cols.sending_first(), rows.sending_first(), weight, *halves)


def settle_kernel(order_ref, *refs):
    out_ref = refs[-1]
    count, block, half = refs[0].shape
    for v in range(2 * count):
        at = order_ref[(v + count) % (2 * count)] * block
        there = pl.ds(pl.multiple_of(at, block), block)
        for part in range(2):
            out_ref[there, part * half : (part + 1) * half] = refs[2 * part + v // count][v % count]


def settle(left, right, rows):
    count, block, half = left[0].shape
    if half % 128 or block % 16:
        return jnp.concatenate([rows.in_order(side, 0) for side in (left, right)], 1)
    vmem = pl.BlockSpec(memory_space=pltpu.VMEM)
    return pl.pallas_call(
        settle_kernel,
        out_shape=jax.ShapeDtypeStruct((2 * count * block, 2 * half), BF16),
        in_specs=[pl.BlockSpec(memory_space=pltpu.SMEM)] + [vmem] * 4,
        out_specs=vmem,
        compiler_params=pltpu.CompilerParams(vmem_limit_bytes=LIMIT),
        cost_estimate=pl.CostEstimate(
            flops=0, bytes_accessed=16 * count * block * half, transcendentals=0
        ),
        name="settle",
    )(rows.sending_first(), *left, *right)


def split(value):
    high = lax.reduce_precision(value, 8, 7)
    return high.astype(BF16), (value - high).astype(BF16)


def local(activations, out_grads, valid_len, weight, sketch):
    width = activations.shape[2]
    rows_here, cols_here = weight.shape
    rank = sketch.shape[1]
    half = rank // 2
    row_count, col_count = lax.axis_size("row"), lax.axis_size("col")
    row, col = lax.axis_index("row"), lax.axis_index("col")
    own_rows = rows_here // col_count
    over_col, over_row = Halving("col"), Halving("row")

    mass = local_mass(activations, out_grads, valid_len)
    mass, sketch = lax.optimization_barrier((mass, sketch))
    fisher = sum_everywhere(mass.reshape(-1, 128)).reshape(width)
    mean = jnp.sum(fisher) / width + 1e-06
    square_scale = lax.dynamic_slice_in_dim(fisher, row * rows_here, rows_here) / mean
    own_square = lax.dynamic_slice_in_dim(square_scale, col * own_rows, own_rows)

    def second_of(part):
        raw = over_col.scatter_sum(*rows_times(weight, sketch, part, half, over_col, True))
        first = (own_square * raw).astype(BF16)
        parts = cols_times_joined(weight, over_col.gather(first), over_col, over_row)
        projected = over_row.gather(over_row.scatter_sum(*parts).astype(BF16))
        parts = rows_times_joined(weight, projected, over_col, over_row)
        return over_col.gather(over_col.scatter_sum(*parts).astype(BF16))

    second = settle(second_of(0), second_of(1), over_col)

    even = (col & 1) == 0
    mine = lax.dynamic_slice_in_dim(second, (col & 1) * half, half, 1).astype(F32)
    rows_of = ((0,), (0,))
    gram = sum(dot(term, second, rows_of) for term in split(square_scale[:, None] * mine))
    gram = sum_everywhere(gram, col=False)
    other = swap(gram, lambda parity: 0, lambda parity: 1)
    gram = jnp.concatenate([jnp.where(even, gram, other), jnp.where(even, other, gram)])

    high, low = split(inverse_factor(gram))
    basis = dot(second, high, NT) + dot(second, low, NT)
    parts = dot((square_scale[:, None] * basis).astype(BF16), weight, rows_of).astype(BF16)
    parts = parts.reshape(row_count, rank // row_count, cols_here)
    order = over_row.sending_first()
    take = lambda places: jnp.stack(
        [lax.dynamic_index_in_dim(parts, order[i], 0, keepdims=False) for i in places]
    )
    coeffs = over_row.scatter_sum(
        take(range(row_count // 2)), take(range(row_count // 2, row_count))
    )

    basis = lax.dynamic_slice_in_dim(basis, col * own_rows, own_rows)
    basis = basis * (jnp.sqrt(own_square)[:, None] * math.sqrt(width))
    return basis, coeffs * math.sqrt(cols_here * col_count)


def solution(mesh):
    placed = (
        P("row", None, None),
        P("row", None, "col"),
        P("row"),
        P("row", "col"),
        P("col", None),
    )
    return jax.shard_map(
        local,
        mesh=mesh,
        in_specs=placed,
        out_specs=(P(("row", "col"), None), P("row", "col")),
        check_vma=False,
    )
```

profile of v0, /device:TPU:0, one launch (start us, length us, event | category | flops | bytes accessed | tf_op | source)
XLA Modules:
  0.0 356.7 jit_solution(1612429164731586352)
XLA Ops:
  6.0 9.3 %row_mass.1 = f32[1,8192]{1,0:T(1,128)S(1)} custom-call(bf16[2,256,8192]{2,1,0:T(8,128)(2,1)} %acts_ref.1, bf16[2,512,256]{2,1,0:T(8,128)(2,1)S(1)} %get-tuple-element.18.gram_ref, f32[2,256,128]{2,1,0:T(8,128)S(1)} %get-tuple-element.19.scale_ref), custom_call_target="tpu_custom_call" | custom-call | flops 4294967296 | bytes 8388608 | tf_op jit(solution)/shard_map/row_mass/pallas_call | solution.py:170
  16.0 12.8 %rows_times.3 = (f32[4,256,256]{2,1,0:T(8,128)}, f32[4,256,256]{2,1,0:T(8,128)}) custom-call(s32[8]{0:T(128)} %stack.40.order_ref.rows_ref, bf16[2048,3584]{1,0:T(8,128)(2,1)} %weight_ref.11, bf16[3584,512]{1,0:T(8,128)(2,1)} %right_ref.1), custom_call_target="tpu_custom_call" | custom-call | flops 3758096384 | bytes 16515072 | tf_op jit(solution)/shard_map/rows_times/pallas_call | solution.py:329
  29.3 12.7 %rows_times.2 = (f32[4,256,256]{2,1,0:T(8,128)}, f32[4,256,256]{2,1,0:T(8,128)}) custom-call(s32[8]{0:T(128)} %stack.40.order_ref.rows_ref, bf16[2048,3584]{1,0:T(8,128)(2,1)} %weight_ref.11, bf16[3584,512]{1,0:T(8,128)(2,1)} %right_ref.1), custom_call_target="tpu_custom_call" | custom-call | flops 3758096384 | bytes 16515072 | tf_op jit(solution)/shard_map/rows_times/pallas_call | solution.py:329
  70.8 5.5 %collective-permute-done.6 = bf16[2,256,256]{2,1,0:T(8,128)(2,1)} collective-permute-done((bf16[2,256,256]{2,1,0:T(8,128)(2,1)S(1)}, bf16[2,256,256]{2,1,0:T(8,128)(2,1)}, u32[]{:S(2)}, u32[]{:S(2)}) %collective-permute-start.6) | collective-permute-done | bytes 262176 | tf_op jit(solution)/shard_map/ppermute | solution.py:23
  86.0 10.0 %collective-permute-done.24 = bf16[1,256,256]{2,1,0:T(8,128)(2,1)S(1)} collective-permute-done((bf16[1,256,256]{2,1,0:T(8,128)(2,1)S(1)}, bf16[1,256,256]{2,1,0:T(8,128)(2,1)S(1)}, u32[]{:S(2)}, u32[]{:S(2)}) %collective-permute-start.24) | collective-permute-done | bytes 131104 | tf_op jit(solution)/shard_map/ppermute | solution.py:23
  98.7 6.7 %collective-permute-done.8 = bf16[1,256,256]{2,1,0:T(8,128)(2,1)S(1)} collective-permute-done((bf16[1,256,256]{2,1,0:T(8,128)(2,1)S(1)}, bf16[1,256,256]{2,1,0:T(8,128)(2,1)S(1)}, u32[]{:S(2)}, u32[]{:S(2)}) %collective-permute-start.8) | collective-permute-done | bytes 131104 | tf_op jit(solution)/shard_map/ppermute | solution.py:23
  106.0 5.9 %collective-permute-done.9 = bf16[2,256,256]{2,1,0:T(8,128)(2,1)S(1)} collective-permute-done((bf16[2,256,256]{2,1,0:T(8,128)(2,1)S(1)}, bf16[2,256,256]{2,1,0:T(8,128)(2,1)S(1)}, u32[]{:S(2)}, u32[]{:S(2)}) %collective-permute-start.9) | collective-permute-done | bytes 262176 | tf_op jit(solution)/shard_map/ppermute | solution.py:23
  113.4 10.6 %cols_times_joined.3 = (bf16[2,256,896]{2,1,0:T(8,128)(2,1)}, f32[2,256,896]{2,1,0:T(8,128)}) custom-call(s32[4]{0:T(128)} %pad_add_fusion.cols_ref, s32[8]{0:T(128)} %stack.40.order_ref.rows_ref, bf16[2048,3584]{1,0:T(8,128)(2,1)} %weight_ref.11, bf16[4,256,256]{2,1,0:T(8,128)(2,1)} %copy-done.6, bf16[4,256,256]{2,1,0:T(8,128)(2,1)} %copy-done.19), custom_call_target="tpu_custom_call" | custom-call | flops 3758096384 | bytes 16515072 | tf_op jit(solution)/shard_map/cols_times_joined/pallas_call | solution.py:444
  124.9 10.5 %cols_times_joined.2 = (bf16[2,256,896]{2,1,0:T(8,128)(2,1)}, f32[2,256,896]{2,1,0:T(8,128)}) custom-call(s32[4]{0:T(128)} %pad_add_fusion.cols_ref, s32[8]{0:T(128)} %stack.40.order_ref.rows_ref, bf16[2048,3584]{1,0:T(8,128)(2,1)} %weight_ref.11, bf16[4,256,256]{2,1,0:T(8,128)(2,1)} %copy-done.7, bf16[4,256,256]{2,1,0:T(8,128)(2,1)} %copy-done.20), custom_call_target="tpu_custom_call" | custom-call | flops 3758096384 | bytes 16515072 | tf_op jit(solution)/shard_map/cols_times_joined/pallas_call | solution.py:444
  138.4 15.5 %collective-permute-done.11 = bf16[2,256,896]{2,1,0:T(8,128)(2,1)S(1)} collective-permute-done((bf16[2,256,896]{2,1,0:T(8,128)(2,1)}, bf16[2,256,896]{2,1,0:T(8,128)(2,1)S(1)}, u32[]{:S(2)}, u32[]{:S(2)}) %collective-permute-start.11) | collective-permute-done | bytes 917536 | tf_op jit(solution)/shard_map/ppermute | solution.py:23
  156.4 6.3 %collective-permute-done.12 = bf16[1,256,896]{2,1,0:T(8,128)(2,1)S(1)} collective-permute-done((bf16[1,256,896]{2,1,0:T(8,128)(2,1)S(1)}, bf16[1,256,896]{2,1,0:T(8,128)(2,1)S(1)}, u32[]{:S(2)}, u32[]{:S(2)}) %collective-permute-start.12) | collective-permute-done | bytes 458784 | tf_op jit(solution)/shard_map/ppermute | solution.py:23
  169.0 6.6 %collective-permute-done.13 = bf16[1,256,896]{2,1,0:T(8,128)(2,1)S(1)} collective-permute-done((bf16[1,256,896]{2,1,0:T(8,128)(2,1)S(1)}, bf16[1,256,896]{2,1,0:T(8,128)(2,1)S(1)}, u32[]{:S(2)}, u32[]{:S(2)}) %collective-permute-start.13) | collective-permute-done | bytes 458784 | tf_op jit(solution)/shard_map/ppermute | solution.py:23
  182.1 11.5 %rows_times_joined.3 = (f32[4,256,256]{2,1,0:T(8,128)}, f32[4,256,256]{2,1,0:T(8,128)}) custom-call(s32[8]{0:T(128)} %stack.40.order_ref.rows_ref, s32[4]{0:T(128)} %pad_add_fusion.cols_ref, bf16[2048,3584]{1,0:T(8,128)(2,1)} %weight_ref.11, bf16[2,256,896]{2,1,0:T(8,128)(2,1)} %copy-done.4, bf16[2,256,896]{2,1,0:T(8,128)(2,1)} %copy-done.17), custom_call_target="tpu_custom_call" | custom-call | flops 3758096384 | bytes 16515072 | tf_op jit(solution)/shard_map/rows_times_joined/pallas_call | solution.py:369
  195.9 11.3 %rows_times_joined.2 = (f32[4,256,256]{2,1,0:T(8,128)}, f32[4,256,256]{2,1,0:T(8,128)}) custom-call(s32[8]{0:T(128)} %stack.40.order_ref.rows_ref, s32[4]{0:T(128)} %pad_add_fusion.cols_ref, bf16[2048,3584]{1,0:T(8,128)(2,1)} %weight_ref.11, bf16[2,256,896]{2,1,0:T(8,128)(2,1)} %copy-done.3, bf16[2,256,896]{2,1,0:T(8,128)(2,1)} %copy-done.16), custom_call_target="tpu_custom_call" | custom-call | flops 3758096384 | bytes 16515072 | tf_op jit(solution)/shard_map/rows_times_joined/pallas_call | solution.py:369
  210.2 5.9 %collective-permute-done.32 = bf16[2,256,256]{2,1,0:T(8,128)(2,1)S(1)} collective-permute-done((bf16[2,256,256]{2,1,0:T(8,128)(2,1)S(1)}, bf16[2,256,256]{2,1,0:T(8,128)(2,1)S(1)}, u32[]{:S(2)}, u32[]{:S(2)}) %collective-permute-start.32) | collective-permute-done | bytes 262176 | tf_op jit(solution)/shard_map/ppermute | solution.py:23
  217.3 6.8 %collective-permute-done.16 = bf16[2,256,256]{2,1,0:T(8,128)(2,1)S(1)} collective-permute-done((bf16[2,256,256]{2,1,0:T(8,128)(2,1)S(1)}, bf16[2,256,256]{2,1,0:T(8,128)(2,1)S(1)}, u32[]{:S(2)}, u32[]{:S(2)}) %collective-permute-start.16) | collective-permute-done | bytes 262176 | tf_op jit(solution)/shard_map/ppermute | solution.py:23
  233.7 9.2 %collective-permute-done.18 = bf16[1,256,256]{2,1,0:T(8,128)(2,1)S(1)} collective-permute-done((bf16[1,256,256]{2,1,0:T(8,128)(2,1)S(1)}, bf16[1,256,256]{2,1,0:T(8,128)(2,1)S(1)}, u32[]{:S(2)}, u32[]{:S(2)}) %collective-permute-start.18) | collective-permute-done | bytes 131104 | tf_op jit(solution)/shard_map/ppermute | solution.py:23
  245.6 5.7 %collective-permute-done.19 = bf16[2,256,256]{2,1,0:T(8,128)(2,1)S(1)} collective-permute-done((bf16[2,256,256]{2,1,0:T(8,128)(2,1)S(1)}, bf16[2,256,256]{2,1,0:T(8,128)(2,1)S(1)}, u32[]{:S(2)}, u32[]{:S(2)}) %collective-permute-start.19) | collective-permute-done | bytes 262176 | tf_op jit(solution)/shard_map/ppermute | solution.py:23
  263.3 8.0 %collective-permute-done.37 = f32[256,512]{1,0:T(8,128)S(1)} collective-permute-done((f32[256,512]{1,0:T(8,128)S(1)}, f32[256,512]{1,0:T(8,128)S(1)}, u32[]{:S(2)}, u32[]{:S(2)}) %collective-permute-start.37) | collective-permute-done | bytes 524320 | tf_op jit(solution)/shard_map/ppermute | solution.py:23
  272.9 7.8 %collective-permute-done.38 = f32[256,512]{1,0:T(8,128)S(1)} collective-permute-done((f32[256,512]{1,0:T(8,128)S(1)}, f32[256,512]{1,0:T(8,128)S(1)}, u32[]{:S(2)}, u32[]{:S(2)}) %collective-permute-start.38) | collective-permute-done | bytes 524320 | tf_op jit(solution)/shard_map/ppermute | solution.py:23
  282.9 22.7 %inverse_factor.1 = f32[512,512]{1,0:T(8,128)S(1)} custom-call(f32[512,512]{1,0:T(8,128)S(1)} %pad_maximum_fusion.1.gram_ref), custom_call_target="tpu_custom_call" | custom-call | flops 5368709120 | bytes 2097152 | tf_op jit(solution)/shard_map/inverse_factor/pallas_call | solution.py:265
  308.8 8.6 %convolution_convert_fusion = bf16[512,3584]{1,0:T(8,128)(2,1)S(1)} fusion(bf16[2048,3584]{1,0:T(8,128)(2,1)S(1)} %bitcast.31, f32[2048,512]{1,0:T(8,128)S(1)} %convolution_add_fusion, f32[2048]{0:T(1024)S(1)} %dynamic-slice_divide_fusion), kind=kOutput, calls=%fused_computation | convolution fusion | flops 7520124928 | bytes 22552576 | tf_op jit(solution)/shard_map/dot_general | solution.py:283
  319.1 22.1 %collective-permute-done.40 = bf16[2,128,3584]{2,1,0:T(8,128)(2,1)S(1)} collective-permute-done((bf16[2,128,3584]{2,1,0:T(8,128)(2,1)S(1)}, bf16[2,128,3584]{2,1,0:T(8,128)(2,1)S(1)}, u32[]{:S(2)}, u32[]{:S(2)}) %collective-permute-start.40) | collective-permute-done | bytes 1835040 | tf_op jit(solution)/shard_map/ppermute | solution.py:23
  344.1 11.1 %collective-permute-done.41 = bf16[1,128,3584]{2,1,0:T(8,128)(2,1)S(1)} collective-permute-done((bf16[1,128,3584]{2,1,0:T(8,128)(2,1)S(1)}, bf16[1,128,3584]{2,1,0:T(8,128)(2,1)S(1)}, u32[]{:S(2)}, u32[]{:S(2)}) %collective-permute-start.41) | collective-permute-done | bytes 917536 | tf_op jit(solution)/shard_map/ppermute | solution.py:23
  (182 shorter events, 111.7 us)
Async XLA Ops:
  28.8 18.6 %collective-permute-start.21 = (f32[4,256,256]{2,1,0:T(8,128)}, f32[4,256,256]{2,1,0:T(8,128)S(1)}, u32[]{:S(2)}, u32[]{:S(2)}) collective-permute-start(f32[4,256,256]{2,1,0:T(8,128)} %get-tuple-element.29), channel_id=1, source_target_pairs={{0,1},{1,0},{2,3},{3,2},{4,5},{5,4},{6,7},{7,6},{8,9},{9,8},{10,11... | collective-permute-start | bytes 3145736 | tf_op jit(solution)/shard_map/ppermute | solution.py:23
  42.0 19.1 %collective-permute-start.5 = (f32[4,256,256]{2,1,0:T(8,128)}, f32[4,256,256]{2,1,0:T(8,128)S(1)}, u32[]{:S(2)}, u32[]{:S(2)}) collective-permute-start(f32[4,256,256]{2,1,0:T(8,128)} %get-tuple-element.23), channel_id=1, source_target_pairs={{0,1},{1,0},{2,3},{3,2},{4,5},{5,4},{6,7},{7,6},{8,9},{9,8},{10,11... | collective-permute-start | bytes 3145736 | tf_op jit(solution)/shard_map/ppermute | solution.py:23
  48.3 19.8 %collective-permute-start.22 = (bf16[2,256,256]{2,1,0:T(8,128)(2,1)}, bf16[2,256,256]{2,1,0:T(8,128)(2,1)S(1)}, u32[]{:S(2)}, u32[]{:S(2)}) collective-permute-start(bf16[2,256,256]{2,1,0:T(8,128)(2,1)} %slice.167), channel_id=1, source_target_pairs={{0,2},{1,5},{2,0},{3,7},{4,6},{5,1},{6,4},{7,3},{8,10},{9,13},{10,... | collective-permute-start | bytes 786440 | tf_op jit(solution)/shard_map/ppermute | solution.py:23
  63.5 12.8 %collective-permute-start.6 = (bf16[2,256,256]{2,1,0:T(8,128)(2,1)S(1)}, bf16[2,256,256]{2,1,0:T(8,128)(2,1)}, u32[]{:S(2)}, u32[]{:S(2)}) collective-permute-start(bf16[2,256,256]{2,1,0:T(8,128)(2,1)S(1)} %slice.169), channel_id=1, source_target_pairs={{0,2},{1,5},{2,0},{3,7},{4,6},{5,1},{6,4},{7,3},{8,10},{9,13},{10,... | collective-permute-start | bytes 786440 | tf_op jit(solution)/shard_map/ppermute | solution.py:23
  68.1 11.3 %collective-permute-start.23 = (bf16[1,256,256]{2,1,0:T(8,128)(2,1)S(1)}, bf16[1,256,256]{2,1,0:T(8,128)(2,1)S(1)}, u32[]{:S(2)}, u32[]{:S(2)}) collective-permute-start(bf16[1,256,256]{2,1,0:T(8,128)(2,1)S(1)} %slice.171), channel_id=1, source_target_pairs={{0,4},{1,3},{2,6},{3,1},{4,0},{5,7},{6,2},{7,5},{8,12},{9,11},{10,... | collective-permute-start | bytes 393224 | tf_op jit(solution)/shard_map/ppermute | solution.py:23
  84.5 11.5 %collective-permute-start.24 = (bf16[1,256,256]{2,1,0:T(8,128)(2,1)S(1)}, bf16[1,256,256]{2,1,0:T(8,128)(2,1)S(1)}, u32[]{:S(2)}, u32[]{:S(2)}) collective-permute-start(bf16[1,256,256]{2,1,0:T(8,128)(2,1)S(1)} %get-tuple-element.44), channel_id=1, source_target_pairs={{0,4},{1,3},{2,6},{3,1},{4,0},{5,7},{6,2},{7,5},{8,12},{9,11},{10,... | collective-permute-start | bytes 393224 | tf_op jit(solution)/shard_map/ppermute | solution.py:23
  96.0 9.8 %collective-permute-start.25 = (bf16[2,256,256]{2,1,0:T(8,128)(2,1)S(1)}, bf16[2,256,256]{2,1,0:T(8,128)(2,1)S(1)}, u32[]{:S(2)}, u32[]{:S(2)}) collective-permute-start(bf16[2,256,256]{2,1,0:T(8,128)(2,1)S(1)} %pad_maximum_fusion.10), channel_id=1, source_target_pairs={{0,2},{1,5},{2,0},{3,7},{4,6},{5,1},{6,4},{7,3},{8,10},{9,13},{10,... | collective-permute-start | bytes 786440 | tf_op jit(solution)/shard_map/ppermute | solution.py:23
  96.1 9.3 %collective-permute-start.8 = (bf16[1,256,256]{2,1,0:T(8,128)(2,1)S(1)}, bf16[1,256,256]{2,1,0:T(8,128)(2,1)S(1)}, u32[]{:S(2)}, u32[]{:S(2)}) collective-permute-start(bf16[1,256,256]{2,1,0:T(8,128)(2,1)S(1)} %get-tuple-element.45), channel_id=1, source_target_pairs={{0,4},{1,3},{2,6},{3,1},{4,0},{5,7},{6,2},{7,5},{8,12},{9,11},{10,... | collective-permute-start | bytes 393224 | tf_op jit(solution)/shard_map/ppermute | solution.py:23
  111.9 12.2 %collective-permute-start.10 = (bf16[4,256,256]{2,1,0:T(8,128)(2,1)S(1)}, bf16[4,256,256]{2,1,0:T(8,128)(2,1)S(1)}, u32[]{:S(2)}, u32[]{:S(2)}) collective-permute-start(bf16[4,256,256]{2,1,0:T(8,128)(2,1)S(1)} %pad_maximum_fusion.4.first_ref), channel_id=1, source_target_pairs={{0,1},{1,0},{2,3},{3,2},{4,5},{5,4},{6,7},{7,6},{8,9},{9,8},{10,11... | collective-permute-start | bytes 1572872 | tf_op jit(solution)/shard_map/ppermute | solution.py:23
  124.0 13.7 %collective-permute-start.27 = (bf16[2,256,896]{2,1,0:T(8,128)(2,1)}, bf16[2,256,896]{2,1,0:T(8,128)(2,1)S(1)}, u32[]{:S(2)}, u32[]{:S(2)}) collective-permute-start(bf16[2,256,896]{2,1,0:T(8,128)(2,1)} %get-tuple-element.31), channel_id=1, source_target_pairs={{0,8},{1,17},{2,10},{3,19},{4,12},{5,21},{6,14},{7,23},{8,0},{9,25... | collective-permute-start | bytes 2752520 | tf_op jit(solution)/shard_map/ppermute | solution.py:23
  135.4 18.5 %collective-permute-start.11 = (bf16[2,256,896]{2,1,0:T(8,128)(2,1)}, bf16[2,256,896]{2,1,0:T(8,128)(2,1)S(1)}, u32[]{:S(2)}, u32[]{:S(2)}) collective-permute-start(bf16[2,256,896]{2,1,0:T(8,128)(2,1)} %get-tuple-element.25), channel_id=1, source_target_pairs={{0,8},{1,17},{2,10},{3,19},{4,12},{5,21},{6,14},{7,23},{8,0},{9,25... | collective-permute-start | bytes 2752520 | tf_op jit(solution)/shard_map/ppermute | solution.py:23
  137.9 17.7 %collective-permute-start.28 = (bf16[1,256,896]{2,1,0:T(8,128)(2,1)S(1)}, bf16[1,256,896]{2,1,0:T(8,128)(2,1)S(1)}, u32[]{:S(2)}, u32[]{:S(2)}) collective-permute-start(bf16[1,256,896]{2,1,0:T(8,128)(2,1)S(1)} %slice.164), channel_id=1, source_target_pairs={{0,16},{1,9},{2,18},{3,11},{4,20},{5,13},{6,22},{7,15},{8,24},{9,1... | collective-permute-start | bytes 1376264 | tf_op jit(solution)/shard_map/ppermute | solution.py:23
  155.7 11.9 %collective-permute-start.29 = (bf16[1,256,896]{2,1,0:T(8,128)(2,1)S(1)}, bf16[1,256,896]{2,1,0:T(8,128)(2,1)S(1)}, u32[]{:S(2)}, u32[]{:S(2)}) collective-permute-start(bf16[1,256,896]{2,1,0:T(8,128)(2,1)S(1)} %fusion.11), channel_id=1, source_target_pairs={{0,16},{1,9},{2,18},{3,11},{4,20},{5,13},{6,22},{7,15},{8,24},{9,1... | collective-permute-start | bytes 1376264 | tf_op jit(solution)/shard_map/ppermute | solution.py:23
  162.8 12.9 %collective-permute-start.13 = (bf16[1,256,896]{2,1,0:T(8,128)(2,1)S(1)}, bf16[1,256,896]{2,1,0:T(8,128)(2,1)S(1)}, u32[]{:S(2)}, u32[]{:S(2)}) collective-permute-start(bf16[1,256,896]{2,1,0:T(8,128)(2,1)S(1)} %fusion.12), channel_id=1, source_target_pairs={{0,16},{1,9},{2,18},{3,11},{4,20},{5,13},{6,22},{7,15},{8,24},{9,1... | collective-permute-start | bytes 1376264 | tf_op jit(solution)/shard_map/ppermute | solution.py:23
  167.7 13.5 %collective-permute-start.30 = (bf16[2,256,896]{2,1,0:T(8,128)(2,1)S(1)}, bf16[2,256,896]{2,1,0:T(8,128)(2,1)S(1)}, u32[]{:S(2)}, u32[]{:S(2)}) collective-permute-start(bf16[2,256,896]{2,1,0:T(8,128)(2,1)S(1)} %pad_maximum_fusion.3.first_ref), channel_id=1, source_target_pairs={{0,8},{1,17},{2,10},{3,19},{4,12},{5,21},{6,14},{7,23},{8,0},{9,25... | collective-permute-start | bytes 2752520 | tf_op jit(solution)/shard_map/ppermute | solution.py:23
  175.8 19.1 %collective-permute-start.14 = (bf16[2,256,896]{2,1,0:T(8,128)(2,1)S(1)}, bf16[2,256,896]{2,1,0:T(8,128)(2,1)S(1)}, u32[]{:S(2)}, u32[]{:S(2)}) collective-permute-start(bf16[2,256,896]{2,1,0:T(8,128)(2,1)S(1)} %pad_maximum_fusion.2.first_ref), channel_id=1, source_target_pairs={{0,8},{1,17},{2,10},{3,19},{4,12},{5,21},{6,14},{7,23},{8,0},{9,25... | collective-permute-start | bytes 2752520 | tf_op jit(solution)/shard_map/ppermute | solution.py:23
  193.6 13.5 %collective-permute-start.31 = (f32[4,256,256]{2,1,0:T(8,128)}, f32[4,256,256]{2,1,0:T(8,128)S(1)}, u32[]{:S(2)}, u32[]{:S(2)}) collective-permute-start(f32[4,256,256]{2,1,0:T(8,128)} %get-tuple-element.33), channel_id=1, source_target_pairs={{0,1},{1,0},{2,3},{3,2},{4,5},{5,4},{6,7},{7,6},{8,9},{9,8},{10,11... | collective-permute-start | bytes 3145736 | tf_op jit(solution)/shard_map/ppermute | solution.py:23
  210.2 13.9 %collective-permute-start.16 = (bf16[2,256,256]{2,1,0:T(8,128)(2,1)S(1)}, bf16[2,256,256]{2,1,0:T(8,128)(2,1)S(1)}, u32[]{:S(2)}, u32[]{:S(2)}) collective-permute-start(bf16[2,256,256]{2,1,0:T(8,128)(2,1)S(1)} %slice.168), channel_id=1, source_target_pairs={{0,2},{1,5},{2,0},{3,7},{4,6},{5,1},{6,4},{7,3},{8,10},{9,13},{10,... | collective-permute-start | bytes 786440 | tf_op jit(solution)/shard_map/ppermute | solution.py:23
  231.0 12.0 %collective-permute-start.18 = (bf16[1,256,256]{2,1,0:T(8,128)(2,1)S(1)}, bf16[1,256,256]{2,1,0:T(8,128)(2,1)S(1)}, u32[]{:S(2)}, u32[]{:S(2)}) collective-permute-start(bf16[1,256,256]{2,1,0:T(8,128)(2,1)S(1)} %fusion.18), channel_id=1, source_target_pairs={{0,4},{1,3},{2,6},{3,1},{4,0},{5,7},{6,2},{7,5},{8,12},{9,11},{10,... | collective-permute-start | bytes 393224 | tf_op jit(solution)/shard_map/ppermute | solution.py:23
  233.6 9.5 %collective-permute-start.35 = (bf16[2,256,256]{2,1,0:T(8,128)(2,1)S(1)}, bf16[2,256,256]{2,1,0:T(8,128)(2,1)S(1)}, u32[]{:S(2)}, u32[]{:S(2)}) collective-permute-start(bf16[2,256,256]{2,1,0:T(8,128)(2,1)S(1)} %pad_maximum_fusion.11), channel_id=1, source_target_pairs={{0,2},{1,5},{2,0},{3,7},{4,6},{5,1},{6,4},{7,3},{8,10},{9,13},{10,... | collective-permute-start | bytes 786440 | tf_op jit(solution)/shard_map/ppermute | solution.py:23
  262.1 9.2 %collective-permute-start.37 = (f32[256,512]{1,0:T(8,128)S(1)}, f32[256,512]{1,0:T(8,128)S(1)}, u32[]{:S(2)}, u32[]{:S(2)}) collective-permute-start(f32[256,512]{1,0:T(8,128)S(1)} %convolution_add_fusion.1), channel_id=1, source_target_pairs={{0,8},{1,17},{2,10},{3,19},{4,12},{5,21},{6,14},{7,23},{8,0},{9,25... | collective-permute-start | bytes 1572872 | tf_op jit(solution)/shard_map/ppermute | solution.py:23
  271.4 9.2 %collective-permute-start.38 = (f32[256,512]{1,0:T(8,128)S(1)}, f32[256,512]{1,0:T(8,128)S(1)}, u32[]{:S(2)}, u32[]{:S(2)}) collective-permute-start(f32[256,512]{1,0:T(8,128)S(1)} %add.133), channel_id=1, source_target_pairs={{0,16},{1,9},{2,18},{3,11},{4,20},{5,13},{6,22},{7,15},{8,24},{9,1... | collective-permute-start | bytes 1572872 | tf_op jit(solution)/shard_map/ppermute | solution.py:23
  317.9 23.3 %collective-permute-start.40 = (bf16[2,128,3584]{2,1,0:T(8,128)(2,1)S(1)}, bf16[2,128,3584]{2,1,0:T(8,128)(2,1)S(1)}, u32[]{:S(2)}, u32[]{:S(2)}) collective-permute-start(bf16[2,128,3584]{2,1,0:T(8,128)(2,1)S(1)} %pad_maximum_fusion), channel_id=1, source_target_pairs={{0,8},{1,17},{2,10},{3,19},{4,12},{5,21},{6,14},{7,23},{8,0},{9,25... | collective-permute-start | bytes 5505032 | tf_op jit(solution)/shard_map/ppermute | solution.py:23
  341.8 13.5 %collective-permute-start.41 = (bf16[1,128,3584]{2,1,0:T(8,128)(2,1)S(1)}, bf16[1,128,3584]{2,1,0:T(8,128)(2,1)S(1)}, u32[]{:S(2)}, u32[]{:S(2)}) collective-permute-start(bf16[1,128,3584]{2,1,0:T(8,128)(2,1)S(1)} %slice.163), channel_id=1, source_target_pairs={{0,16},{1,9},{2,18},{3,11},{4,20},{5,13},{6,22},{7,15},{8,24},{9,1... | collective-permute-start | bytes 2752520 | tf_op jit(solution)/shard_map/ppermute | solution.py:23
  (44 other events, 326.2 us)
where the time goes:
time: 358 us; the launch traced here: 357 us
  waiting for transfers between devices  168 us (47%)
  Pallas kernels  107 us (30%)
  starting transfers between devices  44.8 us (13%)
  matrix products  16.2 us (5%)
  local copies, waits for them, and re-layouts  10.4 us (3%)
  other arithmetic  8.74 us (2%)
    ppermute x42, waiting for transfers between devices, swap(): return lax.ppermute(block, AXES, pairs)  168 us
    ppermute x42, starting transfers between devices, swap(): return lax.ppermute(block, AXES, pairs)  44.8 us
    pallas_call x2, Pallas kernels, rows_times(): pl.pallas_call(functools.partial(rows_plain_kernel, turned), out_shape=sh...  25.5 us
    pallas_call x1, Pallas kernels, inverse_factor(): pl.pallas_call(inverse_factor_kernel, out_shape=jax.ShapeDtypeStruct((siz...  22.7 us
    pallas_call x2, Pallas kernels, rows_times_joined(): pl.pallas_call(rows_joined_kernel, out_shape=shapes, grid_spec=pltpu.Pref...  22.7 us
    pallas_call x2, Pallas kernels, cols_times_joined(): pl.pallas_call(cols_kernel, out_shape=shapes, grid_spec=pltpu.PrefetchSca...  21.1 us
    dot_general x5, matrix products, dot(): lax.dot_general(left, right, (dims, ((), ())), preferred_element_type=F32)  16.2 us
    pallas_call x1, Pallas kernels, local_mass(): pl.pallas_call(row_mass_kernel, out_shape=jax.ShapeDtypeStruct((1, width)...  9.33 us
  transfers between devices with their start and end apart: 42, of which 30 were waited for; matrix products, arithmetic and copies ran while one was open for 2% of the time, Pallas kernels for 16%

commit v1 on v0

--- a/solution.py
+++ b/solution.py
@@ -157,7 +157,7 @@
                 pl.BlockSpec((1, length, 128), whole),
             ),
         ),
-        compiler_params=pltpu.CompilerParams(vmem_limit_bytes=48 << 20),
+        compiler_params=pltpu.CompilerParams(vmem_limit_bytes=LIMIT),
         cost_estimate=pl.CostEstimate(
             flops=2 * seqs * length * length * cols,
             bytes_accessed=2 * out_grads.size,
@@ -177,7 +177,7 @@
             pl.BlockSpec((seqs, length, 128), fixed),
         ],
         out_specs=pl.BlockSpec((1, tile), lambda i: (0, i)),
-        compiler_params=pltpu.CompilerParams(vmem_limit_bytes=48 << 20),
+        compiler_params=pltpu.CompilerParams(vmem_limit_bytes=LIMIT),
         cost_estimate=pl.CostEstimate(
             flops=4 * seqs * length * length * width,
             bytes_accessed=2 * activations.size,
@@ -268,7 +268,7 @@
         in_specs=[pl.BlockSpec(memory_space=pltpu.VMEM)],
         out_specs=pl.BlockSpec(memory_space=pltpu.VMEM),
         scratch_shapes=[pltpu.VMEM((size, size), F32)],
-        compiler_params=pltpu.CompilerParams(vmem_limit_bytes=32 << 20),
+        compiler_params=pltpu.CompilerParams(vmem_limit_bytes=LIMIT),
         cost_estimate=pl.CostEstimate(
             flops=40 * size**3, bytes_accessed=8 * size * size, transcendentals=size
         ),
@@ -276,7 +276,7 @@
     )(gram)
 
 
-LIMIT = 56 << 20
+LIMIT = 24 << 20
 
 
 def dot(left, right, dims=((1,), (0,))):

time: 358 us -> 351 us (0.980)
  Pallas kernels: 107 us -> 80.9 us
  local copies, waits for them, and re-layouts: 10.4 us -> 23.6 us
  waiting for transfers between devices: 168 us -> 179 us
  starting transfers between devices: 44.8 us -> 38.1 us
    unnamed x52 -> x28, local copies, waits for them, and re-layouts: 8.41 us -> 22.1 us
    ppermute x42, waiting for transfers between devices: 168 us -> 179 us  [swap(): return lax.ppermute(block, AXES, pairs)]
    pallas_call x2, Pallas kernels: 25.5 us -> 17.2 us  [rows_times(): pl.pallas_call(functools.partial(rows_plain_kernel, turned), out_shape=sh...]
    pallas_call x2, Pallas kernels: 22.7 us -> 16 us  [rows_times_joined(): pl.pallas_call(rows_joined_kernel, out_shape=shapes, grid_spec=pltpu.Pref...]
    pallas_call x2, Pallas kernels: 21.1 us -> 14.4 us  [cols_times_joined(): pl.pallas_call(cols_kernel, out_shape=shapes, grid_spec=pltpu.PrefetchSca...]
    ppermute x42, starting transfers between devices: 44.8 us -> 38.1 us  [swap(): return lax.ppermute(block, AXES, pairs)]
  transfers between devices with their start and end apart: 42 -> 42, of which waited for: 30 -> 31; matrix products, arithmetic and copies ran while one was open for 2% -> 2% of each run, Pallas kernels for 16% -> 11%
where the time goes in v1:
time: 351 us; the launch traced here: 350 us
  waiting for transfers between devices  179 us (51%)
  Pallas kernels  80.9 us (23%)
  starting transfers between devices  38.1 us (11%)
  local copies, waits for them, and re-layouts  23.6 us (7%)
  matrix products  17.3 us (5%)
  other arithmetic  9.3 us (3%)
    ppermute x42, waiting for transfers between devices, swap(): return lax.ppermute(block, AXES, pairs)  179 us
    ppermute x42, starting transfers between devices, swap(): return lax.ppermute(block, AXES, pairs)  38.1 us
    pallas_call x1, Pallas kernels, inverse_factor(): pl.pallas_call(inverse_factor_kernel, out_shape=jax.ShapeDtypeStruct((siz...  22.7 us
    unnamed x28, local copies, waits for them, and re-layouts  22.1 us
    dot_general x5, matrix products, dot(): lax.dot_general(left, right, (dims, ((), ())), preferred_element_type=F32)  17.3 us
    pallas_call x2, Pallas kernels, rows_times(): pl.pallas_call(functools.partial(rows_plain_kernel, turned), out_shape=sh...  17.2 us
    pallas_call x2, Pallas kernels, rows_times_joined(): pl.pallas_call(rows_joined_kernel, out_shape=shapes, grid_spec=pltpu.Pref...  16 us
    pallas_call x2, Pallas kernels, cols_times_joined(): pl.pallas_call(cols_kernel, out_shape=shapes, grid_spec=pltpu.PrefetchSca...  14.4 us
  transfers between devices with their start and end apart: 42, of which 31 were waited for; matrix products, arithmetic and copies ran while one was open for 2% of the time, Pallas kernels for 11%

profile of v1, /device:TPU:0, one launch (start us, length us, event | category | flops | bytes accessed | tf_op | source)
XLA Modules:
  0.0 350.2 jit_solution(4806083798737864459)
XLA Ops:
  9.4 7.3 %row_mass.1 = f32[1,8192]{1,0:T(1,128)S(1)} custom-call(bf16[2,256,8192]{2,1,0:T(8,128)(2,1)S(1)} %copy-done.9, bf16[2,512,256]{2,1,0:T(8,128)(2,1)S(1)} %get-tuple-element.18.gram_ref, f32[2,256,128]{2,1,0:T(8,128)S(1)} %get-tuple-element.19.scale_ref), custom_call_target="tpu_custom_call" | custom-call | flops 4294967296 | bytes 8388608 | tf_op jit(solution)/shard_map/row_mass/pallas_call | solution.py:170
  24.0 8.6 %rows_times.3 = (f32[4,256,256]{2,1,0:T(8,128)S(1)}, f32[4,256,256]{2,1,0:T(8,128)S(1)}) custom-call(s32[8]{0:T(128)S(1)} %stack.40.order_ref.rows_ref, bf16[2048,3584]{1,0:T(8,128)(2,1)S(1)} %copy-done, bf16[3584,512]{1,0:T(8,128)(2,1)S(1)} %copy-done.2), custom_call_target="tpu_custom_call" | custom-call | flops 3758096384 | bytes 16515072 | tf_op jit(solution)/shard_map/rows_times/pallas_call | solution.py:329
  33.1 8.6 %rows_times.2 = (f32[4,256,256]{2,1,0:T(8,128)S(1)}, f32[4,256,256]{2,1,0:T(8,128)S(1)}) custom-call(s32[8]{0:T(128)S(1)} %stack.40.order_ref.rows_ref, bf16[2048,3584]{1,0:T(8,128)(2,1)S(1)} %copy-done, bf16[3584,512]{1,0:T(8,128)(2,1)S(1)} %copy-done.2), custom_call_target="tpu_custom_call" | custom-call | flops 3758096384 | bytes 16515072 | tf_op jit(solution)/shard_map/rows_times/pallas_call | solution.py:329
  69.5 5.5 %collective-permute-done.6 = bf16[2,256,256]{2,1,0:T(8,128)(2,1)} collective-permute-done((bf16[2,256,256]{2,1,0:T(8,128)(2,1)S(1)}, bf16[2,256,256]{2,1,0:T(8,128)(2,1)}, u32[]{:S(2)}, u32[]{:S(2)}) %collective-permute-start.6) | collective-permute-done | bytes 262176 | tf_op jit(solution)/shard_map/ppermute | solution.py:23
  84.7 9.7 %collective-permute-done.24 = bf16[1,256,256]{2,1,0:T(8,128)(2,1)S(1)} collective-permute-done((bf16[1,256,256]{2,1,0:T(8,128)(2,1)S(1)}, bf16[1,256,256]{2,1,0:T(8,128)(2,1)S(1)}, u32[]{:S(2)}, u32[]{:S(2)}) %collective-permute-start.24) | collective-permute-done | bytes 131104 | tf_op jit(solution)/shard_map/ppermute | solution.py:23
  97.0 6.7 %collective-permute-done.8 = bf16[1,256,256]{2,1,0:T(8,128)(2,1)S(1)} collective-permute-done((bf16[1,256,256]{2,1,0:T(8,128)(2,1)S(1)}, bf16[1,256,256]{2,1,0:T(8,128)(2,1)S(1)}, u32[]{:S(2)}, u32[]{:S(2)}) %collective-permute-start.8) | collective-permute-done | bytes 131104 | tf_op jit(solution)/shard_map/ppermute | solution.py:23
  104.7 5.4 %collective-permute-done.9 = bf16[2,256,256]{2,1,0:T(8,128)(2,1)S(1)} collective-permute-done((bf16[2,256,256]{2,1,0:T(8,128)(2,1)S(1)}, bf16[2,256,256]{2,1,0:T(8,128)(2,1)S(1)}, u32[]{:S(2)}, u32[]{:S(2)}) %collective-permute-start.9) | collective-permute-done | bytes 262176 | tf_op jit(solution)/shard_map/ppermute | solution.py:23
  115.6 7.2 %cols_times_joined.3 = (bf16[2,256,896]{2,1,0:T(8,128)(2,1)S(1)}, f32[2,256,896]{2,1,0:T(8,128)S(1)}) custom-call(s32[4]{0:T(128)S(1)} %pad_add_fusion.cols_ref, s32[8]{0:T(128)S(1)} %stack.40.order_ref.rows_ref, bf16[2048,3584]{1,0:T(8,128)(2,1)S(1)} %copy-done.1, bf16[4,256,256]{2,1,0:T(8,128)(2,1)S(1)} %pad_maximum_fusion.6.first_ref, ...), custom_call_target="tpu_custom_call" | custom-call | flops 3758096384 | bytes 16515072 | tf_op jit(solution)/shard_map/cols_times_joined/pallas_call | solution.py:444
  122.9 7.2 %cols_times_joined.2 = (bf16[2,256,896]{2,1,0:T(8,128)(2,1)S(1)}, f32[2,256,896]{2,1,0:T(8,128)S(1)}) custom-call(s32[4]{0:T(128)S(1)} %pad_add_fusion.cols_ref, s32[8]{0:T(128)S(1)} %stack.40.order_ref.rows_ref, bf16[2048,3584]{1,0:T(8,128)(2,1)S(1)} %copy-done.1, bf16[4,256,256]{2,1,0:T(8,128)(2,1)S(1)} %pad_maximum_fusion.4.first_ref, ...), custom_call_target="tpu_custom_call" | custom-call | flops 3758096384 | bytes 16515072 | tf_op jit(solution)/shard_map/cols_times_joined/pallas_call | solution.py:444
  137.4 13.6 %collective-permute-done.11 = bf16[2,256,896]{2,1,0:T(8,128)(2,1)S(1)} collective-permute-done((bf16[2,256,896]{2,1,0:T(8,128)(2,1)S(1)}, bf16[2,256,896]{2,1,0:T(8,128)(2,1)S(1)}, u32[]{:S(2)}, u32[]{:S(2)}) %collective-permute-start.11) | collective-permute-done | bytes 917536 | tf_op jit(solution)/shard_map/ppermute | solution.py:23
  153.5 6.3 %collective-permute-done.12 = bf16[1,256,896]{2,1,0:T(8,128)(2,1)S(1)} collective-permute-done((bf16[1,256,896]{2,1,0:T(8,128)(2,1)S(1)}, bf16[1,256,896]{2,1,0:T(8,128)(2,1)S(1)}, u32[]{:S(2)}, u32[]{:S(2)}) %collective-permute-start.12) | collective-permute-done | bytes 458784 | tf_op jit(solution)/shard_map/ppermute | solution.py:23
  165.0 7.9 %collective-permute-done.13 = bf16[1,256,896]{2,1,0:T(8,128)(2,1)S(1)} collective-permute-done((bf16[1,256,896]{2,1,0:T(8,128)(2,1)S(1)}, bf16[1,256,896]{2,1,0:T(8,128)(2,1)S(1)}, u32[]{:S(2)}, u32[]{:S(2)}) %collective-permute-start.13) | collective-permute-done | bytes 458784 | tf_op jit(solution)/shard_map/ppermute | solution.py:23
  178.3 8.1 %rows_times_joined.3 = (f32[4,256,256]{2,1,0:T(8,128)S(1)}, f32[4,256,256]{2,1,0:T(8,128)S(1)}) custom-call(s32[8]{0:T(128)S(1)} %stack.40.order_ref.rows_ref, s32[4]{0:T(128)S(1)} %pad_add_fusion.cols_ref, bf16[2048,3584]{1,0:T(8,128)(2,1)S(1)} %copy-done.1, bf16[2,256,896]{2,1,0:T(8,128)(2,1)S(1)} %pad_maximum_fusion.3.first_ref, ...), custom_call_target="tpu_custom_call" | custom-call | flops 3758096384 | bytes 16515072 | tf_op jit(solution)/shard_map/rows_times_joined/pallas_call | solution.py:369
  188.1 7.9 %rows_times_joined.2 = (f32[4,256,256]{2,1,0:T(8,128)S(1)}, f32[4,256,256]{2,1,0:T(8,128)S(1)}) custom-call(s32[8]{0:T(128)S(1)} %stack.40.order_ref.rows_ref, s32[4]{0:T(128)S(1)} %pad_add_fusion.cols_ref, bf16[2048,3584]{1,0:T(8,128)(2,1)S(1)} %copy-done.1, bf16[2,256,896]{2,1,0:T(8,128)(2,1)S(1)} %pad_maximum_fusion.2.first_ref, ...), custom_call_target="tpu_custom_call" | custom-call | flops 3758096384 | bytes 16515072 | tf_op jit(solution)/shard_map/rows_times_joined/pallas_call | solution.py:369
  199.6 6.8 %collective-permute-done.32 = bf16[2,256,256]{2,1,0:T(8,128)(2,1)S(1)} collective-permute-done((bf16[2,256,256]{2,1,0:T(8,128)(2,1)S(1)}, bf16[2,256,256]{2,1,0:T(8,128)(2,1)S(1)}, u32[]{:S(2)}, u32[]{:S(2)}) %collective-permute-start.32) | collective-permute-done | bytes 262176 | tf_op jit(solution)/shard_map/ppermute | solution.py:23
  207.3 7.6 %collective-permute-done.16 = bf16[2,256,256]{2,1,0:T(8,128)(2,1)S(1)} collective-permute-done((bf16[2,256,256]{2,1,0:T(8,128)(2,1)S(1)}, bf16[2,256,256]{2,1,0:T(8,128)(2,1)S(1)}, u32[]{:S(2)}, u32[]{:S(2)}) %collective-permute-start.16) | collective-permute-done | bytes 262176 | tf_op jit(solution)/shard_map/ppermute | solution.py:23
  222.6 10.3 %collective-permute-done.34 = bf16[1,256,256]{2,1,0:T(8,128)(2,1)S(1)} collective-permute-done((bf16[1,256,256]{2,1,0:T(8,128)(2,1)S(1)}, bf16[1,256,256]{2,1,0:T(8,128)(2,1)S(1)}, u32[]{:S(2)}, u32[]{:S(2)}) %collective-permute-start.34) | collective-permute-done | bytes 131104 | tf_op jit(solution)/shard_map/ppermute | solution.py:23
  235.7 5.8 %collective-permute-done.35 = bf16[2,256,256]{2,1,0:T(8,128)(2,1)S(1)} collective-permute-done((bf16[2,256,256]{2,1,0:T(8,128)(2,1)S(1)}, bf16[2,256,256]{2,1,0:T(8,128)(2,1)S(1)}, u32[]{:S(2)}, u32[]{:S(2)}) %collective-permute-start.35) | collective-permute-done | bytes 262176 | tf_op jit(solution)/shard_map/ppermute | solution.py:23
  252.9 9.2 %collective-permute-done.37 = f32[256,512]{1,0:T(8,128)S(1)} collective-permute-done((f32[256,512]{1,0:T(8,128)S(1)}, f32[256,512]{1,0:T(8,128)S(1)}, u32[]{:S(2)}, u32[]{:S(2)}) %collective-permute-start.37) | collective-permute-done | bytes 524320 | tf_op jit(solution)/shard_map/ppermute | solution.py:23
  262.9 8.5 %collective-permute-done.38 = f32[256,512]{1,0:T(8,128)S(1)} collective-permute-done((f32[256,512]{1,0:T(8,128)S(1)}, f32[256,512]{1,0:T(8,128)S(1)}, u32[]{:S(2)}, u32[]{:S(2)}) %collective-permute-start.38) | collective-permute-done | bytes 524320 | tf_op jit(solution)/shard_map/ppermute | solution.py:23
  273.7 22.7 %inverse_factor.1 = f32[512,512]{1,0:T(8,128)S(1)} custom-call(f32[512,512]{1,0:T(8,128)S(1)} %pad_maximum_fusion.1.gram_ref), custom_call_target="tpu_custom_call" | custom-call | flops 5368709120 | bytes 2097152 | tf_op jit(solution)/shard_map/inverse_factor/pallas_call | solution.py:265
  301.1 9.8 %convolution_convert_fusion = bf16[512,3584]{1,0:T(8,128)(2,1)S(1)} fusion(bf16[2048,3584]{1,0:T(8,128)(2,1)S(1)} %bitcast.28, f32[2048,512]{1,0:T(8,128)} %convolution_add_fusion, f32[2048]{0:T(1024)S(1)} %dynamic-slice_divide_fusion), kind=kOutput, calls=%fused_computation | convolution fusion | flops 7520124928 | bytes 22552576 | tf_op jit(solution)/shard_map/dot_general | solution.py:283
  311.5 23.2 %collective-permute-done.40 = bf16[2,128,3584]{2,1,0:T(8,128)(2,1)S(1)} collective-permute-done((bf16[2,128,3584]{2,1,0:T(8,128)(2,1)S(1)}, bf16[2,128,3584]{2,1,0:T(8,128)(2,1)S(1)}, u32[]{:S(2)}, u32[]{:S(2)}) %collective-permute-start.40) | collective-permute-done | bytes 1835040 | tf_op jit(solution)/shard_map/ppermute | solution.py:23
  338.0 10.8 %collective-permute-done.41 = bf16[1,128,3584]{2,1,0:T(8,128)(2,1)S(1)} collective-permute-done((bf16[1,128,3584]{2,1,0:T(8,128)(2,1)S(1)}, bf16[1,128,3584]{2,1,0:T(8,128)(2,1)S(1)}, u32[]{:S(2)}, u32[]{:S(2)}) %collective-permute-start.41) | collective-permute-done | bytes 917536 | tf_op jit(solution)/shard_map/ppermute | solution.py:23
  (158 shorter events, 123.5 us)
Async XLA Ops:
  32.6 14.5 %collective-permute-start.21 = (f32[4,256,256]{2,1,0:T(8,128)S(1)}, f32[4,256,256]{2,1,0:T(8,128)S(1)}, u32[]{:S(2)}, u32[]{:S(2)}) collective-permute-start(f32[4,256,256]{2,1,0:T(8,128)S(1)} %get-tuple-element.29), channel_id=1, source_target_pairs={{0,1},{1,0},{2,3},{3,2},{4,5},{5,4},{6,7},{7,6},{8,9},{9,8},{10,11... | collective-permute-start | bytes 3145736 | tf_op jit(solution)/shard_map/ppermute | solution.py:23
  41.8 19.1 %collective-permute-start.5 = (f32[4,256,256]{2,1,0:T(8,128)S(1)}, f32[4,256,256]{2,1,0:T(8,128)}, u32[]{:S(2)}, u32[]{:S(2)}) collective-permute-start(f32[4,256,256]{2,1,0:T(8,128)S(1)} %get-tuple-element.23), channel_id=1, source_target_pairs={{0,1},{1,0},{2,3},{3,2},{4,5},{5,4},{6,7},{7,6},{8,9},{9,8},{10,11... | collective-permute-start | bytes 3145736 | tf_op jit(solution)/shard_map/ppermute | solution.py:23
  48.0 18.7 %collective-permute-start.22 = (bf16[2,256,256]{2,1,0:T(8,128)(2,1)}, bf16[2,256,256]{2,1,0:T(8,128)(2,1)S(1)}, u32[]{:S(2)}, u32[]{:S(2)}) collective-permute-start(bf16[2,256,256]{2,1,0:T(8,128)(2,1)} %slice.167), channel_id=1, source_target_pairs={{0,2},{1,5},{2,0},{3,7},{4,6},{5,1},{6,4},{7,3},{8,10},{9,13},{10,... | collective-permute-start | bytes 786440 | tf_op jit(solution)/shard_map/ppermute | solution.py:23
  62.2 12.8 %collective-permute-start.6 = (bf16[2,256,256]{2,1,0:T(8,128)(2,1)S(1)}, bf16[2,256,256]{2,1,0:T(8,128)(2,1)}, u32[]{:S(2)}, u32[]{:S(2)}) collective-permute-start(bf16[2,256,256]{2,1,0:T(8,128)(2,1)S(1)} %slice.169), channel_id=1, source_target_pairs={{0,2},{1,5},{2,0},{3,7},{4,6},{5,1},{6,4},{7,3},{8,10},{9,13},{10,... | collective-permute-start | bytes 786440 | tf_op jit(solution)/shard_map/ppermute | solution.py:23
  66.8 11.3 %collective-permute-start.23 = (bf16[1,256,256]{2,1,0:T(8,128)(2,1)S(1)}, bf16[1,256,256]{2,1,0:T(8,128)(2,1)S(1)}, u32[]{:S(2)}, u32[]{:S(2)}) collective-permute-start(bf16[1,256,256]{2,1,0:T(8,128)(2,1)S(1)} %slice.171), channel_id=1, source_target_pairs={{0,4},{1,3},{2,6},{3,1},{4,0},{5,7},{6,2},{7,5},{8,12},{9,11},{10,... | collective-permute-start | bytes 393224 | tf_op jit(solution)/shard_map/ppermute | solution.py:23
  82.8 11.5 %collective-permute-start.24 = (bf16[1,256,256]{2,1,0:T(8,128)(2,1)S(1)}, bf16[1,256,256]{2,1,0:T(8,128)(2,1)S(1)}, u32[]{:S(2)}, u32[]{:S(2)}) collective-permute-start(bf16[1,256,256]{2,1,0:T(8,128)(2,1)S(1)} %get-tuple-element.44), channel_id=1, source_target_pairs={{0,4},{1,3},{2,6},{3,1},{4,0},{5,7},{6,2},{7,5},{8,12},{9,11},{10,... | collective-permute-start | bytes 393224 | tf_op jit(solution)/shard_map/ppermute | solution.py:23
  94.4 10.2 %collective-permute-start.25 = (bf16[2,256,256]{2,1,0:T(8,128)(2,1)S(1)}, bf16[2,256,256]{2,1,0:T(8,128)(2,1)S(1)}, u32[]{:S(2)}, u32[]{:S(2)}) collective-permute-start(bf16[2,256,256]{2,1,0:T(8,128)(2,1)S(1)} %pad_maximum_fusion.10), channel_id=1, source_target_pairs={{0,2},{1,5},{2,0},{3,7},{4,6},{5,1},{6,4},{7,3},{8,10},{9,13},{10,... | collective-permute-start | bytes 786440 | tf_op jit(solution)/shard_map/ppermute | solution.py:23
  94.5 9.2 %collective-permute-start.8 = (bf16[1,256,256]{2,1,0:T(8,128)(2,1)S(1)}, bf16[1,256,256]{2,1,0:T(8,128)(2,1)S(1)}, u32[]{:S(2)}, u32[]{:S(2)}) collective-permute-start(bf16[1,256,256]{2,1,0:T(8,128)(2,1)S(1)} %get-tuple-element.45), channel_id=1, source_target_pairs={{0,4},{1,3},{2,6},{3,1},{4,0},{5,7},{6,2},{7,5},{8,12},{9,11},{10,... | collective-permute-start | bytes 393224 | tf_op jit(solution)/shard_map/ppermute | solution.py:23
  110.2 12.6 %collective-permute-start.10 = (bf16[4,256,256]{2,1,0:T(8,128)(2,1)S(1)}, bf16[4,256,256]{2,1,0:T(8,128)(2,1)S(1)}, u32[]{:S(2)}, u32[]{:S(2)}) collective-permute-start(bf16[4,256,256]{2,1,0:T(8,128)(2,1)S(1)} %pad_maximum_fusion.4.first_ref), channel_id=1, source_target_pairs={{0,1},{1,0},{2,3},{3,2},{4,5},{5,4},{6,7},{7,6},{8,9},{9,8},{10,11... | collective-permute-start | bytes 1572872 | tf_op jit(solution)/shard_map/ppermute | solution.py:23
  122.8 13.5 %collective-permute-start.27 = (bf16[2,256,896]{2,1,0:T(8,128)(2,1)S(1)}, bf16[2,256,896]{2,1,0:T(8,128)(2,1)S(1)}, u32[]{:S(2)}, u32[]{:S(2)}) collective-permute-start(bf16[2,256,896]{2,1,0:T(8,128)(2,1)S(1)} %get-tuple-element.31), channel_id=1, source_target_pairs={{0,8},{1,17},{2,10},{3,19},{4,12},{5,21},{6,14},{7,23},{8,0},{9,25... | collective-permute-start | bytes 2752520 | tf_op jit(solution)/shard_map/ppermute | solution.py:23
  130.1 20.9 %collective-permute-start.11 = (bf16[2,256,896]{2,1,0:T(8,128)(2,1)S(1)}, bf16[2,256,896]{2,1,0:T(8,128)(2,1)S(1)}, u32[]{:S(2)}, u32[]{:S(2)}) collective-permute-start(bf16[2,256,896]{2,1,0:T(8,128)(2,1)S(1)} %get-tuple-element.25), channel_id=1, source_target_pairs={{0,8},{1,17},{2,10},{3,19},{4,12},{5,21},{6,14},{7,23},{8,0},{9,25... | collective-permute-start | bytes 2752520 | tf_op jit(solution)/shard_map/ppermute | solution.py:23
  136.4 15.8 %collective-permute-start.28 = (bf16[1,256,896]{2,1,0:T(8,128)(2,1)S(1)}, bf16[1,256,896]{2,1,0:T(8,128)(2,1)S(1)}, u32[]{:S(2)}, u32[]{:S(2)}) collective-permute-start(bf16[1,256,896]{2,1,0:T(8,128)(2,1)S(1)} %slice.164), channel_id=1, source_target_pairs={{0,16},{1,9},{2,18},{3,11},{4,20},{5,13},{6,22},{7,15},{8,24},{9,1... | collective-permute-start | bytes 1376264 | tf_op jit(solution)/shard_map/ppermute | solution.py:23
  152.3 12.4 %collective-permute-start.29 = (bf16[1,256,896]{2,1,0:T(8,128)(2,1)S(1)}, bf16[1,256,896]{2,1,0:T(8,128)(2,1)S(1)}, u32[]{:S(2)}, u32[]{:S(2)}) collective-permute-start(bf16[1,256,896]{2,1,0:T(8,128)(2,1)S(1)} %fusion.11), channel_id=1, source_target_pairs={{0,16},{1,9},{2,18},{3,11},{4,20},{5,13},{6,22},{7,15},{8,24},{9,1... | collective-permute-start | bytes 1376264 | tf_op jit(solution)/shard_map/ppermute | solution.py:23
  159.9 13.1 %collective-permute-start.13 = (bf16[1,256,896]{2,1,0:T(8,128)(2,1)S(1)}, bf16[1,256,896]{2,1,0:T(8,128)(2,1)S(1)}, u32[]{:S(2)}, u32[]{:S(2)}) collective-permute-start(bf16[1,256,896]{2,1,0:T(8,128)(2,1)S(1)} %fusion.12), channel_id=1, source_target_pairs={{0,16},{1,9},{2,18},{3,11},{4,20},{5,13},{6,22},{7,15},{8,24},{9,1... | collective-permute-start | bytes 1376264 | tf_op jit(solution)/shard_map/ppermute | solution.py:23
  164.8 13.5 %collective-permute-start.30 = (bf16[2,256,896]{2,1,0:T(8,128)(2,1)S(1)}, bf16[2,256,896]{2,1,0:T(8,128)(2,1)S(1)}, u32[]{:S(2)}, u32[]{:S(2)}) collective-permute-start(bf16[2,256,896]{2,1,0:T(8,128)(2,1)S(1)} %pad_maximum_fusion.3.first_ref), channel_id=1, source_target_pairs={{0,8},{1,17},{2,10},{3,19},{4,12},{5,21},{6,14},{7,23},{8,0},{9,25... | collective-permute-start | bytes 2752520 | tf_op jit(solution)/shard_map/ppermute | solution.py:23
  173.1 15.1 %collective-permute-start.14 = (bf16[2,256,896]{2,1,0:T(8,128)(2,1)S(1)}, bf16[2,256,896]{2,1,0:T(8,128)(2,1)S(1)}, u32[]{:S(2)}, u32[]{:S(2)}) collective-permute-start(bf16[2,256,896]{2,1,0:T(8,128)(2,1)S(1)} %pad_maximum_fusion.2.first_ref), channel_id=1, source_target_pairs={{0,8},{1,17},{2,10},{3,19},{4,12},{5,21},{6,14},{7,23},{8,0},{9,25... | collective-permute-start | bytes 2752520 | tf_op jit(solution)/shard_map/ppermute | solution.py:23
  186.4 10.7 %collective-permute-start.31 = (f32[4,256,256]{2,1,0:T(8,128)S(1)}, f32[4,256,256]{2,1,0:T(8,128)S(1)}, u32[]{:S(2)}, u32[]{:S(2)}) collective-permute-start(f32[4,256,256]{2,1,0:T(8,128)S(1)} %get-tuple-element.33), channel_id=1, source_target_pairs={{0,1},{1,0},{2,3},{3,2},{4,5},{5,4},{6,7},{7,6},{8,9},{9,8},{10,11... | collective-permute-start | bytes 3145736 | tf_op jit(solution)/shard_map/ppermute | solution.py:23
  199.5 15.4 %collective-permute-start.16 = (bf16[2,256,256]{2,1,0:T(8,128)(2,1)S(1)}, bf16[2,256,256]{2,1,0:T(8,128)(2,1)S(1)}, u32[]{:S(2)}, u32[]{:S(2)}) collective-permute-start(bf16[2,256,256]{2,1,0:T(8,128)(2,1)S(1)} %slice.168), channel_id=1, source_target_pairs={{0,2},{1,5},{2,0},{3,7},{4,6},{5,1},{6,4},{7,3},{8,10},{9,13},{10,... | collective-permute-start | bytes 786440 | tf_op jit(solution)/shard_map/ppermute | solution.py:23
  215.3 17.6 %collective-permute-start.34 = (bf16[1,256,256]{2,1,0:T(8,128)(2,1)S(1)}, bf16[1,256,256]{2,1,0:T(8,128)(2,1)S(1)}, u32[]{:S(2)}, u32[]{:S(2)}) collective-permute-start(bf16[1,256,256]{2,1,0:T(8,128)(2,1)S(1)} %fusion.15), channel_id=1, source_target_pairs={{0,4},{1,3},{2,6},{3,1},{4,0},{5,7},{6,2},{7,5},{8,12},{9,11},{10,... | collective-permute-start | bytes 393224 | tf_op jit(solution)/shard_map/ppermute | solution.py:23
  222.0 13.6 %collective-permute-start.18 = (bf16[1,256,256]{2,1,0:T(8,128)(2,1)S(1)}, bf16[1,256,256]{2,1,0:T(8,128)(2,1)S(1)}, u32[]{:S(2)}, u32[]{:S(2)}) collective-permute-start(bf16[1,256,256]{2,1,0:T(8,128)(2,1)S(1)} %fusion.18), channel_id=1, source_target_pairs={{0,4},{1,3},{2,6},{3,1},{4,0},{5,7},{6,2},{7,5},{8,12},{9,11},{10,... | collective-permute-start | bytes 393224 | tf_op jit(solution)/shard_map/ppermute | solution.py:23
  252.9 9.2 %collective-permute-start.37 = (f32[256,512]{1,0:T(8,128)S(1)}, f32[256,512]{1,0:T(8,128)S(1)}, u32[]{:S(2)}, u32[]{:S(2)}) collective-permute-start(f32[256,512]{1,0:T(8,128)S(1)} %convolution_add_fusion.1), channel_id=1, source_target_pairs={{0,8},{1,17},{2,10},{3,19},{4,12},{5,21},{6,14},{7,23},{8,0},{9,25... | collective-permute-start | bytes 1572872 | tf_op jit(solution)/shard_map/ppermute | solution.py:23
  262.2 9.2 %collective-permute-start.38 = (f32[256,512]{1,0:T(8,128)S(1)}, f32[256,512]{1,0:T(8,128)S(1)}, u32[]{:S(2)}, u32[]{:S(2)}) collective-permute-start(f32[256,512]{1,0:T(8,128)S(1)} %add.133), channel_id=1, source_target_pairs={{0,16},{1,9},{2,18},{3,11},{4,20},{5,13},{6,22},{7,15},{8,24},{9,1... | collective-permute-start | bytes 1572872 | tf_op jit(solution)/shard_map/ppermute | solution.py:23
  311.4 23.3 %collective-permute-start.40 = (bf16[2,128,3584]{2,1,0:T(8,128)(2,1)S(1)}, bf16[2,128,3584]{2,1,0:T(8,128)(2,1)S(1)}, u32[]{:S(2)}, u32[]{:S(2)}) collective-permute-start(bf16[2,128,3584]{2,1,0:T(8,128)(2,1)S(1)} %pad_maximum_fusion), channel_id=1, source_target_pairs={{0,8},{1,17},{2,10},{3,19},{4,12},{5,21},{6,14},{7,23},{8,0},{9,25... | collective-permute-start | bytes 5505032 | tf_op jit(solution)/shard_map/ppermute | solution.py:23
  335.3 13.5 %collective-permute-start.41 = (bf16[1,128,3584]{2,1,0:T(8,128)(2,1)S(1)}, bf16[1,128,3584]{2,1,0:T(8,128)(2,1)S(1)}, u32[]{:S(2)}, u32[]{:S(2)}) collective-permute-start(bf16[1,128,3584]{2,1,0:T(8,128)(2,1)S(1)} %slice.163), channel_id=1, source_target_pairs={{0,16},{1,9},{2,18},{3,11},{4,20},{5,13},{6,22},{7,15},{8,24},{9,1... | collective-permute-start | bytes 2752520 | tf_op jit(solution)/shard_map/ppermute | solution.py:23
  (32 other events, 188.6 us)

commit v2 on v1

--- a/solution.py
+++ b/solution.py
@@ -306,159 +306,129 @@
         sum_ref[...] += term
 
 
-def rows_plain_kernel(turned, order_ref, weight_ref, right_ref, send_ref, keep_ref, sum_ref):
-    step = pl.program_id(0)
-    add_up(step, dot(weight_ref[...], right_ref[...]), sum_ref)
-
-    @pl.when(step == pl.num_programs(0) - 1)
-    def _():
-        gather_rows(order_ref, sum_ref, send_ref, keep_ref, turned)
-
-
 def two_halves(size, shape, send_type):
     dims = (size // 2,) + shape
-    shapes = (jax.ShapeDtypeStruct(dims, send_type), jax.ShapeDtypeStruct(dims, F32))
-    return shapes, (pl.BlockSpec(dims, lambda *_: (0, 0, 0)),) * 2
-
-
-def rows_times(weight, right, part, width, rows, turned):
+    return (jax.ShapeDtypeStruct(dims, send_type), jax.ShapeDtypeStruct(dims, F32))
+
+
+def product_call(kernel, name, out_shape, scratch, weight, width, indices, arrays):
     height, depth = weight.shape
-    block = height // rows.size
-    chunk = 512 if depth % 512 == 0 else depth
-    shapes, specs = two_halves(rows.size, (width, block) if turned else (block, width), F32)
+    smem, vmem = (pl.BlockSpec(memory_space=space) for space in (pltpu.SMEM, pltpu.VMEM))
     return pl.pallas_call(
-        functools.partial(rows_plain_kernel, turned),
-        out_shape=shapes,
-        grid_spec=pltpu.PrefetchScalarGridSpec(
-            num_scalar_prefetch=1,
-            grid=(depth // chunk,),
-            in_specs=[
-                pl.BlockSpec((height, chunk), lambda i, order: (0, i)),
-                pl.BlockSpec((chunk, width), lambda i, order: (i, part)),
-            ],
-            out_specs=specs,
-            scratch_shapes=[pltpu.VMEM((height, width), F32)],
-        ),
+        kernel,
+        out_shape=out_shape,
+        in_specs=[smem] * len(indices) + [vmem] * (1 + len(arrays)),
+        out_specs=(vmem, vmem),
+        scratch_shapes=[scratch],
         compiler_params=pltpu.CompilerParams(vmem_limit_bytes=LIMIT),
         cost_estimate=pl.CostEstimate(
             flops=2 * height * depth * width,
             bytes_accessed=2 * (height + width) * depth,
             transcendentals=0,
         ),
-        name="rows_times",
-    )(rows.sending_first(), weight, right)
+        name=name,
+    )(*indices, weight, *arrays)
+
+
+def rows_plain_kernel(part, width, turned, order_ref, weight_ref, right_ref, send_ref, keep_ref, sum_ref):
+    depth = weight_ref.shape[1]
+    chunk = 512 if depth % 512 == 0 else depth
+
+    @pl.loop(0, depth // chunk)
+    def _(i):
+        here = pl.ds(pl.multiple_of(i * chunk, chunk), chunk)
+        right = right_ref[here, part * width : (part + 1) * width]
+        add_up(i, dot(weight_ref[:, here], right), sum_ref)
+
+    gather_rows(order_ref, sum_ref, send_ref, keep_ref, turned)
+
+
+def rows_times(weight, right, part, width, rows, turned):
+    height = weight.shape[0]
+    block = height // rows.size
+    shapes = two_halves(rows.size, (width, block) if turned else (block, width), F32)
+    return product_call(
+        functools.partial(rows_plain_kernel, part, width, turned),
+        "rows_times",
+        shapes,
+        pltpu.VMEM((height, width), F32),
+        weight,
+        width,
+        (rows.sending_first(),),
+        (right,),
+    )
 
 
 def rows_joined_kernel(rows_ref, cols_ref, weight_ref, first_ref, second_ref, send_ref, keep_ref, sum_ref):
-    step, steps = pl.program_id(0), pl.num_programs(0)
-    right = jnp.where(step < steps // 2, first_ref[0], second_ref[0])
-    add_up(step, dot(weight_ref[...], right, NT), sum_ref)
-
-    @pl.when(step == steps - 1)
-    def _():
-        gather_rows(rows_ref, sum_ref, send_ref, keep_ref, False)
+    half, _, own = first_ref.shape
+    for part, right_ref in enumerate((first_ref, second_ref)):
+
+        @pl.loop(0, half)
+        def _(i):
+            block = cols_ref[i + half * (1 - part)]
+            here = pl.ds(pl.multiple_of(block * own, 128), own)
+            term = dot(weight_ref[:, here], right_ref[i], NT)
+            add_up(i + half * part, term, sum_ref)
+
+    gather_rows(rows_ref, sum_ref, send_ref, keep_ref, False)
 
 
 def rows_times_joined(weight, halves, rows, cols):
-    height, depth = weight.shape
-    block = height // rows.size
-    half, width, own = halves[0].shape
+    height = weight.shape[0]
+    width, own = halves[0].shape[1:]
     if own % 128:
         return rows_times(weight, cols.in_order(halves, 1).T, 0, width, rows, False)
-    shapes, specs = two_halves(rows.size, (block, width), F32)
-    return pl.pallas_call(
+    return product_call(
         rows_joined_kernel,
-        out_shape=shapes,
-        grid_spec=pltpu.PrefetchScalarGridSpec(
-            num_scalar_prefetch=2,
-            grid=(cols.size,),
-            in_specs=[
-                pl.BlockSpec(
-                    (height, own), lambda i, _, order: (0, order[(i + half) % (2 * half)])
-                ),
-                pl.BlockSpec((1, width, own), lambda i, *_: (jnp.minimum(i, half - 1), 0, 0)),
-                pl.BlockSpec((1, width, own), lambda i, *_: (jnp.maximum(i - half, 0), 0, 0)),
-            ],
-            out_specs=specs,
-            scratch_shapes=[pltpu.VMEM((height, width), F32)],
-        ),
-        compiler_params=pltpu.CompilerParams(vmem_limit_bytes=LIMIT),
-        cost_estimate=pl.CostEstimate(
-            flops=2 * height * depth * width,
-            bytes_accessed=2 * (height + width) * depth,
-            transcendentals=0,
-        ),
-        name="rows_times_joined",
-    )(rows.sending_first(), cols.sending_first(), weight, *halves)
-
-
-def put(value, send_ref, keep_ref):
-    step, half = pl.program_id(0), pl.num_programs(0) // 2
-
-    @pl.when(step < half)
-    def _():
-        send_ref[0] = value.astype(send_ref.dtype)
-
-    @pl.when(step >= half)
-    def _():
-        keep_ref[0] = value.astype(keep_ref.dtype)
-
-
-def halves_out(size, shape, send_type):
-    half = size // 2
-    dims = (half,) + shape
-    shapes = (jax.ShapeDtypeStruct(dims, send_type), jax.ShapeDtypeStruct(dims, F32))
-    specs = (
-        pl.BlockSpec((1,) + shape, lambda i, *_: (jnp.minimum(i, half - 1), 0, 0)),
-        pl.BlockSpec((1,) + shape, lambda i, *_: (jnp.maximum(i - half, 0), 0, 0)),
+        "rows_times_joined",
+        two_halves(rows.size, (height // rows.size, width), F32),
+        pltpu.VMEM((height, width), F32),
+        weight,
+        width,
+        (rows.sending_first(), cols.sending_first()),
+        halves,
     )
-    return shapes, specs
-
-
-def join(order_ref, halves, whole_ref, width):
-    @pl.when(pl.program_id(0) == 0)
-    def _():
-        count = halves[0].shape[0]
-        for v in range(2 * count):
-            block = order_ref[(v + count) % (2 * count)]
-            there = pl.ds(pl.multiple_of(block * width, 128), width)
-            whole_ref[:, there] = halves[v // count][v % count]
-
-
-def cols_kernel(cols_ref, rows_ref, weight_ref, first_ref, second_ref, send_ref, keep_ref, whole_ref):
-    join(rows_ref, (first_ref, second_ref), whole_ref, first_ref.shape[2])
-    put(dot(whole_ref[...], weight_ref[...]), send_ref, keep_ref)
-
-
-def cols_times_joined(weight, halves, rows, cols):
+
+
+def cols_kernel(
+    cols_ref, rows_ref, weight_ref, scale_ref, first_ref, second_ref, send_ref, keep_ref, whole_ref
+):
+    count, _, own = first_ref.shape
+    for v in range(2 * count):
+        block = rows_ref[(v + count) % (2 * count)]
+        there = pl.ds(pl.multiple_of(block * own, 128), own)
+        value = (first_ref, second_ref)[v // count][v % count]
+        whole_ref[:, there] = (value.astype(F32) * scale_ref[:, there]).astype(BF16)
+
+    half, _, block = send_ref.shape
+    for part, out_ref in enumerate((send_ref, keep_ref)):
+
+        @pl.loop(0, half)
+        def _(i):
+            here = pl.ds(pl.multiple_of(cols_ref[i + half * part] * block, 128), block)
+            out_ref[i] = dot(whole_ref[...], weight_ref[:, here]).astype(out_ref.dtype)
+
+
+def cols_times_joined(weight, scale, halves, rows, cols):
     height, depth = weight.shape
     block = depth // cols.size
     width, own = halves[0].shape[1:]
     if own % 128 or block % 128:
-        full = dot(rows.in_order(halves, 1), weight).reshape(width, cols.size, block)
+        left = (scale * rows.in_order(halves, 1)).astype(BF16)
+        full = dot(left, weight).reshape(width, cols.size, block)
         order = cols.sending_first()
         full = jnp.stack([full[:, order[i]] for i in range(cols.size)])
         return full[: cols.size // 2].astype(BF16), full[cols.size // 2 :]
-    shapes, specs = halves_out(cols.size, (width, block), BF16)
-    fixed = pl.BlockSpec(halves[0].shape, lambda i, *_: (0, 0, 0))
-    return pl.pallas_call(
+    return product_call(
         cols_kernel,
-        out_shape=shapes,
-        grid_spec=pltpu.PrefetchScalarGridSpec(
-            num_scalar_prefetch=2,
-            grid=(cols.size,),
-            in_specs=[pl.BlockSpec((height, block), lambda i, order, _: (0, order[i])), fixed, fixed],
-            out_specs=specs,
-            scratch_shapes=[pltpu.VMEM((width, height), BF16)],
-        ),
-        compiler_params=pltpu.CompilerParams(vmem_limit_bytes=LIMIT),
-        cost_estimate=pl.CostEstimate(
-            flops=2 * height * depth * width,
-            bytes_accessed=2 * (height + width) * depth,
-            transcendentals=0,
-        ),
-        name="cols_times_joined",
-    )(cols.sending_first(), rows.sending_first(), weight, *halves)
+        "cols_times_joined",
+        two_halves(cols.size, (width, block), BF16),
+        pltpu.VMEM((width, height), BF16),
+        weight,
+        width,
+        (cols.sending_first(), rows.sending_first()),
+        (scale[None], *halves),
+    )
 
 
 def settle_kernel(order_ref, *refs):
@@ -505,7 +475,6 @@
     over_col, over_row = Halving("col"), Halving("row")
 
     mass = local_mass(activations, out_grads, valid_len)
-    mass, sketch = lax.optimization_barrier((mass, sketch))
     fisher = sum_everywhere(mass.reshape(-1, 128)).reshape(width)
     mean = jnp.sum(fisher) / width + 1e-06
     square_scale = lax.dynamic_slice_in_dim(fisher, row * rows_here, rows_here) / mean
@@ -513,8 +482,8 @@
 
     def second_of(part):
         raw = over_col.scatter_sum(*rows_times(weight, sketch, part, half, over_col, True))
-        first = (own_square * raw).astype(BF16)
-        parts = cols_times_joined(weight, over_col.gather(first), over_col, over_row)
+        first = over_col.gather(raw.astype(BF16))
+        parts = cols_times_joined(weight, square_scale, first, over_col, over_row)
         projected = over_row.gather(over_row.scatter_sum(*parts).astype(BF16))
         parts = rows_times_joined(weight, projected, over_col, over_row)
         return over_col.gather(over_col.scatter_sum(*parts).astype(BF16))
@@ -529,19 +498,23 @@
     other = swap(gram, lambda parity: 0, lambda parity: 1)
     gram = jnp.concatenate([jnp.where(even, gram, other), jnp.where(even, other, gram)])
 
-    high, low = split(inverse_factor(gram))
-    basis = dot(second, high, NT) + dot(second, low, NT)
-    parts = dot((square_scale[:, None] * basis).astype(BF16), weight, rows_of).astype(BF16)
-    parts = parts.reshape(row_count, rank // row_count, cols_here)
+    inverse = inverse_factor(gram)
     order = over_row.sending_first()
-    take = lambda places: jnp.stack(
-        [lax.dynamic_index_in_dim(parts, order[i], 0, keepdims=False) for i in places]
+    blocks = inverse.reshape(row_count, rank // row_count, rank)
+
+    def coeffs_of(places):
+        part = [lax.dynamic_index_in_dim(blocks, order[i], 0, keepdims=False) for i in places]
+        high, low = split(jnp.concatenate(part))
+        basis = dot(second, high, NT) + dot(second, low, NT)
+        parts = dot((square_scale[:, None] * basis).astype(BF16), weight, rows_of)
+        return parts.astype(BF16).reshape(len(part), -1, cols_here)
+
+    coeffs = over_row.scatter_sum(
+        coeffs_of(range(row_count // 2)), coeffs_of(range(row_count // 2, row_count))
     )
-    coeffs = over_row.scatter_sum(
-        take(range(row_count // 2)), take(range(row_count // 2, row_count))
-    )
-
-    basis = lax.dynamic_slice_in_dim(basis, col * own_rows, own_rows)
+
+    own = lax.dynamic_slice_in_dim(second, col * own_rows, own_rows)
+    basis = sum(dot(own, term, NT) for term in split(inverse))
     basis = basis * (jnp.sqrt(own_square)[:, None] * math.sqrt(width))
     return basis, coeffs * math.sqrt(cols_here * col_count)
 

time: 351 us -> 333 us (0.949)
  waiting for transfers between devices: 179 us -> 127 us
  starting transfers between devices: 38.1 us -> 67.2 us
  matrix products: 17.3 us -> 33.6 us
  Pallas kernels: 80.9 us -> 73.2 us
    ppermute x42, waiting for transfers between devices: 179 us -> 127 us  [swap(): return lax.ppermute(block, AXES, pairs)]
    ppermute x42, starting transfers between devices: 38.1 us -> 67.2 us  [swap(): return lax.ppermute(block, AXES, pairs)]
    dot_general x5 -> x8, matrix products: 17.3 us -> 33.6 us  [dot(): lax.dot_general(left, right, (dims, ((), ())), preferred_element_type=F32)]
    pallas_call x6, Pallas kernels: 47.6 us -> 39.9 us  [product_call(): pl.pallas_call(kernel, out_shape=out_shape, in_specs=[smem] * len(indices...]
    unnamed x28 -> x30, local copies, waits for them, and re-layouts: 22.1 us -> 18.7 us
  transfers between devices with their start and end apart: 42 -> 42, of which waited for: 31 -> 29; matrix products, arithmetic and copies ran while one was open for 2% -> 6% of each run, Pallas kernels for 11% -> 13%
where the time goes in v2:
time: 333 us; the launch traced here: 332 us
  waiting for transfers between devices  127 us (38%)
  Pallas kernels  73.2 us (22%)
  starting transfers between devices  67.2 us (20%)
  matrix products  33.6 us (10%)
  local copies, waits for them, and re-layouts  20.8 us (6%)
  other arithmetic  8.26 us (2%)
    ppermute x42, waiting for transfers between devices, swap(): return lax.ppermute(block, AXES, pairs)  127 us
    ppermute x42, starting transfers between devices, swap(): return lax.ppermute(block, AXES, pairs)  67.2 us
    pallas_call x6, Pallas kernels, product_call(): pl.pallas_call(kernel, out_shape=out_shape, in_specs=[smem] * len(indices...  39.9 us
    dot_general x8, matrix products, dot(): lax.dot_general(left, right, (dims, ((), ())), preferred_element_type=F32)  33.6 us
    pallas_call x1, Pallas kernels, inverse_factor(): pl.pallas_call(inverse_factor_kernel, out_shape=jax.ShapeDtypeStruct((siz...  22.7 us
    unnamed x30, local copies, waits for them, and re-layouts  18.7 us
    pallas_call x1, Pallas kernels, local_mass(): pl.pallas_call(row_mass_kernel, out_shape=jax.ShapeDtypeStruct((1, width)...  7.3 us
  transfers between devices with their start and end apart: 42, of which 29 were waited for; matrix products, arithmetic and copies ran while one was open for 6% of the time, Pallas kernels for 13%

profile of v2, /device:TPU:0, one launch (start us, length us, event | category | flops | bytes accessed | tf_op | source)
XLA Modules:
  0.0 332.5 jit_solution(8124612048208846440)
XLA Ops:
  0.7 5.2 %copy-done = bf16[2048,3584]{1,0:T(8,128)(2,1)S(1)} copy-done((bf16[2048,3584]{1,0:T(8,128)(2,1)S(1)}, bf16[2048,3584]{1,0:T(8,128)(2,1)}, u32[]{:S(2)}) %copy-start) | copy-done | bytes 14680088
  8.0 7.4 %rows_times.3 = (f32[4,256,256]{2,1,0:T(8,128)S(1)}, f32[4,256,256]{2,1,0:T(8,128)S(1)}) custom-call(s32[8]{0:T(128)S(1)} %stack.36.order_ref.rows_ref, bf16[2048,3584]{1,0:T(8,128)(2,1)S(1)} %copy-done, bf16[3584,512]{1,0:T(8,128)(2,1)S(1)} %copy-done.2), custom_call_target="tpu_custom_call" | custom-call | flops 3758096384 | bytes 16515072 | tf_op jit(solution)/shard_map/rows_times/pallas_call | solution.py:317
  15.9 7.4 %rows_times.2 = (f32[4,256,256]{2,1,0:T(8,128)S(1)}, f32[4,256,256]{2,1,0:T(8,128)S(1)}) custom-call(s32[8]{0:T(128)S(1)} %stack.36.order_ref.rows_ref, bf16[2048,3584]{1,0:T(8,128)(2,1)S(1)} %copy-done, bf16[3584,512]{1,0:T(8,128)(2,1)S(1)} %copy-done.2), custom_call_target="tpu_custom_call" | custom-call | flops 3758096384 | bytes 16515072 | tf_op jit(solution)/shard_map/rows_times/pallas_call | solution.py:317
  51.5 7.2 %collective-permute-start.25 = (bf16[2,256,256]{2,1,0:T(8,128)(2,1)S(1)}, bf16[2,256,256]{2,1,0:T(8,128)(2,1)S(1)}, u32[]{:S(2)}, u32[]{:S(2)}) collective-permute-start(bf16[2,256,256]{2,1,0:T(8,128)(2,1)S(1)} %pad_maximum_fusion.11), channel_id=1, source_target_pairs={{0,2},{1,5},{2,0},{3,7},{4,6},{5,1},{6,4},{7,3},{8,10},{9,13},{10,... | collective-permute-start | bytes 786440 | tf_op jit(solution)/shard_map/ppermute | solution.py:23
  58.7 7.3 %row_mass.1 = f32[1,8192]{1,0:T(1,128)S(1)} custom-call(bf16[2,256,8192]{2,1,0:T(8,128)(2,1)S(1)} %bitcast.44, bf16[2,512,256]{2,1,0:T(8,128)(2,1)S(1)} %get-tuple-element.16.gram_ref, f32[2,256,128]{2,1,0:T(8,128)S(1)} %get-tuple-element.17.scale_ref), custom_call_target="tpu_custom_call" | custom-call | flops 4294967296 | bytes 8388608 | tf_op jit(solution)/shard_map/row_mass/pallas_call | solution.py:170
  87.1 5.2 %copy-done.1 = bf16[2048,3584]{1,0:T(8,128)(2,1)S(1)} copy-done((bf16[2048,3584]{1,0:T(8,128)(2,1)S(1)}, bf16[2048,3584]{1,0:T(8,128)(2,1)}, u32[]{:S(2)}) %copy-start.1) | copy-done | bytes 14680088
  92.2 5.8 %cols_times_joined.3 = (bf16[2,256,896]{2,1,0:T(8,128)(2,1)S(1)}, f32[2,256,896]{2,1,0:T(8,128)S(1)}) custom-call(s32[4]{0:T(128)S(1)} %pad_add_fusion.cols_ref, s32[8]{0:T(128)S(1)} %stack.36.order_ref.rows_ref, bf16[2048,3584]{1,0:T(8,128)(2,1)S(1)} %copy-done.1, f32[1,2048]{1,0:T(1,128)S(1)} %bitcast.39, ...), custom_call_target="tpu_custom_call" | custom-call | flops 3758096384 | bytes 16515072 | tf_op jit(solution)/shard_map/cols_times_joined/pallas_call | solution.py:317
  99.7 6.0 %cols_times_joined.2 = (bf16[2,256,896]{2,1,0:T(8,128)(2,1)S(1)}, f32[2,256,896]{2,1,0:T(8,128)S(1)}) custom-call(s32[4]{0:T(128)S(1)} %pad_add_fusion.cols_ref, s32[8]{0:T(128)S(1)} %stack.36.order_ref.rows_ref, bf16[2048,3584]{1,0:T(8,128)(2,1)S(1)} %copy-done.1, f32[1,2048]{1,0:T(1,128)S(1)} %bitcast.40, ...), custom_call_target="tpu_custom_call" | custom-call | flops 3758096384 | bytes 16515072 | tf_op jit(solution)/shard_map/cols_times_joined/pallas_call | solution.py:317
  106.2 5.3 %collective-permute-done.27 = bf16[2,256,896]{2,1,0:T(8,128)(2,1)S(1)} collective-permute-done((bf16[2,256,896]{2,1,0:T(8,128)(2,1)S(1)}, bf16[2,256,896]{2,1,0:T(8,128)(2,1)S(1)}, u32[]{:S(2)}, u32[]{:S(2)}) %collective-permute-start.27) | collective-permute-done | bytes 917536 | tf_op jit(solution)/shard_map/ppermute | solution.py:23
  113.3 14.2 %collective-permute-done.11 = bf16[2,256,896]{2,1,0:T(8,128)(2,1)S(1)} collective-permute-done((bf16[2,256,896]{2,1,0:T(8,128)(2,1)S(1)}, bf16[2,256,896]{2,1,0:T(8,128)(2,1)S(1)}, u32[]{:S(2)}, u32[]{:S(2)}) %collective-permute-start.11) | collective-permute-done | bytes 917536 | tf_op jit(solution)/shard_map/ppermute | solution.py:23
  130.0 6.3 %collective-permute-done.12 = bf16[1,256,896]{2,1,0:T(8,128)(2,1)S(1)} collective-permute-done((bf16[1,256,896]{2,1,0:T(8,128)(2,1)S(1)}, bf16[1,256,896]{2,1,0:T(8,128)(2,1)S(1)}, u32[]{:S(2)}, u32[]{:S(2)}) %collective-permute-start.12) | collective-permute-done | bytes 458784 | tf_op jit(solution)/shard_map/ppermute | solution.py:23
  145.3 7.9 %collective-permute-done.13 = bf16[1,256,896]{2,1,0:T(8,128)(2,1)S(1)} collective-permute-done((bf16[1,256,896]{2,1,0:T(8,128)(2,1)S(1)}, bf16[1,256,896]{2,1,0:T(8,128)(2,1)S(1)}, u32[]{:S(2)}, u32[]{:S(2)}) %collective-permute-start.13) | collective-permute-done | bytes 458784 | tf_op jit(solution)/shard_map/ppermute | solution.py:23
  157.0 6.6 %rows_times_joined.3 = (f32[4,256,256]{2,1,0:T(8,128)S(1)}, f32[4,256,256]{2,1,0:T(8,128)S(1)}) custom-call(s32[8]{0:T(128)S(1)} %stack.36.order_ref.rows_ref, s32[4]{0:T(128)S(1)} %pad_add_fusion.cols_ref, bf16[2048,3584]{1,0:T(8,128)(2,1)S(1)} %copy-done.1, bf16[2,256,896]{2,1,0:T(8,128)(2,1)S(1)} %pad_maximum_fusion.2.first_ref, ...), custom_call_target="tpu_custom_call" | custom-call | flops 3758096384 | bytes 16515072 | tf_op jit(solution)/shard_map/rows_times_joined/pallas_call | solution.py:317
  166.8 6.6 %rows_times_joined.2 = (f32[4,256,256]{2,1,0:T(8,128)S(1)}, f32[4,256,256]{2,1,0:T(8,128)S(1)}) custom-call(s32[8]{0:T(128)S(1)} %stack.36.order_ref.rows_ref, s32[4]{0:T(128)S(1)} %pad_add_fusion.cols_ref, bf16[2048,3584]{1,0:T(8,128)(2,1)S(1)} %copy-done.1, bf16[2,256,896]{2,1,0:T(8,128)(2,1)S(1)} %pad_maximum_fusion.1.first_ref, ...), custom_call_target="tpu_custom_call" | custom-call | flops 3758096384 | bytes 16515072 | tf_op jit(solution)/shard_map/rows_times_joined/pallas_call | solution.py:317
  173.7 6.1 %collective-permute-start.32 = (bf16[2,256,256]{2,1,0:T(8,128)(2,1)S(1)}, bf16[2,256,256]{2,1,0:T(8,128)(2,1)S(1)}, u32[]{:S(2)}, u32[]{:S(2)}) collective-permute-start(bf16[2,256,256]{2,1,0:T(8,128)(2,1)S(1)} %slice.162), channel_id=1, source_target_pairs={{0,2},{1,5},{2,0},{3,7},{4,6},{5,1},{6,4},{7,3},{8,10},{9,13},{10,... | collective-permute-start | bytes 786440 | tf_op jit(solution)/shard_map/ppermute | solution.py:23
  202.5 6.6 %collective-permute-done.18 = bf16[1,256,256]{2,1,0:T(8,128)(2,1)S(1)} collective-permute-done((bf16[1,256,256]{2,1,0:T(8,128)(2,1)S(1)}, bf16[1,256,256]{2,1,0:T(8,128)(2,1)S(1)}, u32[]{:S(2)}, u32[]{:S(2)}) %collective-permute-start.18) | collective-permute-done | bytes 131104 | tf_op jit(solution)/shard_map/ppermute | solution.py:23
  213.4 5.5 %collective-permute-done.19 = bf16[2,256,256]{2,1,0:T(8,128)(2,1)S(1)} collective-permute-done((bf16[2,256,256]{2,1,0:T(8,128)(2,1)S(1)}, bf16[2,256,256]{2,1,0:T(8,128)(2,1)S(1)}, u32[]{:S(2)}, u32[]{:S(2)}) %collective-permute-start.19) | collective-permute-done | bytes 262176 | tf_op jit(solution)/shard_map/ppermute | solution.py:23
  228.9 7.7 %collective-permute-done.37 = f32[256,512]{1,0:T(8,128)S(1)} collective-permute-done((f32[256,512]{1,0:T(8,128)S(1)}, f32[256,512]{1,0:T(8,128)S(1)}, u32[]{:S(2)}, u32[]{:S(2)}) %collective-permute-start.37) | collective-permute-done | bytes 524320 | tf_op jit(solution)/shard_map/ppermute | solution.py:23
  239.2 7.2 %collective-permute-done.38 = f32[256,512]{1,0:T(8,128)S(1)} collective-permute-done((f32[256,512]{1,0:T(8,128)S(1)}, f32[256,512]{1,0:T(8,128)S(1)}, u32[]{:S(2)}, u32[]{:S(2)}) %collective-permute-start.38) | collective-permute-done | bytes 524320 | tf_op jit(solution)/shard_map/ppermute | solution.py:23
  248.6 22.7 %inverse_factor.1 = f32[512,512]{1,0:T(8,128)S(1)} custom-call(f32[512,512]{1,0:T(8,128)S(1)} %pad_maximum_fusion.gram_ref), custom_call_target="tpu_custom_call" | custom-call | flops 5368709120 | bytes 2097152 | tf_op jit(solution)/shard_map/inverse_factor/pallas_call | solution.py:265
  275.0 12.2 %convolution_convert_fusion = bf16[256,3584]{1,0:T(8,128)(2,1)} fusion(bf16[2048,3584]{1,0:T(8,128)(2,1)} %weight_ref.11, f32[2048,256]{1,0:T(8,128)} %fusion.23, bf16[2048,512]{1,0:T(8,128)(2,1)S(1)} %settle.1, f32[2048]{0:T(1024)S(1)} %dynamic-slice_divide_fusion, f32[128,512]{1,0:T(8,128)} %copy-done.12, f32[128,512]{1,0:T(8,128)} %copy-done.11), kind=kOutput, calls=%fused_computation | convolution fusion | flops 4297850880 | bytes 21241856 | tf_op jit(solution)/shard_map/dot_general | solution.py:283
  291.8 12.0 %convolution_convert_fusion.1 = bf16[256,3584]{1,0:T(8,128)(2,1)} fusion(bf16[2048,3584]{1,0:T(8,128)(2,1)} %weight_ref.11, f32[2048,256]{1,0:T(8,128)} %fusion.25, bf16[2048,512]{1,0:T(8,128)(2,1)S(1)} %settle.1, f32[2048]{0:T(1024)S(1)} %dynamic-slice_divide_fusion, f32[128,512]{1,0:T(8,128)S(1)} %get-tuple-element.32, f32[128,512]{1,0:T(8,128)} %get-tuple-element.33), kind=kOutput, calls=%fused_computation.1 | convolution fusion | flops 4297850880 | bytes 21241856 | tf_op jit(solution)/shard_map/dot_general | solution.py:283
  303.8 6.9 %collective-permute-done.40 = bf16[2,128,3584]{2,1,0:T(8,128)(2,1)} collective-permute-done((bf16[2,128,3584]{2,1,0:T(8,128)(2,1)}, bf16[2,128,3584]{2,1,0:T(8,128)(2,1)}, u32[]{:S(2)}, u32[]{:S(2)}) %collective-permute-start.40) | collective-permute-done | bytes 1835040 | tf_op jit(solution)/shard_map/ppermute | solution.py:23
  319.7 10.1 %collective-permute-done.41 = bf16[1,128,3584]{2,1,0:T(8,128)(2,1)} collective-permute-done((bf16[1,128,3584]{2,1,0:T(8,128)(2,1)}, bf16[1,128,3584]{2,1,0:T(8,128)(2,1)}, u32[]{:S(2)}, u32[]{:S(2)}) %collective-permute-start.41) | collective-permute-done | bytes 917536 | tf_op jit(solution)/shard_map/ppermute | solution.py:23
  (162 shorter events, 135.2 us)
Async XLA Ops:
  23.7 9.9 %collective-permute-start.22 = (bf16[2,256,256]{2,1,0:T(8,128)(2,1)S(1)}, bf16[2,256,256]{2,1,0:T(8,128)(2,1)S(1)}, u32[]{:S(2)}, u32[]{:S(2)}) collective-permute-start(bf16[2,256,256]{2,1,0:T(8,128)(2,1)S(1)} %slice.163), channel_id=1, source_target_pairs={{0,2},{1,5},{2,0},{3,7},{4,6},{5,1},{6,4},{7,3},{8,10},{9,13},{10,... | collective-permute-start | bytes 786440 | tf_op jit(solution)/shard_map/ppermute | solution.py:23
  26.9 15.1 %collective-permute-start.6 = (bf16[2,256,256]{2,1,0:T(8,128)(2,1)S(1)}, bf16[2,256,256]{2,1,0:T(8,128)(2,1)S(1)}, u32[]{:S(2)}, u32[]{:S(2)}) collective-permute-start(bf16[2,256,256]{2,1,0:T(8,128)(2,1)S(1)} %slice.165), channel_id=1, source_target_pairs={{0,2},{1,5},{2,0},{3,7},{4,6},{5,1},{6,4},{7,3},{8,10},{9,13},{10,... | collective-permute-start | bytes 786440 | tf_op jit(solution)/shard_map/ppermute | solution.py:23
  33.7 10.5 %collective-permute-start.23 = (bf16[1,256,256]{2,1,0:T(8,128)(2,1)S(1)}, bf16[1,256,256]{2,1,0:T(8,128)(2,1)S(1)}, u32[]{:S(2)}, u32[]{:S(2)}) collective-permute-start(bf16[1,256,256]{2,1,0:T(8,128)(2,1)S(1)} %slice.167), channel_id=1, source_target_pairs={{0,4},{1,3},{2,6},{3,1},{4,0},{5,7},{6,2},{7,5},{8,12},{9,11},{10,... | collective-permute-start | bytes 393224 | tf_op jit(solution)/shard_map/ppermute | solution.py:23
  48.2 19.1 %collective-permute-start.8 = (bf16[1,256,256]{2,1,0:T(8,128)(2,1)S(1)}, bf16[1,256,256]{2,1,0:T(8,128)(2,1)S(1)}, u32[]{:S(2)}, u32[]{:S(2)}) collective-permute-start(bf16[1,256,256]{2,1,0:T(8,128)(2,1)S(1)} %fusion.30), channel_id=1, source_target_pairs={{0,4},{1,3},{2,6},{3,1},{4,0},{5,7},{6,2},{7,5},{8,12},{9,11},{10,... | collective-permute-start | bytes 393224 | tf_op jit(solution)/shard_map/ppermute | solution.py:23
  51.5 17.9 %collective-permute-start.25 = (bf16[2,256,256]{2,1,0:T(8,128)(2,1)S(1)}, bf16[2,256,256]{2,1,0:T(8,128)(2,1)S(1)}, u32[]{:S(2)}, u32[]{:S(2)}) collective-permute-start(bf16[2,256,256]{2,1,0:T(8,128)(2,1)S(1)} %pad_maximum_fusion.11), channel_id=1, source_target_pairs={{0,2},{1,5},{2,0},{3,7},{4,6},{5,1},{6,4},{7,3},{8,10},{9,13},{10,... | collective-permute-start | bytes 786440 | tf_op jit(solution)/shard_map/ppermute | solution.py:23
  67.4 16.1 %collective-permute-start.9 = (bf16[2,256,256]{2,1,0:T(8,128)(2,1)S(1)}, bf16[2,256,256]{2,1,0:T(8,128)(2,1)S(1)}, u32[]{:S(2)}, u32[]{:S(2)}) collective-permute-start(bf16[2,256,256]{2,1,0:T(8,128)(2,1)S(1)} %pad_maximum_fusion.9), channel_id=1, source_target_pairs={{0,2},{1,5},{2,0},{3,7},{4,6},{5,1},{6,4},{7,3},{8,10},{9,13},{10,... | collective-permute-start | bytes 786440 | tf_op jit(solution)/shard_map/ppermute | solution.py:23
  69.5 17.6 %collective-permute-start.26 = (bf16[4,256,256]{2,1,0:T(8,128)(2,1)S(1)}, bf16[4,256,256]{2,1,0:T(8,128)(2,1)S(1)}, u32[]{:S(2)}, u32[]{:S(2)}) collective-permute-start(bf16[4,256,256]{2,1,0:T(8,128)(2,1)S(1)} %pad_maximum_fusion.5.first_ref), channel_id=1, source_target_pairs={{0,1},{1,0},{2,3},{3,2},{4,5},{5,4},{6,7},{7,6},{8,9},{9,8},{10,11... | collective-permute-start | bytes 1572872 | tf_op jit(solution)/shard_map/ppermute | solution.py:23
  83.5 16.2 %collective-permute-start.10 = (bf16[4,256,256]{2,1,0:T(8,128)(2,1)S(1)}, bf16[4,256,256]{2,1,0:T(8,128)(2,1)S(1)}, u32[]{:S(2)}, u32[]{:S(2)}) collective-permute-start(bf16[4,256,256]{2,1,0:T(8,128)(2,1)S(1)} %pad_maximum_fusion.3.first_ref), channel_id=1, source_target_pairs={{0,1},{1,0},{2,3},{3,2},{4,5},{5,4},{6,7},{7,6},{8,9},{9,8},{10,11... | collective-permute-start | bytes 1572872 | tf_op jit(solution)/shard_map/ppermute | solution.py:23
  98.0 13.5 %collective-permute-start.27 = (bf16[2,256,896]{2,1,0:T(8,128)(2,1)S(1)}, bf16[2,256,896]{2,1,0:T(8,128)(2,1)S(1)}, u32[]{:S(2)}, u32[]{:S(2)}) collective-permute-start(bf16[2,256,896]{2,1,0:T(8,128)(2,1)S(1)} %get-tuple-element.27), channel_id=1, source_target_pairs={{0,8},{1,17},{2,10},{3,19},{4,12},{5,21},{6,14},{7,23},{8,0},{9,25... | collective-permute-start | bytes 2752520 | tf_op jit(solution)/shard_map/ppermute | solution.py:23
  105.7 21.9 %collective-permute-start.11 = (bf16[2,256,896]{2,1,0:T(8,128)(2,1)S(1)}, bf16[2,256,896]{2,1,0:T(8,128)(2,1)S(1)}, u32[]{:S(2)}, u32[]{:S(2)}) collective-permute-start(bf16[2,256,896]{2,1,0:T(8,128)(2,1)S(1)} %get-tuple-element.21), channel_id=1, source_target_pairs={{0,8},{1,17},{2,10},{3,19},{4,12},{5,21},{6,14},{7,23},{8,0},{9,25... | collective-permute-start | bytes 2752520 | tf_op jit(solution)/shard_map/ppermute | solution.py:23
  111.7 18.1 %collective-permute-start.28 = (bf16[1,256,896]{2,1,0:T(8,128)(2,1)S(1)}, bf16[1,256,896]{2,1,0:T(8,128)(2,1)S(1)}, u32[]{:S(2)}, u32[]{:S(2)}) collective-permute-start(bf16[1,256,896]{2,1,0:T(8,128)(2,1)S(1)} %slice.160), channel_id=1, source_target_pairs={{0,16},{1,9},{2,18},{3,11},{4,20},{5,13},{6,22},{7,15},{8,24},{9,1... | collective-permute-start | bytes 1376264 | tf_op jit(solution)/shard_map/ppermute | solution.py:23
  129.9 13.5 %collective-permute-start.29 = (bf16[1,256,896]{2,1,0:T(8,128)(2,1)S(1)}, bf16[1,256,896]{2,1,0:T(8,128)(2,1)S(1)}, u32[]{:S(2)}, u32[]{:S(2)}) collective-permute-start(bf16[1,256,896]{2,1,0:T(8,128)(2,1)S(1)} %fusion.17), channel_id=1, source_target_pairs={{0,16},{1,9},{2,18},{3,11},{4,20},{5,13},{6,22},{7,15},{8,24},{9,1... | collective-permute-start | bytes 1376264 | tf_op jit(solution)/shard_map/ppermute | solution.py:23
  136.4 16.9 %collective-permute-start.13 = (bf16[1,256,896]{2,1,0:T(8,128)(2,1)S(1)}, bf16[1,256,896]{2,1,0:T(8,128)(2,1)S(1)}, u32[]{:S(2)}, u32[]{:S(2)}) collective-permute-start(bf16[1,256,896]{2,1,0:T(8,128)(2,1)S(1)} %fusion.18), channel_id=1, source_target_pairs={{0,16},{1,9},{2,18},{3,11},{4,20},{5,13},{6,22},{7,15},{8,24},{9,1... | collective-permute-start | bytes 1376264 | tf_op jit(solution)/shard_map/ppermute | solution.py:23
  143.6 13.5 %collective-permute-start.30 = (bf16[2,256,896]{2,1,0:T(8,128)(2,1)S(1)}, bf16[2,256,896]{2,1,0:T(8,128)(2,1)S(1)}, u32[]{:S(2)}, u32[]{:S(2)}) collective-permute-start(bf16[2,256,896]{2,1,0:T(8,128)(2,1)S(1)} %pad_maximum_fusion.2.first_ref), channel_id=1, source_target_pairs={{0,8},{1,17},{2,10},{3,19},{4,12},{5,21},{6,14},{7,23},{8,0},{9,25... | collective-permute-start | bytes 2752520 | tf_op jit(solution)/shard_map/ppermute | solution.py:23
  153.4 13.5 %collective-permute-start.14 = (bf16[2,256,896]{2,1,0:T(8,128)(2,1)S(1)}, bf16[2,256,896]{2,1,0:T(8,128)(2,1)S(1)}, u32[]{:S(2)}, u32[]{:S(2)}) collective-permute-start(bf16[2,256,896]{2,1,0:T(8,128)(2,1)S(1)} %pad_maximum_fusion.1.first_ref), channel_id=1, source_target_pairs={{0,8},{1,17},{2,10},{3,19},{4,12},{5,21},{6,14},{7,23},{8,0},{9,25... | collective-permute-start | bytes 2752520 | tf_op jit(solution)/shard_map/ppermute | solution.py:23
  163.7 9.9 %collective-permute-start.31 = (f32[4,256,256]{2,1,0:T(8,128)S(1)}, f32[4,256,256]{2,1,0:T(8,128)S(1)}, u32[]{:S(2)}, u32[]{:S(2)}) collective-permute-start(f32[4,256,256]{2,1,0:T(8,128)S(1)} %get-tuple-element.29), channel_id=1, source_target_pairs={{0,1},{1,0},{2,3},{3,2},{4,5},{5,4},{6,7},{7,6},{8,9},{9,8},{10,11... | collective-permute-start | bytes 3145736 | tf_op jit(solution)/shard_map/ppermute | solution.py:23
  173.7 13.6 %collective-permute-start.32 = (bf16[2,256,256]{2,1,0:T(8,128)(2,1)S(1)}, bf16[2,256,256]{2,1,0:T(8,128)(2,1)S(1)}, u32[]{:S(2)}, u32[]{:S(2)}) collective-permute-start(bf16[2,256,256]{2,1,0:T(8,128)(2,1)S(1)} %slice.162), channel_id=1, source_target_pairs={{0,2},{1,5},{2,0},{3,7},{4,6},{5,1},{6,4},{7,3},{8,10},{9,13},{10,... | collective-permute-start | bytes 786440 | tf_op jit(solution)/shard_map/ppermute | solution.py:23
  180.0 10.1 %collective-permute-start.16 = (bf16[2,256,256]{2,1,0:T(8,128)(2,1)S(1)}, bf16[2,256,256]{2,1,0:T(8,128)(2,1)S(1)}, u32[]{:S(2)}, u32[]{:S(2)}) collective-permute-start(bf16[2,256,256]{2,1,0:T(8,128)(2,1)S(1)} %slice.164), channel_id=1, source_target_pairs={{0,2},{1,5},{2,0},{3,7},{4,6},{5,1},{6,4},{7,3},{8,10},{9,13},{10,... | collective-permute-start | bytes 786440 | tf_op jit(solution)/shard_map/ppermute | solution.py:23
  196.4 12.7 %collective-permute-start.18 = (bf16[1,256,256]{2,1,0:T(8,128)(2,1)S(1)}, bf16[1,256,256]{2,1,0:T(8,128)(2,1)S(1)}, u32[]{:S(2)}, u32[]{:S(2)}) collective-permute-start(bf16[1,256,256]{2,1,0:T(8,128)(2,1)S(1)} %fusion.29), channel_id=1, source_target_pairs={{0,4},{1,3},{2,6},{3,1},{4,0},{5,7},{6,2},{7,5},{8,12},{9,11},{10,... | collective-permute-start | bytes 393224 | tf_op jit(solution)/shard_map/ppermute | solution.py:23
  209.1 9.8 %collective-permute-start.19 = (bf16[2,256,256]{2,1,0:T(8,128)(2,1)S(1)}, bf16[2,256,256]{2,1,0:T(8,128)(2,1)S(1)}, u32[]{:S(2)}, u32[]{:S(2)}) collective-permute-start(bf16[2,256,256]{2,1,0:T(8,128)(2,1)S(1)} %pad_maximum_fusion.10), channel_id=1, source_target_pairs={{0,2},{1,5},{2,0},{3,7},{4,6},{5,1},{6,4},{7,3},{8,10},{9,13},{10,... | collective-permute-start | bytes 786440 | tf_op jit(solution)/shard_map/ppermute | solution.py:23
  227.4 9.2 %collective-permute-start.37 = (f32[256,512]{1,0:T(8,128)S(1)}, f32[256,512]{1,0:T(8,128)S(1)}, u32[]{:S(2)}, u32[]{:S(2)}) collective-permute-start(f32[256,512]{1,0:T(8,128)S(1)} %convolution_add_fusion.2), channel_id=1, source_target_pairs={{0,8},{1,17},{2,10},{3,19},{4,12},{5,21},{6,14},{7,23},{8,0},{9,25... | collective-permute-start | bytes 1572872 | tf_op jit(solution)/shard_map/ppermute | solution.py:23
  236.7 9.7 %collective-permute-start.38 = (f32[256,512]{1,0:T(8,128)S(1)}, f32[256,512]{1,0:T(8,128)S(1)}, u32[]{:S(2)}, u32[]{:S(2)}) collective-permute-start(f32[256,512]{1,0:T(8,128)S(1)} %add.139), channel_id=1, source_target_pairs={{0,16},{1,9},{2,18},{3,11},{4,20},{5,13},{6,22},{7,15},{8,24},{9,1... | collective-permute-start | bytes 1572872 | tf_op jit(solution)/shard_map/ppermute | solution.py:23
  287.2 23.5 %collective-permute-start.40 = (bf16[2,128,3584]{2,1,0:T(8,128)(2,1)}, bf16[2,128,3584]{2,1,0:T(8,128)(2,1)}, u32[]{:S(2)}, u32[]{:S(2)}) collective-permute-start(bf16[2,128,3584]{2,1,0:T(8,128)(2,1)} %bitcast.46), channel_id=1, source_target_pairs={{0,8},{1,17},{2,10},{3,19},{4,12},{5,21},{6,14},{7,23},{8,0},{9,25... | collective-permute-start | bytes 5505032 | tf_op jit(solution)/shard_map/ppermute | solution.py:23
  316.1 13.7 %collective-permute-start.41 = (bf16[1,128,3584]{2,1,0:T(8,128)(2,1)}, bf16[1,128,3584]{2,1,0:T(8,128)(2,1)}, u32[]{:S(2)}, u32[]{:S(2)}) collective-permute-start(bf16[1,128,3584]{2,1,0:T(8,128)(2,1)} %slice.159), channel_id=1, source_target_pairs={{0,16},{1,9},{2,18},{3,11},{4,20},{5,13},{6,22},{7,15},{8,24},{9,1... | collective-permute-start | bytes 2752520 | tf_op jit(solution)/shard_map/ppermute | solution.py:23
  (33 other events, 236.9 us)

commit v3 on v2

--- a/solution.py
+++ b/solution.py
@@ -105,7 +105,7 @@
     return value
 
 
-def token_gram_kernel(valid_ref, grads_ref, gram_ref, scale_ref):
+def token_gram_kernel(valid_ref, grads_ref, after_ref, weight_ref, gram_ref, scale_ref):
     seq = pl.program_id(0)
     length = grads_ref.shape[1]
     tokens = lax.broadcasted_iota(jnp.int32, (length, 1), 0)
@@ -127,7 +127,7 @@
     scale_ref[0] = jnp.broadcast_to(scale, (length, 128))
 
 
-def row_mass_kernel(acts_ref, gram_ref, scale_ref, mass_ref):
+def row_mass_kernel(acts_ref, gram_ref, scale_ref, weight_ref, mass_ref):
     length = acts_ref.shape[1]
     total = jnp.zeros((1, acts_ref.shape[2]), F32)
     for seq in range(acts_ref.shape[0]):
@@ -138,7 +138,7 @@
     mass_ref[...] = total
 
 
-def local_mass(activations, out_grads, valid_len):
+def local_mass(activations, out_grads, valid_len, after, weight):
     seqs, length, width = activations.shape
     cols = out_grads.shape[2]
     whole = lambda seq, valid: (seq, 0, 0)
@@ -151,7 +151,11 @@
         grid_spec=pltpu.PrefetchScalarGridSpec(
             num_scalar_prefetch=1,
             grid=(seqs,),
-            in_specs=[pl.BlockSpec((1, length, cols), whole)],
+            in_specs=[
+                pl.BlockSpec((1, length, cols), whole),
+                pl.BlockSpec(memory_space=pl.ANY),
+                pl.BlockSpec(memory_space=pltpu.VMEM),
+            ],
             out_specs=(
                 pl.BlockSpec((1, 2 * length, length), whole),
                 pl.BlockSpec((1, length, 128), whole),
@@ -164,7 +168,7 @@
             transcendentals=0,
         ),
         name="token_gram",
-    )(valid_len, out_grads)
+    )(valid_len, out_grads, after, weight)
     tile = math.gcd(width, 1024)
     fixed = lambda i: (0, 0, 0)
     mass = pl.pallas_call(
@@ -175,6 +179,7 @@
             pl.BlockSpec((seqs, length, tile), lambda i: (0, 0, i)),
             pl.BlockSpec((seqs, 2 * length, length), fixed),
             pl.BlockSpec((seqs, length, 128), fixed),
+            pl.BlockSpec(memory_space=pltpu.VMEM),
         ],
         out_specs=pl.BlockSpec((1, tile), lambda i: (0, i)),
         compiler_params=pltpu.CompilerParams(vmem_limit_bytes=LIMIT),
@@ -184,7 +189,7 @@
             transcendentals=0,
         ),
         name="row_mass",
-    )(activations, gram, scale)
+    )(activations, gram, scale, weight)
     return mass.reshape(width)
 
 
@@ -206,12 +211,14 @@
             pivot = jnp.broadcast_to(column[k][k : k + 1], (8, size))
             row = jnp.broadcast_to(now[k : k + 1], (8, size))
             out = jnp.where(here, row * lax.rsqrt(pivot), out)
-            inverse = 1.0 / pivot
+            inverse = pl.reciprocal(pivot, approx=True)
+            inverse = inverse * (2.0 - pivot * inverse)
             row = row * inverse
             now = jnp.where(here, row, now - column[k] * row)
             for j in range(k + 1, 8):
-                part = jnp.broadcast_to(column[j][k : k + 1], (8, size)) * inverse
-                column[j] = jnp.where(here, part, column[j] - column[k] * part)
+                part = jnp.broadcast_to(column[j][k : k + 1], (8, size))
+                product = column[k] * part
+                column[j] = jnp.where(here, part * inverse, column[j] - product * inverse)
         done.append(jnp.where(lane < base + 8, out, 0.0))
         rows = [jnp.broadcast_to(now[s : s + 1], (8, size)) for s in range(8)]
         for i in range(g + 1, size // 8):
@@ -276,7 +283,7 @@
     )(gram)
 
 
-LIMIT = 24 << 20
+LIMIT = 16 << 20
 
 
 def dot(left, right, dims=((1,), (0,))):
@@ -296,28 +303,20 @@
         target[i % half] = value.T if turned else value
 
 
-def add_up(step, term, sum_ref):
-    @pl.when(step == 0)
-    def _():
-        sum_ref[...] = term
-
-    @pl.when(step > 0)
-    def _():
-        sum_ref[...] += term
-
-
 def two_halves(size, shape, send_type):
     dims = (size // 2,) + shape
     return (jax.ShapeDtypeStruct(dims, send_type), jax.ShapeDtypeStruct(dims, F32))
 
 
-def product_call(kernel, name, out_shape, scratch, weight, width, indices, arrays):
+def product_call(kernel, name, out_shape, scratch, weight, width, indices, arrays, after=()):
     height, depth = weight.shape
     smem, vmem = (pl.BlockSpec(memory_space=space) for space in (pltpu.SMEM, pltpu.VMEM))
     return pl.pallas_call(
-        kernel,
+        lambda *refs: kernel(*refs[len(after) :]),
         out_shape=out_shape,
-        in_specs=[smem] * len(indices) + [vmem] * (1 + len(arrays)),
+        in_specs=[pl.BlockSpec(memory_space=pl.ANY)] * len(after)
+        + [smem] * len(indices)
+        + [vmem] * (1 + len(arrays)),
         out_specs=(vmem, vmem),
         scratch_shapes=[scratch],
         compiler_params=pltpu.CompilerParams(vmem_limit_bytes=LIMIT),
@@ -327,23 +326,27 @@
             transcendentals=0,
         ),
         name=name,
-    )(*indices, weight, *arrays)
+    )(*after, *indices, weight, *arrays)
 
 
 def rows_plain_kernel(part, width, turned, order_ref, weight_ref, right_ref, send_ref, keep_ref, sum_ref):
     depth = weight_ref.shape[1]
     chunk = 512 if depth % 512 == 0 else depth
 
-    @pl.loop(0, depth // chunk)
+    def term(start):
+        here = pl.ds(start, chunk)
+        return dot(weight_ref[:, here], right_ref[here, part * width : (part + 1) * width])
+
+    sum_ref[...] = term(0)
+
+    @pl.loop(1, depth // chunk)
     def _(i):
-        here = pl.ds(pl.multiple_of(i * chunk, chunk), chunk)
-        right = right_ref[here, part * width : (part + 1) * width]
-        add_up(i, dot(weight_ref[:, here], right), sum_ref)
+        sum_ref[...] += term(pl.multiple_of(i * chunk, chunk))
 
     gather_rows(order_ref, sum_ref, send_ref, keep_ref, turned)
 
 
-def rows_times(weight, right, part, width, rows, turned):
+def rows_times(weight, right, part, width, rows, turned, after=()):
     height = weight.shape[0]
     block = height // rows.size
     shapes = two_halves(rows.size, (width, block) if turned else (block, width), F32)
@@ -356,19 +359,24 @@
         width,
         (rows.sending_first(),),
         (right,),
+        after,
     )
 
 
 def rows_joined_kernel(rows_ref, cols_ref, weight_ref, first_ref, second_ref, send_ref, keep_ref, sum_ref):
     half, _, own = first_ref.shape
-    for part, right_ref in enumerate((first_ref, second_ref)):
-
-        @pl.loop(0, half)
+
+    def term(part, i):
+        block = cols_ref[i + half * (1 - part)]
+        here = pl.ds(pl.multiple_of(block * own, 128), own)
+        return dot(weight_ref[:, here], (first_ref, second_ref)[part][i], NT)
+
+    sum_ref[...] = term(0, 0)
+    for part in range(2):
+
+        @pl.loop(1 - part, half)
         def _(i):
-            block = cols_ref[i + half * (1 - part)]
-            here = pl.ds(pl.multiple_of(block * own, 128), own)
-            term = dot(weight_ref[:, here], right_ref[i], NT)
-            add_up(i + half * part, term, sum_ref)
+            sum_ref[...] += term(part, i)
 
     gather_rows(rows_ref, sum_ref, send_ref, keep_ref, False)
 
@@ -431,6 +439,36 @@
     )
 
 
+def rank_kernel(weight_ref, basis_ref, out_ref):
+    depth = weight_ref.shape[1]
+    tile = math.gcd(depth, 512)
+
+    @pl.loop(0, depth // tile)
+    def _(i):
+        here = pl.ds(pl.multiple_of(i * tile, tile), tile)
+        out_ref[:, here] = dot(basis_ref[...], weight_ref[:, here]).astype(BF16)
+
+
+def rank_times(weight, basis):
+    height, depth = weight.shape
+    if depth % 512:
+        return dot(basis, weight).astype(BF16)
+    vmem = pl.BlockSpec(memory_space=pltpu.VMEM)
+    return pl.pallas_call(
+        rank_kernel,
+        out_shape=jax.ShapeDtypeStruct((basis.shape[0], depth), BF16),
+        in_specs=[vmem, vmem],
+        out_specs=vmem,
+        compiler_params=pltpu.CompilerParams(vmem_limit_bytes=LIMIT),
+        cost_estimate=pl.CostEstimate(
+            flops=2 * height * depth * basis.shape[0],
+            bytes_accessed=2 * (height + basis.shape[0]) * depth,
+            transcendentals=0,
+        ),
+        name="rank_times",
+    )(weight, basis)
+
+
 def settle_kernel(order_ref, *refs):
     out_ref = refs[-1]
     count, block, half = refs[0].shape
@@ -474,21 +512,23 @@
     own_rows = rows_here // col_count
     over_col, over_row = Halving("col"), Halving("row")
 
-    mass = local_mass(activations, out_grads, valid_len)
+    raw = [rows_times(weight, sketch, 0, half, over_col, True)]
+    mass = local_mass(activations, out_grads, valid_len, raw[0][1], weight)
+    raw.append(rows_times(weight, sketch, 1, half, over_col, True, (mass,)))
     fisher = sum_everywhere(mass.reshape(-1, 128)).reshape(width)
     mean = jnp.sum(fisher) / width + 1e-06
     square_scale = lax.dynamic_slice_in_dim(fisher, row * rows_here, rows_here) / mean
     own_square = lax.dynamic_slice_in_dim(square_scale, col * own_rows, own_rows)
 
-    def second_of(part):
-        raw = over_col.scatter_sum(*rows_times(weight, sketch, part, half, over_col, True))
+    def second_of(parts):
+        raw = over_col.scatter_sum(*parts)
         first = over_col.gather(raw.astype(BF16))
         parts = cols_times_joined(weight, square_scale, first, over_col, over_row)
         projected = over_row.gather(over_row.scatter_sum(*parts).astype(BF16))
         parts = rows_times_joined(weight, projected, over_col, over_row)
         return over_col.gather(over_col.scatter_sum(*parts).astype(BF16))
 
-    second = settle(second_of(0), second_of(1), over_col)
+    second = settle(second_of(raw[0]), second_of(raw[1]), over_col)
 
     even = (col & 1) == 0
     mine = lax.dynamic_slice_in_dim(second, (col & 1) * half, half, 1).astype(F32)
@@ -505,9 +545,8 @@
     def coeffs_of(places):
         part = [lax.dynamic_index_in_dim(blocks, order[i], 0, keepdims=False) for i in places]
         high, low = split(jnp.concatenate(part))
-        basis = dot(second, high, NT) + dot(second, low, NT)
-        parts = dot((square_scale[:, None] * basis).astype(BF16), weight, rows_of)
-        return parts.astype(BF16).reshape(len(part), -1, cols_here)
+        basis = (dot(high, second, NT) + dot(low, second, NT)) * square_scale
+        return rank_times(weight, basis.astype(BF16)).reshape(len(part), -1, cols_here)
 
     coeffs = over_row.scatter_sum(
         coeffs_of(range(row_count // 2)), coeffs_of(range(row_count // 2, row_count))

time: 333 us -> 334 us (level)
  matrix products: 33.6 us -> 7.31 us
  waiting for transfers between devices: 127 us -> 142 us
  Pallas kernels: 73.2 us -> 83 us
  starting transfers between devices: 67.2 us -> 71.2 us
    dot_general x8, matrix products: 33.6 us -> 7.31 us  [dot(): lax.dot_general(left, right, (dims, ((), ())), preferred_element_type=F32)]
    ppermute x42, waiting for transfers between devices: 127 us -> 142 us  [swap(): return lax.ppermute(block, AXES, pairs)]
    pallas_call x6 -> x8, Pallas kernels: 39.9 us -> 45.9 us  [the longest x6 36 us: product_call(): pl.pallas_call(lambda *refs: kernel(*refs[len(after):]), out_shape=out_sh...]
    ppermute x42, starting transfers between devices: 67.2 us -> 71.2 us  [swap(): return lax.ppermute(block, AXES, pairs)]
    pallas_call x1, Pallas kernels: 22.7 us -> 26.4 us  [inverse_factor(): pl.pallas_call(inverse_factor_kernel, out_shape=jax.ShapeDtypeStruct((siz...]
    unnamed x30 -> x46, local copies, waits for them, and re-layouts: 18.7 us -> 18.7 us
  transfers between devices with their start and end apart: 42 -> 42, of which waited for: 29 -> 31; matrix products, arithmetic and copies ran while one was open for 6% -> 2% of each run, Pallas kernels for 13% -> 13%
where the time goes in v3:
time: 334 us; the launch traced here: 333 us
  waiting for transfers between devices  142 us (43%)
  Pallas kernels  83 us (25%)
  starting transfers between devices  71.2 us (21%)
  local copies, waits for them, and re-layouts  20.2 us (6%)
  other arithmetic  7.32 us (2%)
  matrix products  7.31 us (2%)
    ppermute x42, waiting for transfers between devices, swap(): return lax.ppermute(block, AXES, pairs)  142 us
    ppermute x42, starting transfers between devices, swap(): return lax.ppermute(block, AXES, pairs)  71.2 us
    pallas_call x6, Pallas kernels, product_call(): pl.pallas_call(lambda *refs: kernel(*refs[len(after):]), out_shape=out_sh...  36 us
    pallas_call x1, Pallas kernels, inverse_factor(): pl.pallas_call(inverse_factor_kernel, out_shape=jax.ShapeDtypeStruct((siz...  26.4 us
    unnamed x46, local copies, waits for them, and re-layouts  18.7 us
    pallas_call x2, Pallas kernels, rank_times(): pl.pallas_call(rank_kernel, out_shape=jax.ShapeDtypeStruct((basis.shape[0...  9.91 us
    pallas_call x1, Pallas kernels, local_mass(): pl.pallas_call(row_mass_kernel, out_shape=jax.ShapeDtypeStruct((1, width)...  7.37 us
    dot_general x8, matrix products, dot(): lax.dot_general(left, right, (dims, ((), ())), preferred_element_type=F32)  7.31 us
  transfers between devices with their start and end apart: 42, of which 31 were waited for; matrix products, arithmetic and copies ran while one was open for 2% of the time, Pallas kernels for 13%

profile of v3, /device:TPU:0, one launch (start us, length us, event | category | flops | bytes accessed | tf_op | source)
XLA Modules:
  0.0 333.2 jit_solution(10061014375709123480)
XLA Ops:
  8.0 6.3 %rows_times.2 = (f32[4,256,256]{2,1,0:T(8,128)S(1)}, f32[4,256,256]{2,1,0:T(8,128)S(1)}) custom-call(s32[8]{0:T(128)S(1)} %stack.36.refs_0_.refs_1_.order_ref, bf16[2048,3584]{1,0:T(8,128)(2,1)S(1)} %copy-done, bf16[3584,512]{1,0:T(8,128)(2,1)S(1)} %copy-done.3), custom_call_target="tpu_custom_call" | custom-call | flops 3758096384 | bytes 16515072 | tf_op jit(solution)/shard_map/rows_times/pallas_call | solution.py:314
  18.3 7.4 %row_mass.1 = f32[1,8192]{1,0:T(1,128)S(1)} custom-call(bf16[2,256,8192]{2,1,0:T(8,128)(2,1)S(1)} %bitcast.43, bf16[2,512,256]{2,1,0:T(8,128)(2,1)S(1)} %get-tuple-element.17.gram_ref, f32[2,256,128]{2,1,0:T(8,128)S(1)} %get-tuple-element.18.scale_ref, bf16[2048,3584]{1,0:T(8,128)(2,1)S(1)} %copy-done.1), custom_call_target="tpu_custom_call" | custom-call | flops 4294967296 | bytes 8388608 | tf_op jit(solution)/shard_map/row_mass/pallas_call | solution.py:174
  25.7 6.1 %rows_times.3 = (f32[4,256,256]{2,1,0:T(8,128)S(1)}, f32[4,256,256]{2,1,0:T(8,128)S(1)}) custom-call(f32[8192]{0:T(1024)S(1)} %bitcast.46, s32[8]{0:T(128)S(1)} %stack.36.refs_0_.refs_1_.order_ref, bf16[2048,3584]{1,0:T(8,128)(2,1)S(1)} %copy-done.1, bf16[3584,512]{1,0:T(8,128)(2,1)S(1)} %copy-done.4), custom_call_target="tpu_custom_call" | custom-call | flops 3758096384 | bytes 16515072 | tf_op jit(solution)/shard_map/rows_times/pallas_call | solution.py:314
  35.3 6.8 %collective-permute-done.6 = bf16[2,256,256]{2,1,0:T(8,128)(2,1)S(1)} collective-permute-done((bf16[2,256,256]{2,1,0:T(8,128)(2,1)S(1)}, bf16[2,256,256]{2,1,0:T(8,128)(2,1)S(1)}, u32[]{:S(2)}, u32[]{:S(2)}) %collective-permute-start.6) | collective-permute-done | bytes 262176 | tf_op jit(solution)/shard_map/ppermute | solution.py:23
  50.7 6.1 %collective-permute-done.22 = bf16[2,256,256]{2,1,0:T(8,128)(2,1)S(1)} collective-permute-done((bf16[2,256,256]{2,1,0:T(8,128)(2,1)S(1)}, bf16[2,256,256]{2,1,0:T(8,128)(2,1)S(1)}, u32[]{:S(2)}, u32[]{:S(2)}) %collective-permute-start.22) | collective-permute-done | bytes 262176 | tf_op jit(solution)/shard_map/ppermute | solution.py:23
  57.6 7.6 %collective-permute-start.9 = (bf16[2,256,256]{2,1,0:T(8,128)(2,1)S(1)}, bf16[2,256,256]{2,1,0:T(8,128)(2,1)S(1)}, u32[]{:S(2)}, u32[]{:S(2)}) collective-permute-start(bf16[2,256,256]{2,1,0:T(8,128)(2,1)S(1)} %pad_maximum_fusion.9), channel_id=1, source_target_pairs={{0,2},{1,5},{2,0},{3,7},{4,6},{5,1},{6,4},{7,3},{8,10},{9,13},{10,... | collective-permute-start | bytes 786440 | tf_op jit(solution)/shard_map/ppermute | solution.py:23
  95.5 5.8 %cols_times_joined.2 = (bf16[2,256,896]{2,1,0:T(8,128)(2,1)S(1)}, f32[2,256,896]{2,1,0:T(8,128)S(1)}) custom-call(s32[4]{0:T(128)S(1)} %pad_add_fusion.refs_0_.refs_1_, s32[8]{0:T(128)S(1)} %stack.36.refs_0_.refs_1_.order_ref, bf16[2048,3584]{1,0:T(8,128)(2,1)S(1)} %copy-done.2, f32[1,2048]{1,0:T(1,128)S(1)} %bitcast.49, ...), custom_call_target="tpu_custom_call" | custom-call | flops 3758096384 | bytes 16515072 | tf_op jit(solution)/shard_map/cols_times_joined/pallas_call | solution.py:314
  102.9 6.0 %cols_times_joined.3 = (bf16[2,256,896]{2,1,0:T(8,128)(2,1)S(1)}, f32[2,256,896]{2,1,0:T(8,128)S(1)}) custom-call(s32[4]{0:T(128)S(1)} %pad_add_fusion.refs_0_.refs_1_, s32[8]{0:T(128)S(1)} %stack.36.refs_0_.refs_1_.order_ref, bf16[2048,3584]{1,0:T(8,128)(2,1)S(1)} %copy-done.2, f32[1,2048]{1,0:T(1,128)S(1)} %bitcast.50, ...), custom_call_target="tpu_custom_call" | custom-call | flops 3758096384 | bytes 16515072 | tf_op jit(solution)/shard_map/cols_times_joined/pallas_call | solution.py:314
  109.4 5.3 %collective-permute-done.11 = bf16[2,256,896]{2,1,0:T(8,128)(2,1)S(1)} collective-permute-done((bf16[2,256,896]{2,1,0:T(8,128)(2,1)S(1)}, bf16[2,256,896]{2,1,0:T(8,128)(2,1)S(1)}, u32[]{:S(2)}, u32[]{:S(2)}) %collective-permute-start.11) | collective-permute-done | bytes 917536 | tf_op jit(solution)/shard_map/ppermute | solution.py:23
  116.6 12.9 %collective-permute-done.27 = bf16[2,256,896]{2,1,0:T(8,128)(2,1)S(1)} collective-permute-done((bf16[2,256,896]{2,1,0:T(8,128)(2,1)S(1)}, bf16[2,256,896]{2,1,0:T(8,128)(2,1)S(1)}, u32[]{:S(2)}, u32[]{:S(2)}) %collective-permute-start.27) | collective-permute-done | bytes 917536 | tf_op jit(solution)/shard_map/ppermute | solution.py:23
  132.0 6.3 %collective-permute-done.28 = bf16[1,256,896]{2,1,0:T(8,128)(2,1)S(1)} collective-permute-done((bf16[1,256,896]{2,1,0:T(8,128)(2,1)S(1)}, bf16[1,256,896]{2,1,0:T(8,128)(2,1)S(1)}, u32[]{:S(2)}, u32[]{:S(2)}) %collective-permute-start.28) | collective-permute-done | bytes 458784 | tf_op jit(solution)/shard_map/ppermute | solution.py:23
  144.9 7.1 %collective-permute-done.29 = bf16[1,256,896]{2,1,0:T(8,128)(2,1)S(1)} collective-permute-done((bf16[1,256,896]{2,1,0:T(8,128)(2,1)S(1)}, bf16[1,256,896]{2,1,0:T(8,128)(2,1)S(1)}, u32[]{:S(2)}, u32[]{:S(2)}) %collective-permute-start.29) | collective-permute-done | bytes 458784 | tf_op jit(solution)/shard_map/ppermute | solution.py:23
  156.8 5.7 %rows_times_joined.2 = (f32[4,256,256]{2,1,0:T(8,128)S(1)}, f32[4,256,256]{2,1,0:T(8,128)S(1)}) custom-call(s32[8]{0:T(128)S(1)} %stack.36.refs_0_.refs_1_.order_ref, s32[4]{0:T(128)S(1)} %pad_add_fusion.refs_0_.refs_1_, bf16[2048,3584]{1,0:T(8,128)(2,1)S(1)} %bitcast.38, bf16[2,256,896]{2,1,0:T(8,128)(2,1)S(1)} %pad_maximum_fusion.1.refs_3_, ...), custom_call_target="tpu_custom_call" | custom-call | flops 3758096384 | bytes 16515072 | tf_op jit(solution)/shard_map/rows_times_joined/pallas_call | solution.py:314
  166.6 6.0 %rows_times_joined.3 = (f32[4,256,256]{2,1,0:T(8,128)S(1)}, f32[4,256,256]{2,1,0:T(8,128)S(1)}) custom-call(s32[8]{0:T(128)S(1)} %stack.36.refs_0_.refs_1_.order_ref, s32[4]{0:T(128)S(1)} %pad_add_fusion.refs_0_.refs_1_, bf16[2048,3584]{1,0:T(8,128)(2,1)S(1)} %bitcast.38, bf16[2,256,896]{2,1,0:T(8,128)(2,1)S(1)} %pad_maximum_fusion.2.refs_3_, ...), custom_call_target="tpu_custom_call" | custom-call | flops 3758096384 | bytes 16515072 | tf_op jit(solution)/shard_map/rows_times_joined/pallas_call | solution.py:314
  173.8 8.0 %collective-permute-start.16 = (bf16[2,256,256]{2,1,0:T(8,128)(2,1)S(1)}, bf16[2,256,256]{2,1,0:T(8,128)(2,1)S(1)}, u32[]{:S(2)}, u32[]{:S(2)}) collective-permute-start(bf16[2,256,256]{2,1,0:T(8,128)(2,1)S(1)} %slice.164), channel_id=1, source_target_pairs={{0,2},{1,5},{2,0},{3,7},{4,6},{5,1},{6,4},{7,3},{8,10},{9,13},{10,... | collective-permute-start | bytes 786440 | tf_op jit(solution)/shard_map/ppermute | solution.py:23
  184.4 5.9 %collective-permute-done.16 = bf16[2,256,256]{2,1,0:T(8,128)(2,1)S(1)} collective-permute-done((bf16[2,256,256]{2,1,0:T(8,128)(2,1)S(1)}, bf16[2,256,256]{2,1,0:T(8,128)(2,1)S(1)}, u32[]{:S(2)}, u32[]{:S(2)}) %collective-permute-start.16) | collective-permute-done | bytes 262176 | tf_op jit(solution)/shard_map/ppermute | solution.py:23
  191.4 5.4 %collective-permute-done.32 = bf16[2,256,256]{2,1,0:T(8,128)(2,1)S(1)} collective-permute-done((bf16[2,256,256]{2,1,0:T(8,128)(2,1)S(1)}, bf16[2,256,256]{2,1,0:T(8,128)(2,1)S(1)}, u32[]{:S(2)}, u32[]{:S(2)}) %collective-permute-start.32) | collective-permute-done | bytes 262176 | tf_op jit(solution)/shard_map/ppermute | solution.py:23
  207.0 6.6 %collective-permute-start.19 = (bf16[2,256,256]{2,1,0:T(8,128)(2,1)S(1)}, bf16[2,256,256]{2,1,0:T(8,128)(2,1)S(1)}, u32[]{:S(2)}, u32[]{:S(2)}) collective-permute-start(bf16[2,256,256]{2,1,0:T(8,128)(2,1)S(1)} %pad_maximum_fusion.10), channel_id=1, source_target_pairs={{0,2},{1,5},{2,0},{3,7},{4,6},{5,1},{6,4},{7,3},{8,10},{9,13},{10,... | collective-permute-start | bytes 786440 | tf_op jit(solution)/shard_map/ppermute | solution.py:23
  217.1 6.3 %collective-permute-done.19 = bf16[2,256,256]{2,1,0:T(8,128)(2,1)S(1)} collective-permute-done((bf16[2,256,256]{2,1,0:T(8,128)(2,1)S(1)}, bf16[2,256,256]{2,1,0:T(8,128)(2,1)S(1)}, u32[]{:S(2)}, u32[]{:S(2)}) %collective-permute-start.19) | collective-permute-done | bytes 262176 | tf_op jit(solution)/shard_map/ppermute | solution.py:23
  236.5 7.4 %collective-permute-done.37 = f32[256,512]{1,0:T(8,128)S(1)} collective-permute-done((f32[256,512]{1,0:T(8,128)S(1)}, f32[256,512]{1,0:T(8,128)S(1)}, u32[]{:S(2)}, u32[]{:S(2)}) %collective-permute-start.37) | collective-permute-done | bytes 524320 | tf_op jit(solution)/shard_map/ppermute | solution.py:23
  246.5 7.2 %collective-permute-done.38 = f32[256,512]{1,0:T(8,128)S(1)} collective-permute-done((f32[256,512]{1,0:T(8,128)S(1)}, f32[256,512]{1,0:T(8,128)S(1)}, u32[]{:S(2)}, u32[]{:S(2)}) %collective-permute-start.38) | collective-permute-done | bytes 524320 | tf_op jit(solution)/shard_map/ppermute | solution.py:23
  257.1 26.4 %inverse_factor.1 = f32[512,512]{1,0:T(8,128)S(1)} custom-call(f32[512,512]{1,0:T(8,128)S(1)} %pad_maximum_fusion.gram_ref), custom_call_target="tpu_custom_call" | custom-call | flops 5368709120 | bytes 2097152 | tf_op jit(solution)/shard_map/inverse_factor/pallas_call | solution.py:272
  298.5 15.0 %collective-permute-done.40 = bf16[2,128,3584]{2,1,0:T(8,128)(2,1)S(1)} collective-permute-done((bf16[2,128,3584]{2,1,0:T(8,128)(2,1)S(1)}, bf16[2,128,3584]{2,1,0:T(8,128)(2,1)S(1)}, u32[]{:S(2)}, u32[]{:S(2)}) %collective-permute-start.40) | collective-permute-done | bytes 1835040 | tf_op jit(solution)/shard_map/ppermute | solution.py:23
  320.4 10.1 %collective-permute-done.41 = bf16[1,128,3584]{2,1,0:T(8,128)(2,1)} collective-permute-done((bf16[1,128,3584]{2,1,0:T(8,128)(2,1)}, bf16[1,128,3584]{2,1,0:T(8,128)(2,1)}, u32[]{:S(2)}, u32[]{:S(2)}) %collective-permute-start.41) | collective-permute-done | bytes 917536 | tf_op jit(solution)/shard_map/ppermute | solution.py:23
  (182 shorter events, 137.5 us)
Async XLA Ops:
  14.3 17.7 %collective-permute-start.5 = (f32[4,256,256]{2,1,0:T(8,128)S(1)}, f32[4,256,256]{2,1,0:T(8,128)S(1)}, u32[]{:S(2)}, u32[]{:S(2)}) collective-permute-start(f32[4,256,256]{2,1,0:T(8,128)S(1)} %get-tuple-element.19), channel_id=1, source_target_pairs={{0,1},{1,0},{2,3},{3,2},{4,5},{5,4},{6,7},{7,6},{8,9},{9,8},{10,11... | collective-permute-start | bytes 3145736 | tf_op jit(solution)/shard_map/ppermute | solution.py:23
  31.8 12.8 %collective-permute-start.21 = (f32[4,256,256]{2,1,0:T(8,128)S(1)}, f32[4,256,256]{2,1,0:T(8,128)S(1)}, u32[]{:S(2)}, u32[]{:S(2)}) collective-permute-start(f32[4,256,256]{2,1,0:T(8,128)S(1)} %get-tuple-element.25), channel_id=1, source_target_pairs={{0,1},{1,0},{2,3},{3,2},{4,5},{5,4},{6,7},{7,6},{8,9},{9,8},{10,11... | collective-permute-start | bytes 3145736 | tf_op jit(solution)/shard_map/ppermute | solution.py:23
  32.2 9.9 %collective-permute-start.6 = (bf16[2,256,256]{2,1,0:T(8,128)(2,1)S(1)}, bf16[2,256,256]{2,1,0:T(8,128)(2,1)S(1)}, u32[]{:S(2)}, u32[]{:S(2)}) collective-permute-start(bf16[2,256,256]{2,1,0:T(8,128)(2,1)S(1)} %slice.165), channel_id=1, source_target_pairs={{0,2},{1,5},{2,0},{3,7},{4,6},{5,1},{6,4},{7,3},{8,10},{9,13},{10,... | collective-permute-start | bytes 786440 | tf_op jit(solution)/shard_map/ppermute | solution.py:23
  44.8 12.0 %collective-permute-start.22 = (bf16[2,256,256]{2,1,0:T(8,128)(2,1)S(1)}, bf16[2,256,256]{2,1,0:T(8,128)(2,1)S(1)}, u32[]{:S(2)}, u32[]{:S(2)}) collective-permute-start(bf16[2,256,256]{2,1,0:T(8,128)(2,1)S(1)} %slice.163), channel_id=1, source_target_pairs={{0,2},{1,5},{2,0},{3,7},{4,6},{5,1},{6,4},{7,3},{8,10},{9,13},{10,... | collective-permute-start | bytes 786440 | tf_op jit(solution)/shard_map/ppermute | solution.py:23
  56.9 11.7 %collective-permute-start.23 = (bf16[1,256,256]{2,1,0:T(8,128)(2,1)S(1)}, bf16[1,256,256]{2,1,0:T(8,128)(2,1)S(1)}, u32[]{:S(2)}, u32[]{:S(2)}) collective-permute-start(bf16[1,256,256]{2,1,0:T(8,128)(2,1)S(1)} %slice.167), channel_id=1, source_target_pairs={{0,4},{1,3},{2,6},{3,1},{4,0},{5,7},{6,2},{7,5},{8,12},{9,11},{10,... | collective-permute-start | bytes 393224 | tf_op jit(solution)/shard_map/ppermute | solution.py:23
  57.6 18.0 %collective-permute-start.9 = (bf16[2,256,256]{2,1,0:T(8,128)(2,1)S(1)}, bf16[2,256,256]{2,1,0:T(8,128)(2,1)S(1)}, u32[]{:S(2)}, u32[]{:S(2)}) collective-permute-start(bf16[2,256,256]{2,1,0:T(8,128)(2,1)S(1)} %pad_maximum_fusion.9), channel_id=1, source_target_pairs={{0,2},{1,5},{2,0},{3,7},{4,6},{5,1},{6,4},{7,3},{8,10},{9,13},{10,... | collective-permute-start | bytes 786440 | tf_op jit(solution)/shard_map/ppermute | solution.py:23
  75.5 11.1 %collective-permute-start.25 = (bf16[2,256,256]{2,1,0:T(8,128)(2,1)S(1)}, bf16[2,256,256]{2,1,0:T(8,128)(2,1)S(1)}, u32[]{:S(2)}, u32[]{:S(2)}) collective-permute-start(bf16[2,256,256]{2,1,0:T(8,128)(2,1)S(1)} %pad_maximum_fusion.11), channel_id=1, source_target_pairs={{0,2},{1,5},{2,0},{3,7},{4,6},{5,1},{6,4},{7,3},{8,10},{9,13},{10,... | collective-permute-start | bytes 786440 | tf_op jit(solution)/shard_map/ppermute | solution.py:23
  75.7 14.6 %collective-permute-start.10 = (bf16[4,256,256]{2,1,0:T(8,128)(2,1)S(1)}, bf16[4,256,256]{2,1,0:T(8,128)(2,1)S(1)}, u32[]{:S(2)}, u32[]{:S(2)}) collective-permute-start(bf16[4,256,256]{2,1,0:T(8,128)(2,1)S(1)} %pad_maximum_fusion.3.refs_4_), channel_id=1, source_target_pairs={{0,1},{1,0},{2,3},{3,2},{4,5},{5,4},{6,7},{7,6},{8,9},{9,8},{10,11... | collective-permute-start | bytes 1572872 | tf_op jit(solution)/shard_map/ppermute | solution.py:23
  86.7 16.2 %collective-permute-start.26 = (bf16[4,256,256]{2,1,0:T(8,128)(2,1)S(1)}, bf16[4,256,256]{2,1,0:T(8,128)(2,1)S(1)}, u32[]{:S(2)}, u32[]{:S(2)}) collective-permute-start(bf16[4,256,256]{2,1,0:T(8,128)(2,1)S(1)} %pad_maximum_fusion.5.refs_4_), channel_id=1, source_target_pairs={{0,1},{1,0},{2,3},{3,2},{4,5},{5,4},{6,7},{7,6},{8,9},{9,8},{10,11... | collective-permute-start | bytes 1572872 | tf_op jit(solution)/shard_map/ppermute | solution.py:23
  101.3 13.5 %collective-permute-start.11 = (bf16[2,256,896]{2,1,0:T(8,128)(2,1)S(1)}, bf16[2,256,896]{2,1,0:T(8,128)(2,1)S(1)}, u32[]{:S(2)}, u32[]{:S(2)}) collective-permute-start(bf16[2,256,896]{2,1,0:T(8,128)(2,1)S(1)} %get-tuple-element.21), channel_id=1, source_target_pairs={{0,8},{1,17},{2,10},{3,19},{4,12},{5,21},{6,14},{7,23},{8,0},{9,25... | collective-permute-start | bytes 2752520 | tf_op jit(solution)/shard_map/ppermute | solution.py:23
  108.9 20.6 %collective-permute-start.27 = (bf16[2,256,896]{2,1,0:T(8,128)(2,1)S(1)}, bf16[2,256,896]{2,1,0:T(8,128)(2,1)S(1)}, u32[]{:S(2)}, u32[]{:S(2)}) collective-permute-start(bf16[2,256,896]{2,1,0:T(8,128)(2,1)S(1)} %get-tuple-element.27), channel_id=1, source_target_pairs={{0,8},{1,17},{2,10},{3,19},{4,12},{5,21},{6,14},{7,23},{8,0},{9,25... | collective-permute-start | bytes 2752520 | tf_op jit(solution)/shard_map/ppermute | solution.py:23
  115.0 16.4 %collective-permute-start.12 = (bf16[1,256,896]{2,1,0:T(8,128)(2,1)S(1)}, bf16[1,256,896]{2,1,0:T(8,128)(2,1)S(1)}, u32[]{:S(2)}, u32[]{:S(2)}) collective-permute-start(bf16[1,256,896]{2,1,0:T(8,128)(2,1)S(1)} %slice.161), channel_id=1, source_target_pairs={{0,16},{1,9},{2,18},{3,11},{4,20},{5,13},{6,22},{7,15},{8,24},{9,1... | collective-permute-start | bytes 1376264 | tf_op jit(solution)/shard_map/ppermute | solution.py:23
  131.4 11.8 %collective-permute-start.13 = (bf16[1,256,896]{2,1,0:T(8,128)(2,1)S(1)}, bf16[1,256,896]{2,1,0:T(8,128)(2,1)S(1)}, u32[]{:S(2)}, u32[]{:S(2)}) collective-permute-start(bf16[1,256,896]{2,1,0:T(8,128)(2,1)S(1)} %fusion.16), channel_id=1, source_target_pairs={{0,16},{1,9},{2,18},{3,11},{4,20},{5,13},{6,22},{7,15},{8,24},{9,1... | collective-permute-start | bytes 1376264 | tf_op jit(solution)/shard_map/ppermute | solution.py:23
  138.4 13.6 %collective-permute-start.29 = (bf16[1,256,896]{2,1,0:T(8,128)(2,1)S(1)}, bf16[1,256,896]{2,1,0:T(8,128)(2,1)S(1)}, u32[]{:S(2)}, u32[]{:S(2)}) collective-permute-start(bf16[1,256,896]{2,1,0:T(8,128)(2,1)S(1)} %fusion.15), channel_id=1, source_target_pairs={{0,16},{1,9},{2,18},{3,11},{4,20},{5,13},{6,22},{7,15},{8,24},{9,1... | collective-permute-start | bytes 1376264 | tf_op jit(solution)/shard_map/ppermute | solution.py:23
  143.3 13.5 %collective-permute-start.14 = (bf16[2,256,896]{2,1,0:T(8,128)(2,1)S(1)}, bf16[2,256,896]{2,1,0:T(8,128)(2,1)S(1)}, u32[]{:S(2)}, u32[]{:S(2)}) collective-permute-start(bf16[2,256,896]{2,1,0:T(8,128)(2,1)S(1)} %pad_maximum_fusion.1.refs_3_), channel_id=1, source_target_pairs={{0,8},{1,17},{2,10},{3,19},{4,12},{5,21},{6,14},{7,23},{8,0},{9,25... | collective-permute-start | bytes 2752520 | tf_op jit(solution)/shard_map/ppermute | solution.py:23
  152.1 14.5 %collective-permute-start.30 = (bf16[2,256,896]{2,1,0:T(8,128)(2,1)S(1)}, bf16[2,256,896]{2,1,0:T(8,128)(2,1)S(1)}, u32[]{:S(2)}, u32[]{:S(2)}) collective-permute-start(bf16[2,256,896]{2,1,0:T(8,128)(2,1)S(1)} %pad_maximum_fusion.2.refs_3_), channel_id=1, source_target_pairs={{0,8},{1,17},{2,10},{3,19},{4,12},{5,21},{6,14},{7,23},{8,0},{9,25... | collective-permute-start | bytes 2752520 | tf_op jit(solution)/shard_map/ppermute | solution.py:23
  162.5 11.1 %collective-permute-start.15 = (f32[4,256,256]{2,1,0:T(8,128)S(1)}, f32[4,256,256]{2,1,0:T(8,128)S(1)}, u32[]{:S(2)}, u32[]{:S(2)}) collective-permute-start(f32[4,256,256]{2,1,0:T(8,128)S(1)} %get-tuple-element.23), channel_id=1, source_target_pairs={{0,1},{1,0},{2,3},{3,2},{4,5},{5,4},{6,7},{7,6},{8,9},{9,8},{10,11... | collective-permute-start | bytes 3145736 | tf_op jit(solution)/shard_map/ppermute | solution.py:23
  173.8 16.5 %collective-permute-start.16 = (bf16[2,256,256]{2,1,0:T(8,128)(2,1)S(1)}, bf16[2,256,256]{2,1,0:T(8,128)(2,1)S(1)}, u32[]{:S(2)}, u32[]{:S(2)}) collective-permute-start(bf16[2,256,256]{2,1,0:T(8,128)(2,1)S(1)} %slice.164), channel_id=1, source_target_pairs={{0,2},{1,5},{2,0},{3,7},{4,6},{5,1},{6,4},{7,3},{8,10},{9,13},{10,... | collective-permute-start | bytes 786440 | tf_op jit(solution)/shard_map/ppermute | solution.py:23
  181.9 14.9 %collective-permute-start.32 = (bf16[2,256,256]{2,1,0:T(8,128)(2,1)S(1)}, bf16[2,256,256]{2,1,0:T(8,128)(2,1)S(1)}, u32[]{:S(2)}, u32[]{:S(2)}) collective-permute-start(bf16[2,256,256]{2,1,0:T(8,128)(2,1)S(1)} %slice.162), channel_id=1, source_target_pairs={{0,2},{1,5},{2,0},{3,7},{4,6},{5,1},{6,4},{7,3},{8,10},{9,13},{10,... | collective-permute-start | bytes 786440 | tf_op jit(solution)/shard_map/ppermute | solution.py:23
  203.8 13.2 %collective-permute-start.34 = (bf16[1,256,256]{2,1,0:T(8,128)(2,1)S(1)}, bf16[1,256,256]{2,1,0:T(8,128)(2,1)S(1)}, u32[]{:S(2)}, u32[]{:S(2)}) collective-permute-start(bf16[1,256,256]{2,1,0:T(8,128)(2,1)S(1)} %fusion.25), channel_id=1, source_target_pairs={{0,4},{1,3},{2,6},{3,1},{4,0},{5,7},{6,2},{7,5},{8,12},{9,11},{10,... | collective-permute-start | bytes 393224 | tf_op jit(solution)/shard_map/ppermute | solution.py:23
  207.0 16.4 %collective-permute-start.19 = (bf16[2,256,256]{2,1,0:T(8,128)(2,1)S(1)}, bf16[2,256,256]{2,1,0:T(8,128)(2,1)S(1)}, u32[]{:S(2)}, u32[]{:S(2)}) collective-permute-start(bf16[2,256,256]{2,1,0:T(8,128)(2,1)S(1)} %pad_maximum_fusion.10), channel_id=1, source_target_pairs={{0,2},{1,5},{2,0},{3,7},{4,6},{5,1},{6,4},{7,3},{8,10},{9,13},{10,... | collective-permute-start | bytes 786440 | tf_op jit(solution)/shard_map/ppermute | solution.py:23
  244.0 9.7 %collective-permute-start.38 = (f32[256,512]{1,0:T(8,128)S(1)}, f32[256,512]{1,0:T(8,128)S(1)}, u32[]{:S(2)}, u32[]{:S(2)}) collective-permute-start(f32[256,512]{1,0:T(8,128)S(1)} %add.139), channel_id=1, source_target_pairs={{0,16},{1,9},{2,18},{3,11},{4,20},{5,13},{6,22},{7,15},{8,24},{9,1... | collective-permute-start | bytes 1572872 | tf_op jit(solution)/shard_map/ppermute | solution.py:23
  290.2 23.3 %collective-permute-start.40 = (bf16[2,128,3584]{2,1,0:T(8,128)(2,1)S(1)}, bf16[2,128,3584]{2,1,0:T(8,128)(2,1)S(1)}, u32[]{:S(2)}, u32[]{:S(2)}) collective-permute-start(bf16[2,128,3584]{2,1,0:T(8,128)(2,1)S(1)} %bitcast.45), channel_id=1, source_target_pairs={{0,8},{1,17},{2,10},{3,19},{4,12},{5,21},{6,14},{7,23},{8,0},{9,25... | collective-permute-start | bytes 5505032 | tf_op jit(solution)/shard_map/ppermute | solution.py:23
  316.8 13.7 %collective-permute-start.41 = (bf16[1,128,3584]{2,1,0:T(8,128)(2,1)}, bf16[1,128,3584]{2,1,0:T(8,128)(2,1)}, u32[]{:S(2)}, u32[]{:S(2)}) collective-permute-start(bf16[1,128,3584]{2,1,0:T(8,128)(2,1)} %slice.159), channel_id=1, source_target_pairs={{0,16},{1,9},{2,18},{3,11},{4,20},{5,13},{6,22},{7,15},{8,24},{9,1... | collective-permute-start | bytes 2752520 | tf_op jit(solution)/shard_map/ppermute | solution.py:23
  (41 other events, 435.3 us)

commit v4 on v3

--- a/solution.py
+++ b/solution.py
@@ -63,11 +63,15 @@
         return jnp.stack([self.block(v) for v in places]).astype(jnp.int32)
 
     def scatter_sum(self, send, keep):
+        terms = [keep]
         for t in range(len(self.orders[0])):
-            now = keep.astype(F32) + self.step(t, send).astype(F32)
-            half = now.shape[0] // 2
-            send, keep = now[half:].astype(BF16), now[:half]
-        return keep[0] if keep.shape[0] else now[0]
+            terms.append(self.step(t, send))
+            half = terms[0].shape[0] // 2
+            add = lambda part: sum(term[part].astype(F32) for term in terms)
+            if half:
+                send = add(slice(half, None)).astype(BF16)
+                terms = [term[:half] for term in terms]
+        return add(0)
 
     def gather(self, own):
         now = own[None]
@@ -205,21 +209,21 @@
         now = groups[g]
         column = [jnp.broadcast_to(now[:, base + j : base + j + 1], (8, size)) for j in range(8)]
         now = jnp.where(inside, jnp.where(lane - base == sub, 1.0, 0.0), now)
-        out = jnp.zeros((8, size), F32)
+        out, pivots, inverses = (jnp.ones((8, size), F32) for _ in range(3))
         for k in range(8):
             here = sub == k
             pivot = jnp.broadcast_to(column[k][k : k + 1], (8, size))
-            row = jnp.broadcast_to(now[k : k + 1], (8, size))
-            out = jnp.where(here, row * lax.rsqrt(pivot), out)
             inverse = pl.reciprocal(pivot, approx=True)
             inverse = inverse * (2.0 - pivot * inverse)
-            row = row * inverse
-            now = jnp.where(here, row, now - column[k] * row)
+            out, pivots = jnp.where(here, now, out), jnp.where(here, pivot, pivots)
+            inverses = jnp.where(here, inverse, inverses)
+            factor = jnp.where(here, 0.0, column[k]) * inverse
+            now = now - factor * jnp.broadcast_to(now[k : k + 1], (8, size))
             for j in range(k + 1, 8):
-                part = jnp.broadcast_to(column[j][k : k + 1], (8, size))
-                product = column[k] * part
-                column[j] = jnp.where(here, part * inverse, column[j] - product * inverse)
-        done.append(jnp.where(lane < base + 8, out, 0.0))
+                across = jnp.broadcast_to(column[j][k : k + 1], (8, size))
+                column[j] = column[j] - factor * across
+        now = now * inverses
+        done.append(jnp.where(lane < base + 8, out * lax.rsqrt(pivots), 0.0))
         rows = [jnp.broadcast_to(now[s : s + 1], (8, size)) for s in range(8)]
         for i in range(g + 1, size // 8):
             left = groups[i]
@@ -300,7 +304,7 @@
         here = pl.ds(pl.multiple_of(order_ref[i] * block, block), block)
         value = sum_ref[here, :]
         target = send_ref if i < half else keep_ref
-        target[i % half] = value.T if turned else value
+        target[i % half] = (value.T if turned else value).astype(target.dtype)
 
 
 def two_halves(size, shape, send_type):
@@ -389,7 +393,7 @@
     return product_call(
         rows_joined_kernel,
         "rows_times_joined",
-        two_halves(rows.size, (height // rows.size, width), F32),
+        two_halves(rows.size, (height // rows.size, width), BF16),
         pltpu.VMEM((height, width), F32),
         weight,
         width,
@@ -520,15 +524,17 @@
     square_scale = lax.dynamic_slice_in_dim(fisher, row * rows_here, rows_here) / mean
     own_square = lax.dynamic_slice_in_dim(square_scale, col * own_rows, own_rows)
 
-    def second_of(parts):
-        raw = over_col.scatter_sum(*parts)
-        first = over_col.gather(raw.astype(BF16))
-        parts = cols_times_joined(weight, square_scale, first, over_col, over_row)
+    def second_of(part):
+        first, scale = over_col.scatter_sum(*raw[part]), square_scale
+        if part:
+            first, scale = first * own_square, jnp.ones_like(square_scale)
+        first = over_col.gather(first.astype(BF16))
+        parts = cols_times_joined(weight, scale, first, over_col, over_row)
         projected = over_row.gather(over_row.scatter_sum(*parts).astype(BF16))
         parts = rows_times_joined(weight, projected, over_col, over_row)
         return over_col.gather(over_col.scatter_sum(*parts).astype(BF16))
 
-    second = settle(second_of(raw[0]), second_of(raw[1]), over_col)
+    second = settle(second_of(0), second_of(1), over_col)
 
     even = (col & 1) == 0
     mine = lax.dynamic_slice_in_dim(second, (col & 1) * half, half, 1).astype(F32)

time: 334 us -> 333 us (level)
  starting transfers between devices: 71.2 us -> 41.7 us
  waiting for transfers between devices: 142 us -> 171 us
    ppermute x42, starting transfers between devices: 71.2 us -> 41.7 us  [swap(): return lax.ppermute(block, AXES, pairs)]
    ppermute x42, waiting for transfers between devices: 142 us -> 171 us  [swap(): return lax.ppermute(block, AXES, pairs)]
    convert_element_type x2 -> x13, other arithmetic: 0.07 us -> 5.94 us  [the longest x11 3.87 us: scatter_sum(): send = add(slice(half, None)).astype(BF16)]
    unnamed x46 -> x36, local copies, waits for them, and re-layouts: 18.7 us -> 16.9 us
  transfers between devices with their start and end apart: 42 -> 42, of which waited for: 31 -> 31; matrix products, arithmetic and copies ran while one was open for 2% -> 3% of each run, Pallas kernels for 13% -> 13%
where the time goes in v4:
time: 333 us; the launch traced here: 332 us
  waiting for transfers between devices  171 us (51%)
  Pallas kernels  83.8 us (25%)
  starting transfers between devices  41.7 us (13%)
  local copies, waits for them, and re-layouts  17.1 us (5%)
  other arithmetic  9.62 us (3%)
  matrix products  7.41 us (2%)
    ppermute x42, waiting for transfers between devices, swap(): return lax.ppermute(block, AXES, pairs)  171 us
    ppermute x42, starting transfers between devices, swap(): return lax.ppermute(block, AXES, pairs)  41.7 us
    pallas_call x6, Pallas kernels, product_call(): pl.pallas_call(lambda *refs: kernel(*refs[len(after):]), out_shape=out_sh...  35.4 us
    pallas_call x1, Pallas kernels, inverse_factor(): pl.pallas_call(inverse_factor_kernel, out_shape=jax.ShapeDtypeStruct((siz...  27.8 us
    unnamed x36, local copies, waits for them, and re-layouts  16.9 us
    pallas_call x2, Pallas kernels, rank_times(): pl.pallas_call(rank_kernel, out_shape=jax.ShapeDtypeStruct((basis.shape[0...  9.91 us
    dot_general x8, matrix products, dot(): lax.dot_general(left, right, (dims, ((), ())), preferred_element_type=F32)  7.41 us
    pallas_call x1, Pallas kernels, local_mass(): pl.pallas_call(row_mass_kernel, out_shape=jax.ShapeDtypeStruct((1, width)...  7.37 us
  transfers between devices with their start and end apart: 42, of which 31 were waited for; matrix products, arithmetic and copies ran while one was open for 3% of the time, Pallas kernels for 13%

profile of v4, /device:TPU:0, one launch (start us, length us, event | category | flops | bytes accessed | tf_op | source)
XLA Modules:
  0.0 332.5 jit_solution(10907680015974720416)
XLA Ops:
  8.0 6.1 %rows_times.2 = (f32[4,256,256]{2,1,0:T(8,128)S(1)}, f32[4,256,256]{2,1,0:T(8,128)S(1)}) custom-call(s32[8]{0:T(128)S(1)} %stack.36.refs_0_.refs_1_.order_ref, bf16[2048,3584]{1,0:T(8,128)(2,1)S(1)} %copy-done, bf16[3584,512]{1,0:T(8,128)(2,1)S(1)} %copy-done.3), custom_call_target="tpu_custom_call" | custom-call | flops 3758096384 | bytes 16515072 | tf_op jit(solution)/shard_map/rows_times/pallas_call | solution.py:318
  18.0 7.4 %row_mass.1 = f32[1,8192]{1,0:T(1,128)S(1)} custom-call(bf16[2,256,8192]{2,1,0:T(8,128)(2,1)S(1)} %bitcast.50, bf16[2,512,256]{2,1,0:T(8,128)(2,1)S(1)} %get-tuple-element.17.gram_ref, f32[2,256,128]{2,1,0:T(8,128)S(1)} %get-tuple-element.18.scale_ref, bf16[2048,3584]{1,0:T(8,128)(2,1)S(1)} %copy-done.1), custom_call_target="tpu_custom_call" | custom-call | flops 4294967296 | bytes 8388608 | tf_op jit(solution)/shard_map/row_mass/pallas_call | solution.py:178
  25.4 6.1 %rows_times.3 = (f32[4,256,256]{2,1,0:T(8,128)S(1)}, f32[4,256,256]{2,1,0:T(8,128)S(1)}) custom-call(f32[8192]{0:T(1024)S(1)} %bitcast.52, s32[8]{0:T(128)S(1)} %stack.36.refs_0_.refs_1_.order_ref, bf16[2048,3584]{1,0:T(8,128)(2,1)S(1)} %copy-done.1, bf16[3584,512]{1,0:T(8,128)(2,1)S(1)} %copy-done.4), custom_call_target="tpu_custom_call" | custom-call | flops 3758096384 | bytes 16515072 | tf_op jit(solution)/shard_map/rows_times/pallas_call | solution.py:318
  37.0 5.8 %collective-permute-done.1 = f32[64,128]{1,0:T(8,128)S(1)} collective-permute-done((f32[64,128]{1,0:T(8,128)S(1)}, f32[64,128]{1,0:T(8,128)S(1)}, u32[]{:S(2)}, u32[]{:S(2)}) %collective-permute-start.1) | collective-permute-done | bytes 32800 | tf_op jit(solution)/shard_map/ppermute | solution.py:23
  72.7 8.6 %collective-permute-done.8 = bf16[1,256,256]{2,1,0:T(8,128)(2,1)S(1)} collective-permute-done((bf16[1,256,256]{2,1,0:T(8,128)(2,1)S(1)}, bf16[1,256,256]{2,1,0:T(8,128)(2,1)S(1)}, u32[]{:S(2)}, u32[]{:S(2)}) %collective-permute-start.8) | collective-permute-done | bytes 131104 | tf_op jit(solution)/shard_map/ppermute | solution.py:23
  87.0 6.4 %collective-permute-done.24 = bf16[1,256,256]{2,1,0:T(8,128)(2,1)S(1)} collective-permute-done((bf16[1,256,256]{2,1,0:T(8,128)(2,1)S(1)}, bf16[1,256,256]{2,1,0:T(8,128)(2,1)S(1)}, u32[]{:S(2)}, u32[]{:S(2)}) %collective-permute-start.24) | collective-permute-done | bytes 131104 | tf_op jit(solution)/shard_map/ppermute | solution.py:23
  93.6 6.2 %collective-permute-done.25 = bf16[2,256,256]{2,1,0:T(8,128)(2,1)S(1)} collective-permute-done((bf16[2,256,256]{2,1,0:T(8,128)(2,1)S(1)}, bf16[2,256,256]{2,1,0:T(8,128)(2,1)S(1)}, u32[]{:S(2)}, u32[]{:S(2)}) %collective-permute-start.25) | collective-permute-done | bytes 262176 | tf_op jit(solution)/shard_map/ppermute | solution.py:23
  105.3 5.8 %cols_times_joined.2 = (bf16[2,256,896]{2,1,0:T(8,128)(2,1)S(1)}, f32[2,256,896]{2,1,0:T(8,128)S(1)}) custom-call(s32[4]{0:T(128)S(1)} %pad_add_fusion.refs_0_.refs_1_, s32[8]{0:T(128)S(1)} %stack.36.refs_0_.refs_1_.order_ref, bf16[2048,3584]{1,0:T(8,128)(2,1)S(1)} %copy-done.2, f32[1,2048]{1,0:T(1,128)S(1)} %bitcast.55, ...), custom_call_target="tpu_custom_call" | custom-call | flops 3758096384 | bytes 16515072 | tf_op jit(solution)/shard_map/cols_times_joined/pallas_call | solution.py:318
  112.6 6.0 %cols_times_joined.3 = (bf16[2,256,896]{2,1,0:T(8,128)(2,1)S(1)}, f32[2,256,896]{2,1,0:T(8,128)S(1)}) custom-call(s32[4]{0:T(128)S(1)} %pad_add_fusion.refs_0_.refs_1_, s32[8]{0:T(128)S(1)} %stack.36.refs_0_.refs_1_.order_ref, bf16[2048,3584]{1,0:T(8,128)(2,1)S(1)} %copy-done.2, f32[1,2048]{1,0:T(1,128)S(1)} %broadcast_in_dim_broadcast_in_dim.3.refs_3_, ...), custom_call_target="tpu_custom_call" | custom-call | flops 3758096384 | bytes 16515072 | tf_op jit(solution)/shard_map/cols_times_joined/pallas_call | solution.py:318
  119.2 5.3 %collective-permute-done.11 = bf16[2,256,896]{2,1,0:T(8,128)(2,1)S(1)} collective-permute-done((bf16[2,256,896]{2,1,0:T(8,128)(2,1)S(1)}, bf16[2,256,896]{2,1,0:T(8,128)(2,1)S(1)}, u32[]{:S(2)}, u32[]{:S(2)}) %collective-permute-start.11) | collective-permute-done | bytes 917536 | tf_op jit(solution)/shard_map/ppermute | solution.py:23
  126.2 13.1 %collective-permute-done.27 = bf16[2,256,896]{2,1,0:T(8,128)(2,1)S(1)} collective-permute-done((bf16[2,256,896]{2,1,0:T(8,128)(2,1)S(1)}, bf16[2,256,896]{2,1,0:T(8,128)(2,1)S(1)}, u32[]{:S(2)}, u32[]{:S(2)}) %collective-permute-start.27) | collective-permute-done | bytes 917536 | tf_op jit(solution)/shard_map/ppermute | solution.py:23
  141.7 6.2 %collective-permute-done.28 = bf16[1,256,896]{2,1,0:T(8,128)(2,1)S(1)} collective-permute-done((bf16[1,256,896]{2,1,0:T(8,128)(2,1)S(1)}, bf16[1,256,896]{2,1,0:T(8,128)(2,1)S(1)}, u32[]{:S(2)}, u32[]{:S(2)}) %collective-permute-start.28) | collective-permute-done | bytes 458784 | tf_op jit(solution)/shard_map/ppermute | solution.py:23
  154.5 6.6 %collective-permute-done.29 = bf16[1,256,896]{2,1,0:T(8,128)(2,1)S(1)} collective-permute-done((bf16[1,256,896]{2,1,0:T(8,128)(2,1)S(1)}, bf16[1,256,896]{2,1,0:T(8,128)(2,1)S(1)}, u32[]{:S(2)}, u32[]{:S(2)}) %collective-permute-start.29) | collective-permute-done | bytes 458784 | tf_op jit(solution)/shard_map/ppermute | solution.py:23
  166.4 5.7 %rows_times_joined.2 = (bf16[4,256,256]{2,1,0:T(8,128)(2,1)S(1)}, f32[4,256,256]{2,1,0:T(8,128)S(1)}) custom-call(s32[8]{0:T(128)S(1)} %stack.36.refs_0_.refs_1_.order_ref, s32[4]{0:T(128)S(1)} %pad_add_fusion.refs_0_.refs_1_, bf16[2048,3584]{1,0:T(8,128)(2,1)S(1)} %copy-done.2, bf16[2,256,896]{2,1,0:T(8,128)(2,1)S(1)} %pad_maximum_fusion.1.refs_3_, ...), custom_call_target="tpu_custom_call" | custom-call | flops 3758096384 | bytes 16515072 | tf_op jit(solution)/shard_map/rows_times_joined/pallas_call | solution.py:318
  176.2 5.7 %rows_times_joined.3 = (bf16[4,256,256]{2,1,0:T(8,128)(2,1)S(1)}, f32[4,256,256]{2,1,0:T(8,128)S(1)}) custom-call(s32[8]{0:T(128)S(1)} %stack.36.refs_0_.refs_1_.order_ref, s32[4]{0:T(128)S(1)} %pad_add_fusion.refs_0_.refs_1_, bf16[2048,3584]{1,0:T(8,128)(2,1)S(1)} %copy-done.2, bf16[2,256,896]{2,1,0:T(8,128)(2,1)S(1)} %pad_maximum_fusion.2.refs_3_, ...), custom_call_target="tpu_custom_call" | custom-call | flops 3758096384 | bytes 16515072 | tf_op jit(solution)/shard_map/rows_times_joined/pallas_call | solution.py:318
  185.3 7.0 %collective-permute-done.16 = bf16[2,256,256]{2,1,0:T(8,128)(2,1)S(1)} collective-permute-done((bf16[2,256,256]{2,1,0:T(8,128)(2,1)S(1)}, bf16[2,256,256]{2,1,0:T(8,128)(2,1)S(1)}, u32[]{:S(2)}, u32[]{:S(2)}) %collective-permute-start.16) | collective-permute-done | bytes 262176 | tf_op jit(solution)/shard_map/ppermute | solution.py:23
  192.8 7.9 %collective-permute-done.32 = bf16[2,256,256]{2,1,0:T(8,128)(2,1)S(1)} collective-permute-done((bf16[2,256,256]{2,1,0:T(8,128)(2,1)S(1)}, bf16[2,256,256]{2,1,0:T(8,128)(2,1)S(1)}, u32[]{:S(2)}, u32[]{:S(2)}) %collective-permute-start.32) | collective-permute-done | bytes 262176 | tf_op jit(solution)/shard_map/ppermute | solution.py:23
  208.2 10.3 %collective-permute-done.18 = bf16[1,256,256]{2,1,0:T(8,128)(2,1)S(1)} collective-permute-done((bf16[1,256,256]{2,1,0:T(8,128)(2,1)S(1)}, bf16[1,256,256]{2,1,0:T(8,128)(2,1)S(1)}, u32[]{:S(2)}, u32[]{:S(2)}) %collective-permute-start.18) | collective-permute-done | bytes 131104 | tf_op jit(solution)/shard_map/ppermute | solution.py:23
  221.4 5.9 %collective-permute-done.19 = bf16[2,256,256]{2,1,0:T(8,128)(2,1)S(1)} collective-permute-done((bf16[2,256,256]{2,1,0:T(8,128)(2,1)S(1)}, bf16[2,256,256]{2,1,0:T(8,128)(2,1)S(1)}, u32[]{:S(2)}, u32[]{:S(2)}) %collective-permute-start.19) | collective-permute-done | bytes 262176 | tf_op jit(solution)/shard_map/ppermute | solution.py:23
  240.1 7.7 %collective-permute-done.37 = f32[256,512]{1,0:T(8,128)S(1)} collective-permute-done((f32[256,512]{1,0:T(8,128)S(1)}, f32[256,512]{1,0:T(8,128)S(1)}, u32[]{:S(2)}, u32[]{:S(2)}) %collective-permute-start.37) | collective-permute-done | bytes 524320 | tf_op jit(solution)/shard_map/ppermute | solution.py:23
  249.4 7.7 %collective-permute-done.38 = f32[256,512]{1,0:T(8,128)S(1)} collective-permute-done((f32[256,512]{1,0:T(8,128)S(1)}, f32[256,512]{1,0:T(8,128)S(1)}, u32[]{:S(2)}, u32[]{:S(2)}) %collective-permute-start.38) | collective-permute-done | bytes 524320 | tf_op jit(solution)/shard_map/ppermute | solution.py:23
  259.4 27.8 %inverse_factor.1 = f32[512,512]{1,0:T(8,128)S(1)} custom-call(f32[512,512]{1,0:T(8,128)S(1)} %pad_maximum_fusion.gram_ref), custom_call_target="tpu_custom_call" | custom-call | flops 5368709120 | bytes 2097152 | tf_op jit(solution)/shard_map/inverse_factor/pallas_call | solution.py:276
  302.0 15.3 %collective-permute-done.40 = bf16[2,128,3584]{2,1,0:T(8,128)(2,1)S(1)} collective-permute-done((bf16[2,128,3584]{2,1,0:T(8,128)(2,1)S(1)}, bf16[2,128,3584]{2,1,0:T(8,128)(2,1)S(1)}, u32[]{:S(2)}, u32[]{:S(2)}) %collective-permute-start.40) | collective-permute-done | bytes 1835040 | tf_op jit(solution)/shard_map/ppermute | solution.py:23
  320.4 10.4 %collective-permute-done.41 = bf16[1,128,3584]{2,1,0:T(8,128)(2,1)S(1)} collective-permute-done((bf16[1,128,3584]{2,1,0:T(8,128)(2,1)S(1)}, bf16[1,128,3584]{2,1,0:T(8,128)(2,1)S(1)}, u32[]{:S(2)}, u32[]{:S(2)}) %collective-permute-start.41) | collective-permute-done | bytes 917536 | tf_op jit(solution)/shard_map/ppermute | solution.py:23
  (161 shorter events, 129.5 us)
Async XLA Ops:
  14.1 18.1 %collective-permute-start.5 = (f32[4,256,256]{2,1,0:T(8,128)S(1)}, f32[4,256,256]{2,1,0:T(8,128)S(1)}, u32[]{:S(2)}, u32[]{:S(2)}) collective-permute-start(f32[4,256,256]{2,1,0:T(8,128)S(1)} %get-tuple-element.19), channel_id=1, source_target_pairs={{0,1},{1,0},{2,3},{3,2},{4,5},{5,4},{6,7},{7,6},{8,9},{9,8},{10,11... | collective-permute-start | bytes 3145736 | tf_op jit(solution)/shard_map/ppermute | solution.py:23
  31.5 28.8 %collective-permute-start.21 = (f32[4,256,256]{2,1,0:T(8,128)S(1)}, f32[4,256,256]{2,1,0:T(8,128)}, u32[]{:S(2)}, u32[]{:S(2)}) collective-permute-start(f32[4,256,256]{2,1,0:T(8,128)S(1)} %get-tuple-element.25), channel_id=1, source_target_pairs={{0,1},{1,0},{2,3},{3,2},{4,5},{5,4},{6,7},{7,6},{8,9},{9,8},{10,11... | collective-permute-start | bytes 3145736 | tf_op jit(solution)/shard_map/ppermute | solution.py:23
  32.2 24.8 %collective-permute-start.6 = (bf16[2,256,256]{2,1,0:T(8,128)(2,1)S(1)}, bf16[2,256,256]{2,1,0:T(8,128)(2,1)}, u32[]{:S(2)}, u32[]{:S(2)}) collective-permute-start(bf16[2,256,256]{2,1,0:T(8,128)(2,1)S(1)} %fusion.20), channel_id=1, source_target_pairs={{0,2},{1,5},{2,0},{3,7},{4,6},{5,1},{6,4},{7,3},{8,10},{9,13},{10,... | collective-permute-start | bytes 786440 | tf_op jit(solution)/shard_map/ppermute | solution.py:23
  58.0 9.6 %collective-permute-start.7 = (bf16[1,256,256]{2,1,0:T(8,128)(2,1)S(1)}, bf16[1,256,256]{2,1,0:T(8,128)(2,1)S(1)}, u32[]{:S(2)}, u32[]{:S(2)}) collective-permute-start(bf16[1,256,256]{2,1,0:T(8,128)(2,1)S(1)} %fusion.32), channel_id=1, source_target_pairs={{0,4},{1,3},{2,6},{3,1},{4,0},{5,7},{6,2},{7,5},{8,12},{9,11},{10,... | collective-permute-start | bytes 393224 | tf_op jit(solution)/shard_map/ppermute | solution.py:23
  61.4 9.7 %collective-permute-start.22 = (bf16[2,256,256]{2,1,0:T(8,128)(2,1)S(1)}, bf16[2,256,256]{2,1,0:T(8,128)(2,1)S(1)}, u32[]{:S(2)}, u32[]{:S(2)}) collective-permute-start(bf16[2,256,256]{2,1,0:T(8,128)(2,1)S(1)} %fusion.19), channel_id=1, source_target_pairs={{0,2},{1,5},{2,0},{3,7},{4,6},{5,1},{6,4},{7,3},{8,10},{9,13},{10,... | collective-permute-start | bytes 786440 | tf_op jit(solution)/shard_map/ppermute | solution.py:23
  68.6 12.8 %collective-permute-start.8 = (bf16[1,256,256]{2,1,0:T(8,128)(2,1)S(1)}, bf16[1,256,256]{2,1,0:T(8,128)(2,1)S(1)}, u32[]{:S(2)}, u32[]{:S(2)}) collective-permute-start(bf16[1,256,256]{2,1,0:T(8,128)(2,1)S(1)} %fusion.35), channel_id=1, source_target_pairs={{0,4},{1,3},{2,6},{3,1},{4,0},{5,7},{6,2},{7,5},{8,12},{9,11},{10,... | collective-permute-start | bytes 393224 | tf_op jit(solution)/shard_map/ppermute | solution.py:23
  72.1 13.8 %collective-permute-start.23 = (bf16[1,256,256]{2,1,0:T(8,128)(2,1)S(1)}, bf16[1,256,256]{2,1,0:T(8,128)(2,1)S(1)}, u32[]{:S(2)}, u32[]{:S(2)}) collective-permute-start(bf16[1,256,256]{2,1,0:T(8,128)(2,1)S(1)} %fusion.26), channel_id=1, source_target_pairs={{0,4},{1,3},{2,6},{3,1},{4,0},{5,7},{6,2},{7,5},{8,12},{9,11},{10,... | collective-permute-start | bytes 393224 | tf_op jit(solution)/shard_map/ppermute | solution.py:23
  81.4 12.1 %collective-permute-start.9 = (bf16[2,256,256]{2,1,0:T(8,128)(2,1)S(1)}, bf16[2,256,256]{2,1,0:T(8,128)(2,1)S(1)}, u32[]{:S(2)}, u32[]{:S(2)}) collective-permute-start(bf16[2,256,256]{2,1,0:T(8,128)(2,1)S(1)} %pad_maximum_fusion.9), channel_id=1, source_target_pairs={{0,2},{1,5},{2,0},{3,7},{4,6},{5,1},{6,4},{7,3},{8,10},{9,13},{10,... | collective-permute-start | bytes 786440 | tf_op jit(solution)/shard_map/ppermute | solution.py:23
  99.9 12.7 %collective-permute-start.26 = (bf16[4,256,256]{2,1,0:T(8,128)(2,1)S(1)}, bf16[4,256,256]{2,1,0:T(8,128)(2,1)S(1)}, u32[]{:S(2)}, u32[]{:S(2)}) collective-permute-start(bf16[4,256,256]{2,1,0:T(8,128)(2,1)S(1)} %pad_maximum_fusion.5.refs_4_), channel_id=1, source_target_pairs={{0,1},{1,0},{2,3},{3,2},{4,5},{5,4},{6,7},{7,6},{8,9},{9,8},{10,11... | collective-permute-start | bytes 1572872 | tf_op jit(solution)/shard_map/ppermute | solution.py:23
  111.1 13.5 %collective-permute-start.11 = (bf16[2,256,896]{2,1,0:T(8,128)(2,1)S(1)}, bf16[2,256,896]{2,1,0:T(8,128)(2,1)S(1)}, u32[]{:S(2)}, u32[]{:S(2)}) collective-permute-start(bf16[2,256,896]{2,1,0:T(8,128)(2,1)S(1)} %get-tuple-element.21), channel_id=1, source_target_pairs={{0,8},{1,17},{2,10},{3,19},{4,12},{5,21},{6,14},{7,23},{8,0},{9,25... | collective-permute-start | bytes 2752520 | tf_op jit(solution)/shard_map/ppermute | solution.py:23
  118.6 20.7 %collective-permute-start.27 = (bf16[2,256,896]{2,1,0:T(8,128)(2,1)S(1)}, bf16[2,256,896]{2,1,0:T(8,128)(2,1)S(1)}, u32[]{:S(2)}, u32[]{:S(2)}) collective-permute-start(bf16[2,256,896]{2,1,0:T(8,128)(2,1)S(1)} %get-tuple-element.27), channel_id=1, source_target_pairs={{0,8},{1,17},{2,10},{3,19},{4,12},{5,21},{6,14},{7,23},{8,0},{9,25... | collective-permute-start | bytes 2752520 | tf_op jit(solution)/shard_map/ppermute | solution.py:23
  124.6 16.3 %collective-permute-start.12 = (bf16[1,256,896]{2,1,0:T(8,128)(2,1)S(1)}, bf16[1,256,896]{2,1,0:T(8,128)(2,1)S(1)}, u32[]{:S(2)}, u32[]{:S(2)}) collective-permute-start(bf16[1,256,896]{2,1,0:T(8,128)(2,1)S(1)} %add_convert_fusion.3), channel_id=1, source_target_pairs={{0,16},{1,9},{2,18},{3,11},{4,20},{5,13},{6,22},{7,15},{8,24},{9,1... | collective-permute-start | bytes 1376264 | tf_op jit(solution)/shard_map/ppermute | solution.py:23
  141.1 11.7 %collective-permute-start.13 = (bf16[1,256,896]{2,1,0:T(8,128)(2,1)S(1)}, bf16[1,256,896]{2,1,0:T(8,128)(2,1)S(1)}, u32[]{:S(2)}, u32[]{:S(2)}) collective-permute-start(bf16[1,256,896]{2,1,0:T(8,128)(2,1)S(1)} %add_convert_fusion.2), channel_id=1, source_target_pairs={{0,16},{1,9},{2,18},{3,11},{4,20},{5,13},{6,22},{7,15},{8,24},{9,1... | collective-permute-start | bytes 1376264 | tf_op jit(solution)/shard_map/ppermute | solution.py:23
  148.1 13.0 %collective-permute-start.29 = (bf16[1,256,896]{2,1,0:T(8,128)(2,1)S(1)}, bf16[1,256,896]{2,1,0:T(8,128)(2,1)S(1)}, u32[]{:S(2)}, u32[]{:S(2)}) collective-permute-start(bf16[1,256,896]{2,1,0:T(8,128)(2,1)S(1)} %add_convert_fusion), channel_id=1, source_target_pairs={{0,16},{1,9},{2,18},{3,11},{4,20},{5,13},{6,22},{7,15},{8,24},{9,1... | collective-permute-start | bytes 1376264 | tf_op jit(solution)/shard_map/ppermute | solution.py:23
  152.9 13.5 %collective-permute-start.14 = (bf16[2,256,896]{2,1,0:T(8,128)(2,1)S(1)}, bf16[2,256,896]{2,1,0:T(8,128)(2,1)S(1)}, u32[]{:S(2)}, u32[]{:S(2)}) collective-permute-start(bf16[2,256,896]{2,1,0:T(8,128)(2,1)S(1)} %pad_maximum_fusion.1.refs_3_), channel_id=1, source_target_pairs={{0,8},{1,17},{2,10},{3,19},{4,12},{5,21},{6,14},{7,23},{8,0},{9,25... | collective-permute-start | bytes 2752520 | tf_op jit(solution)/shard_map/ppermute | solution.py:23
  161.2 15.1 %collective-permute-start.30 = (bf16[2,256,896]{2,1,0:T(8,128)(2,1)S(1)}, bf16[2,256,896]{2,1,0:T(8,128)(2,1)S(1)}, u32[]{:S(2)}, u32[]{:S(2)}) collective-permute-start(bf16[2,256,896]{2,1,0:T(8,128)(2,1)S(1)} %pad_maximum_fusion.2.refs_3_), channel_id=1, source_target_pairs={{0,8},{1,17},{2,10},{3,19},{4,12},{5,21},{6,14},{7,23},{8,0},{9,25... | collective-permute-start | bytes 2752520 | tf_op jit(solution)/shard_map/ppermute | solution.py:23
  172.1 10.9 %collective-permute-start.15 = (bf16[4,256,256]{2,1,0:T(8,128)(2,1)S(1)}, bf16[4,256,256]{2,1,0:T(8,128)(2,1)S(1)}, u32[]{:S(2)}, u32[]{:S(2)}) collective-permute-start(bf16[4,256,256]{2,1,0:T(8,128)(2,1)S(1)} %get-tuple-element.23), channel_id=1, source_target_pairs={{0,1},{1,0},{2,3},{3,2},{4,5},{5,4},{6,7},{7,6},{8,9},{9,8},{10,11... | collective-permute-start | bytes 1572872 | tf_op jit(solution)/shard_map/ppermute | solution.py:23
  184.6 16.1 %collective-permute-start.32 = (bf16[2,256,256]{2,1,0:T(8,128)(2,1)S(1)}, bf16[2,256,256]{2,1,0:T(8,128)(2,1)S(1)}, u32[]{:S(2)}, u32[]{:S(2)}) collective-permute-start(bf16[2,256,256]{2,1,0:T(8,128)(2,1)S(1)} %add_convert_fusion.4), channel_id=1, source_target_pairs={{0,2},{1,5},{2,0},{3,7},{4,6},{5,1},{6,4},{7,3},{8,10},{9,13},{10,... | collective-permute-start | bytes 786440 | tf_op jit(solution)/shard_map/ppermute | solution.py:23
  201.0 17.5 %collective-permute-start.18 = (bf16[1,256,256]{2,1,0:T(8,128)(2,1)S(1)}, bf16[1,256,256]{2,1,0:T(8,128)(2,1)S(1)}, u32[]{:S(2)}, u32[]{:S(2)}) collective-permute-start(bf16[1,256,256]{2,1,0:T(8,128)(2,1)S(1)} %add_convert_fusion.8), channel_id=1, source_target_pairs={{0,4},{1,3},{2,6},{3,1},{4,0},{5,7},{6,2},{7,5},{8,12},{9,11},{10,... | collective-permute-start | bytes 393224 | tf_op jit(solution)/shard_map/ppermute | solution.py:23
  207.9 13.5 %collective-permute-start.34 = (bf16[1,256,256]{2,1,0:T(8,128)(2,1)S(1)}, bf16[1,256,256]{2,1,0:T(8,128)(2,1)S(1)}, u32[]{:S(2)}, u32[]{:S(2)}) collective-permute-start(bf16[1,256,256]{2,1,0:T(8,128)(2,1)S(1)} %add_convert_fusion.6), channel_id=1, source_target_pairs={{0,4},{1,3},{2,6},{3,1},{4,0},{5,7},{6,2},{7,5},{8,12},{9,11},{10,... | collective-permute-start | bytes 393224 | tf_op jit(solution)/shard_map/ppermute | solution.py:23
  238.6 9.2 %collective-permute-start.37 = (f32[256,512]{1,0:T(8,128)S(1)}, f32[256,512]{1,0:T(8,128)S(1)}, u32[]{:S(2)}, u32[]{:S(2)}) collective-permute-start(f32[256,512]{1,0:T(8,128)S(1)} %convolution_add_fusion.2), channel_id=1, source_target_pairs={{0,8},{1,17},{2,10},{3,19},{4,12},{5,21},{6,14},{7,23},{8,0},{9,25... | collective-permute-start | bytes 1572872 | tf_op jit(solution)/shard_map/ppermute | solution.py:23
  247.9 9.2 %collective-permute-start.38 = (f32[256,512]{1,0:T(8,128)S(1)}, f32[256,512]{1,0:T(8,128)S(1)}, u32[]{:S(2)}, u32[]{:S(2)}) collective-permute-start(f32[256,512]{1,0:T(8,128)S(1)} %add.214), channel_id=1, source_target_pairs={{0,16},{1,9},{2,18},{3,11},{4,20},{5,13},{6,22},{7,15},{8,24},{9,1... | collective-permute-start | bytes 1572872 | tf_op jit(solution)/shard_map/ppermute | solution.py:23
  293.9 23.3 %collective-permute-start.40 = (bf16[2,128,3584]{2,1,0:T(8,128)(2,1)S(1)}, bf16[2,128,3584]{2,1,0:T(8,128)(2,1)S(1)}, u32[]{:S(2)}, u32[]{:S(2)}) collective-permute-start(bf16[2,128,3584]{2,1,0:T(8,128)(2,1)S(1)} %bitcast.51), channel_id=1, source_target_pairs={{0,8},{1,17},{2,10},{3,19},{4,12},{5,21},{6,14},{7,23},{8,0},{9,25... | collective-permute-start | bytes 5505032 | tf_op jit(solution)/shard_map/ppermute | solution.py:23
  317.4 13.5 %collective-permute-start.41 = (bf16[1,128,3584]{2,1,0:T(8,128)(2,1)S(1)}, bf16[1,128,3584]{2,1,0:T(8,128)(2,1)S(1)}, u32[]{:S(2)}, u32[]{:S(2)}) collective-permute-start(bf16[1,128,3584]{2,1,0:T(8,128)(2,1)S(1)} %fusion.6), channel_id=1, source_target_pairs={{0,16},{1,9},{2,18},{3,11},{4,20},{5,13},{6,22},{7,15},{8,24},{9,1... | collective-permute-start | bytes 2752520 | tf_op jit(solution)/shard_map/ppermute | solution.py:23
  (36 other events, 246.0 us)

commit v5 on v4

--- a/solution.py
+++ b/solution.py
@@ -21,6 +21,11 @@
             other = (row ^ row_bit(col & 1)) * cols + (col ^ col_bit(col & 1))
             pairs.append((row * cols + col, other))
     return lax.ppermute(block, AXES, pairs)
+
+
+def split(value):
+    high = lax.reduce_precision(value, 8, 7)
+    return high.astype(BF16), (value - high).astype(BF16)
 
 
 class Halving:
@@ -62,16 +67,26 @@
         places = [*range(half, self.size), *range(half)]
         return jnp.stack([self.block(v) for v in places]).astype(jnp.int32)
 
-    def scatter_sum(self, send, keep):
+    def scatter_sum(self, send, keep, rider=None):
         terms = [keep]
         for t in range(len(self.orders[0])):
-            terms.append(self.step(t, send))
+            came = self.step(t, send)
+            if rider is not None:
+                height = rider.shape[0]
+                *parts, blocks = jnp.split(came, [height] if t == 0 else [height, 2 * height])
+                rider = rider + sum(part.astype(F32) for part in parts)
+                came = blocks.reshape(terms[0].shape)
+            terms.append(came)
             half = terms[0].shape[0] // 2
             add = lambda part: sum(term[part].astype(F32) for term in terms)
             if half:
                 send = add(slice(half, None)).astype(BF16)
                 terms = [term[:half] for term in terms]
-        return add(0)
+                if rider is not None:
+                    parts = split(rider)
+                    rider = sum(part.astype(F32) for part in parts)
+                    send = jnp.concatenate([*parts, send.reshape(-1, send.shape[-1])])
+        return add(0) if rider is None else (add(0), rider)
 
     def gather(self, own):
         now = own[None]
@@ -213,15 +228,14 @@
         for k in range(8):
             here = sub == k
             pivot = jnp.broadcast_to(column[k][k : k + 1], (8, size))
-            inverse = pl.reciprocal(pivot, approx=True)
-            inverse = inverse * (2.0 - pivot * inverse)
+            inverse = 1.0 / pivot
             out, pivots = jnp.where(here, now, out), jnp.where(here, pivot, pivots)
             inverses = jnp.where(here, inverse, inverses)
-            factor = jnp.where(here, 0.0, column[k]) * inverse
-            now = now - factor * jnp.broadcast_to(now[k : k + 1], (8, size))
+            factor = jnp.where(here, 0.0, column[k])
+            now = now - factor * jnp.broadcast_to(now[k : k + 1], (8, size)) * inverse
             for j in range(k + 1, 8):
                 across = jnp.broadcast_to(column[j][k : k + 1], (8, size))
-                column[j] = column[j] - factor * across
+                column[j] = column[j] - factor * across * inverse
         now = now * inverses
         done.append(jnp.where(lane < base + 8, out * lax.rsqrt(pivots), 0.0))
         rows = [jnp.broadcast_to(now[s : s + 1], (8, size)) for s in range(8)]
@@ -298,13 +312,20 @@
 
 
 def gather_rows(order_ref, sum_ref, send_ref, keep_ref, turned):
-    half = send_ref.shape[0]
+    half, height = keep_ref.shape[:2]
+    above = send_ref.shape[0] - half * height
     block = sum_ref.shape[0] // (2 * half)
     for i in range(2 * half):
         here = pl.ds(pl.multiple_of(order_ref[i] * block, block), block)
         value = sum_ref[here, :]
-        target = send_ref if i < half else keep_ref
-        target[i % half] = (value.T if turned else value).astype(target.dtype)
+        value = value.T if turned else value
+        if i >= half:
+            keep_ref[i - half] = value
+        elif len(send_ref.shape) == 3:
+            send_ref[i] = value.astype(send_ref.dtype)
+        else:
+            start = above + i * height
+            send_ref[start : start + height] = value
 
 
 def two_halves(size, shape, send_type):
@@ -312,15 +333,13 @@
     return (jax.ShapeDtypeStruct(dims, send_type), jax.ShapeDtypeStruct(dims, F32))
 
 
-def product_call(kernel, name, out_shape, scratch, weight, width, indices, arrays, after=()):
+def product_call(kernel, name, out_shape, scratch, weight, width, indices, arrays):
     height, depth = weight.shape
     smem, vmem = (pl.BlockSpec(memory_space=space) for space in (pltpu.SMEM, pltpu.VMEM))
     return pl.pallas_call(
-        lambda *refs: kernel(*refs[len(after) :]),
+        kernel,
         out_shape=out_shape,
-        in_specs=[pl.BlockSpec(memory_space=pl.ANY)] * len(after)
-        + [smem] * len(indices)
-        + [vmem] * (1 + len(arrays)),
+        in_specs=[smem] * len(indices) + [vmem] * (1 + len(arrays)),
         out_specs=(vmem, vmem),
         scratch_shapes=[scratch],
         compiler_params=pltpu.CompilerParams(vmem_limit_bytes=LIMIT),
@@ -330,10 +349,11 @@
             transcendentals=0,
         ),
         name=name,
-    )(*after, *indices, weight, *arrays)
-
-
-def rows_plain_kernel(part, width, turned, order_ref, weight_ref, right_ref, send_ref, keep_ref, sum_ref):
+    )(*indices, weight, *arrays)
+
+
+def rows_plain_kernel(part, width, turned, order_ref, weight_ref, right_ref, *refs):
+    *rider_ref, send_ref, keep_ref, sum_ref = refs
     depth = weight_ref.shape[1]
     chunk = 512 if depth % 512 == 0 else depth
 
@@ -347,13 +367,18 @@
     def _(i):
         sum_ref[...] += term(pl.multiple_of(i * chunk, chunk))
 
+    if rider_ref:
+        send_ref[: rider_ref[0].shape[0]] = rider_ref[0][...]
     gather_rows(order_ref, sum_ref, send_ref, keep_ref, turned)
 
 
-def rows_times(weight, right, part, width, rows, turned, after=()):
+def rows_times(weight, right, part, width, rows, turned, rider=()):
     height = weight.shape[0]
     block = height // rows.size
     shapes = two_halves(rows.size, (width, block) if turned else (block, width), F32)
+    for load in rider:
+        dims = (load.shape[0] + rows.size // 2 * width, block)
+        shapes = (jax.ShapeDtypeStruct(dims, F32), shapes[1])
     return product_call(
         functools.partial(rows_plain_kernel, part, width, turned),
         "rows_times",
@@ -362,8 +387,7 @@
         weight,
         width,
         (rows.sending_first(),),
-        (right,),
-        after,
+        (right, *rider),
     )
 
 
@@ -501,11 +525,6 @@
     )(rows.sending_first(), *left, *right)
 
 
-def split(value):
-    high = lax.reduce_precision(value, 8, 7)
-    return high.astype(BF16), (value - high).astype(BF16)
-
-
 def local(activations, out_grads, valid_len, weight, sketch):
     width = activations.shape[2]
     rows_here, cols_here = weight.shape
@@ -516,25 +535,25 @@
     own_rows = rows_here // col_count
     over_col, over_row = Halving("col"), Halving("row")
 
-    raw = [rows_times(weight, sketch, 0, half, over_col, True)]
-    mass = local_mass(activations, out_grads, valid_len, raw[0][1], weight)
-    raw.append(rows_times(weight, sketch, 1, half, over_col, True, (mass,)))
-    fisher = sum_everywhere(mass.reshape(-1, 128)).reshape(width)
+    raw = rows_times(weight, sketch, 0, half, over_col, True)
+    mass = local_mass(activations, out_grads, valid_len, raw[1], weight)
+    mass = mass.reshape(-1, own_rows)
+    later = rows_times(weight, sketch, 1, half, over_col, True, (mass,))
+    raw = over_col.scatter_sum(*raw)
+    later, fisher = over_col.scatter_sum(*later, mass)
+    fisher = sum_everywhere(fisher, col=False).reshape(width)
     mean = jnp.sum(fisher) / width + 1e-06
     square_scale = lax.dynamic_slice_in_dim(fisher, row * rows_here, rows_here) / mean
     own_square = lax.dynamic_slice_in_dim(square_scale, col * own_rows, own_rows)
 
-    def second_of(part):
-        first, scale = over_col.scatter_sum(*raw[part]), square_scale
-        if part:
-            first, scale = first * own_square, jnp.ones_like(square_scale)
-        first = over_col.gather(first.astype(BF16))
-        parts = cols_times_joined(weight, scale, first, over_col, over_row)
+    def second_of(raw):
+        first = over_col.gather(raw.astype(BF16))
+        parts = cols_times_joined(weight, square_scale, first, over_col, over_row)
         projected = over_row.gather(over_row.scatter_sum(*parts).astype(BF16))
         parts = rows_times_joined(weight, projected, over_col, over_row)
         return over_col.gather(over_col.scatter_sum(*parts).astype(BF16))
 
-    second = settle(second_of(0), second_of(1), over_col)
+    second = settle(second_of(raw), second_of(later), over_col)
 
     even = (col & 1) == 0
     mine = lax.dynamic_slice_in_dim(second, (col & 1) * half, half, 1).astype(F32)

time: 333 us -> 324 us (0.973)
  waiting for transfers between devices: 171 us -> 153 us
  local copies, waits for them, and re-layouts: 17.1 us -> 24.9 us
  Pallas kernels: 83.8 us -> 77.8 us
  starting transfers between devices: 41.7 us -> 46.5 us
    ppermute x42 -> x39, waiting for transfers between devices: 171 us -> 153 us  [swap(): return lax.ppermute(block, AXES, pairs)]
    unnamed x36 -> x45, local copies, waits for them, and re-layouts: 16.9 us -> 24.2 us
    pallas_call x1, Pallas kernels: 27.8 us -> 21.3 us  [inverse_factor(): pl.pallas_call(inverse_factor_kernel, out_shape=jax.ShapeDtypeStruct((siz...]
    ppermute x42 -> x39, starting transfers between devices: 41.7 us -> 46.5 us  [swap(): return lax.ppermute(block, AXES, pairs)]
  transfers between devices with their start and end apart: 42 -> 39, of which waited for: 31 -> 29; matrix products, arithmetic and copies ran while one was open for 3% -> 3% of each run, Pallas kernels for 13% -> 14%
where the time goes in v5:
time: 324 us; the launch traced here: 323 us
  waiting for transfers between devices  153 us (47%)
  Pallas kernels  77.8 us (24%)
  starting transfers between devices  46.5 us (14%)
  local copies, waits for them, and re-layouts  24.9 us (8%)
  other arithmetic  11.9 us (4%)
  matrix products  7.31 us (2%)
    ppermute x39, waiting for transfers between devices, swap(): return lax.ppermute(block, AXES, pairs)  153 us
    ppermute x39, starting transfers between devices, swap(): return lax.ppermute(block, AXES, pairs)  46.5 us
    pallas_call x6, Pallas kernels, product_call(): pl.pallas_call(kernel, out_shape=out_shape, in_specs=[smem] * len(indices...  35.9 us
    unnamed x45, local copies, waits for them, and re-layouts  24.2 us
    pallas_call x1, Pallas kernels, inverse_factor(): pl.pallas_call(inverse_factor_kernel, out_shape=jax.ShapeDtypeStruct((siz...  21.3 us
    pallas_call x2, Pallas kernels, rank_times(): pl.pallas_call(rank_kernel, out_shape=jax.ShapeDtypeStruct((basis.shape[0...  9.91 us
    pallas_call x1, Pallas kernels, local_mass(): pl.pallas_call(row_mass_kernel, out_shape=jax.ShapeDtypeStruct((1, width)...  7.4 us
    dot_general x8, matrix products, dot(): lax.dot_general(left, right, (dims, ((), ())), preferred_element_type=F32)  7.31 us
  transfers between devices with their start and end apart: 39, of which 29 were waited for; matrix products, arithmetic and copies ran while one was open for 3% of the time, Pallas kernels for 14%

profile of v5, /device:TPU:0, one launch (start us, length us, event | category | flops | bytes accessed | tf_op | source)
XLA Modules:
  0.0 323.2 jit_solution(12568324412274081223)
XLA Ops:
  0.7 5.2 %copy-done = bf16[2048,3584]{1,0:T(8,128)(2,1)S(1)} copy-done((bf16[2048,3584]{1,0:T(8,128)(2,1)S(1)}, bf16[2048,3584]{1,0:T(8,128)(2,1)}, u32[]{:S(2)}) %copy-start) | copy-done | bytes 14680088
  8.0 6.3 %rows_times.2 = (f32[4,256,256]{2,1,0:T(8,128)S(1)}, f32[4,256,256]{2,1,0:T(8,128)S(1)}) custom-call(s32[8]{0:T(128)S(1)} %stack.36.order_ref.rows_ref, bf16[2048,3584]{1,0:T(8,128)(2,1)S(1)} %copy-done, bf16[3584,512]{1,0:T(8,128)(2,1)S(1)} %copy-done.4), custom_call_target="tpu_custom_call" | custom-call | flops 3758096384 | bytes 16515072 | tf_op jit(solution)/shard_map/rows_times/pallas_call | solution.py:339
  18.3 7.4 %row_mass.1 = f32[1,8192]{1,0:T(1,128)S(1)} custom-call(bf16[2,256,8192]{2,1,0:T(8,128)(2,1)S(1)} %bitcast.74, bf16[2,512,256]{2,1,0:T(8,128)(2,1)S(1)} %get-tuple-element.17.gram_ref, f32[2,256,128]{2,1,0:T(8,128)S(1)} %get-tuple-element.18.scale_ref, bf16[2048,3584]{1,0:T(8,128)(2,1)S(1)} %copy-done.1), custom_call_target="tpu_custom_call" | custom-call | flops 4294967296 | bytes 8388608 | tf_op jit(solution)/shard_map/row_mass/pallas_call | solution.py:193
  27.0 5.2 %copy-done.2 = bf16[2048,3584]{1,0:T(8,128)(2,1)S(1)} copy-done((bf16[2048,3584]{1,0:T(8,128)(2,1)S(1)}, bf16[2048,3584]{1,0:T(8,128)(2,1)}, u32[]{:S(2)}) %copy-start.2) | copy-done | bytes 14680088
  34.2 6.3 %rows_times.3 = (f32[1056,256]{1,0:T(8,128)S(1)}, f32[4,256,256]{2,1,0:T(8,128)S(1)}) custom-call(s32[8]{0:T(128)S(1)} %stack.36.order_ref.rows_ref, bf16[2048,3584]{1,0:T(8,128)(2,1)S(1)} %copy-done.2, bf16[3584,512]{1,0:T(8,128)(2,1)S(1)} %copy-done.5, f32[32,256]{1,0:T(8,128)S(1)} %reshape_reshape.3.refs_0_), custom_call_target="tpu_custom_call" | custom-call | flops 3758096384 | bytes 16515072 | tf_op jit(solution)/shard_map/rows_times/pallas_call | solution.py:339
  46.2 5.3 %collective-permute-done.6 = bf16[2,256,256]{2,1,0:T(8,128)(2,1)S(1)} collective-permute-done((bf16[2,256,256]{2,1,0:T(8,128)(2,1)S(1)}, bf16[2,256,256]{2,1,0:T(8,128)(2,1)S(1)}, u32[]{:S(2)}, u32[]{:S(2)}) %collective-permute-start.6) | collective-permute-done | bytes 262176 | tf_op jit(solution)/shard_map/ppermute | solution.py:23
  71.6 6.3 %collective-permute-done.2 = bf16[320,256]{1,0:T(8,128)(2,1)S(1)} collective-permute-done((bf16[320,256]{1,0:T(8,128)(2,1)S(1)}, bf16[320,256]{1,0:T(8,128)(2,1)S(1)}, u32[]{:S(2)}, u32[]{:S(2)}) %collective-permute-start.2) | collective-permute-done | bytes 163872 | tf_op jit(solution)/shard_map/ppermute | solution.py:23
  78.0 11.4 %collective-permute-done.21 = bf16[1,256,256]{2,1,0:T(8,128)(2,1)S(1)} collective-permute-done((bf16[1,256,256]{2,1,0:T(8,128)(2,1)S(1)}, bf16[1,256,256]{2,1,0:T(8,128)(2,1)S(1)}, u32[]{:S(2)}, u32[]{:S(2)}) %collective-permute-start.21) | collective-permute-done | bytes 131104 | tf_op jit(solution)/shard_map/ppermute | solution.py:23
  98.9 5.2 %copy-done.3 = bf16[2048,3584]{1,0:T(8,128)(2,1)S(1)} copy-done((bf16[2048,3584]{1,0:T(8,128)(2,1)S(1)}, bf16[2048,3584]{1,0:T(8,128)(2,1)}, u32[]{:S(2)}) %copy-start.3) | copy-done | bytes 14680088
  104.1 5.8 %cols_times_joined.2 = (bf16[2,256,896]{2,1,0:T(8,128)(2,1)S(1)}, f32[2,256,896]{2,1,0:T(8,128)S(1)}) custom-call(s32[4]{0:T(128)S(1)} %pad_add_fusion.cols_ref, s32[8]{0:T(128)S(1)} %stack.36.order_ref.rows_ref, bf16[2048,3584]{1,0:T(8,128)(2,1)S(1)} %copy-done.3, f32[1,2048]{1,0:T(1,128)S(1)} %bitcast.76, ...), custom_call_target="tpu_custom_call" | custom-call | flops 3758096384 | bytes 16515072 | tf_op jit(solution)/shard_map/cols_times_joined/pallas_call | solution.py:339
  111.5 6.0 %cols_times_joined.3 = (bf16[2,256,896]{2,1,0:T(8,128)(2,1)S(1)}, f32[2,256,896]{2,1,0:T(8,128)S(1)}) custom-call(s32[4]{0:T(128)S(1)} %pad_add_fusion.cols_ref, s32[8]{0:T(128)S(1)} %stack.36.order_ref.rows_ref, bf16[2048,3584]{1,0:T(8,128)(2,1)S(1)} %copy-done.3, f32[1,2048]{1,0:T(1,128)S(1)} %bitcast.77, ...), custom_call_target="tpu_custom_call" | custom-call | flops 3758096384 | bytes 16515072 | tf_op jit(solution)/shard_map/cols_times_joined/pallas_call | solution.py:339
  118.0 5.3 %collective-permute-done.11 = bf16[2,256,896]{2,1,0:T(8,128)(2,1)S(1)} collective-permute-done((bf16[2,256,896]{2,1,0:T(8,128)(2,1)S(1)}, bf16[2,256,896]{2,1,0:T(8,128)(2,1)S(1)}, u32[]{:S(2)}, u32[]{:S(2)}) %collective-permute-start.11) | collective-permute-done | bytes 917536 | tf_op jit(solution)/shard_map/ppermute | solution.py:23
  125.1 13.1 %collective-permute-done.24 = bf16[2,256,896]{2,1,0:T(8,128)(2,1)S(1)} collective-permute-done((bf16[2,256,896]{2,1,0:T(8,128)(2,1)S(1)}, bf16[2,256,896]{2,1,0:T(8,128)(2,1)S(1)}, u32[]{:S(2)}, u32[]{:S(2)}) %collective-permute-start.24) | collective-permute-done | bytes 917536 | tf_op jit(solution)/shard_map/ppermute | solution.py:23
  140.6 6.2 %collective-permute-done.25 = bf16[1,256,896]{2,1,0:T(8,128)(2,1)S(1)} collective-permute-done((bf16[1,256,896]{2,1,0:T(8,128)(2,1)S(1)}, bf16[1,256,896]{2,1,0:T(8,128)(2,1)S(1)}, u32[]{:S(2)}, u32[]{:S(2)}) %collective-permute-start.25) | collective-permute-done | bytes 458784 | tf_op jit(solution)/shard_map/ppermute | solution.py:23
  154.2 8.2 %collective-permute-done.26 = bf16[1,256,896]{2,1,0:T(8,128)(2,1)S(1)} collective-permute-done((bf16[1,256,896]{2,1,0:T(8,128)(2,1)S(1)}, bf16[1,256,896]{2,1,0:T(8,128)(2,1)S(1)}, u32[]{:S(2)}, u32[]{:S(2)}) %collective-permute-start.26) | collective-permute-done | bytes 458784 | tf_op jit(solution)/shard_map/ppermute | solution.py:23
  166.1 5.7 %rows_times_joined.2 = (bf16[4,256,256]{2,1,0:T(8,128)(2,1)S(1)}, f32[4,256,256]{2,1,0:T(8,128)S(1)}) custom-call(s32[8]{0:T(128)S(1)} %stack.36.order_ref.rows_ref, s32[4]{0:T(128)S(1)} %pad_add_fusion.cols_ref, bf16[2048,3584]{1,0:T(8,128)(2,1)S(1)} %copy-done.3, bf16[2,256,896]{2,1,0:T(8,128)(2,1)S(1)} %pad_maximum_fusion.1.first_ref, ...), custom_call_target="tpu_custom_call" | custom-call | flops 3758096384 | bytes 16515072 | tf_op jit(solution)/shard_map/rows_times_joined/pallas_call | solution.py:339
  175.9 5.7 %rows_times_joined.3 = (bf16[4,256,256]{2,1,0:T(8,128)(2,1)S(1)}, f32[4,256,256]{2,1,0:T(8,128)S(1)}) custom-call(s32[8]{0:T(128)S(1)} %stack.36.order_ref.rows_ref, s32[4]{0:T(128)S(1)} %pad_add_fusion.cols_ref, bf16[2048,3584]{1,0:T(8,128)(2,1)S(1)} %copy-done.3, bf16[2,256,896]{2,1,0:T(8,128)(2,1)S(1)} %pad_maximum_fusion.2.first_ref, ...), custom_call_target="tpu_custom_call" | custom-call | flops 3758096384 | bytes 16515072 | tf_op jit(solution)/shard_map/rows_times_joined/pallas_call | solution.py:339
  187.5 6.8 %collective-permute-done.16 = bf16[2,256,256]{2,1,0:T(8,128)(2,1)S(1)} collective-permute-done((bf16[2,256,256]{2,1,0:T(8,128)(2,1)S(1)}, bf16[2,256,256]{2,1,0:T(8,128)(2,1)S(1)}, u32[]{:S(2)}, u32[]{:S(2)}) %collective-permute-start.16) | collective-permute-done | bytes 262176 | tf_op jit(solution)/shard_map/ppermute | solution.py:23
  218.3 5.1 %collective-permute-done.32 = bf16[2,256,256]{2,1,0:T(8,128)(2,1)S(1)} collective-permute-done((bf16[2,256,256]{2,1,0:T(8,128)(2,1)S(1)}, bf16[2,256,256]{2,1,0:T(8,128)(2,1)S(1)}, u32[]{:S(2)}, u32[]{:S(2)}) %collective-permute-start.32) | collective-permute-done | bytes 262176 | tf_op jit(solution)/shard_map/ppermute | solution.py:23
  233.4 7.7 %collective-permute-done.34 = f32[256,512]{1,0:T(8,128)S(1)} collective-permute-done((f32[256,512]{1,0:T(8,128)S(1)}, f32[256,512]{1,0:T(8,128)S(1)}, u32[]{:S(2)}, u32[]{:S(2)}) %collective-permute-start.34) | collective-permute-done | bytes 524320 | tf_op jit(solution)/shard_map/ppermute | solution.py:23
  242.2 8.2 %collective-permute-done.35 = f32[256,512]{1,0:T(8,128)S(1)} collective-permute-done((f32[256,512]{1,0:T(8,128)S(1)}, f32[256,512]{1,0:T(8,128)S(1)}, u32[]{:S(2)}, u32[]{:S(2)}) %collective-permute-start.35) | collective-permute-done | bytes 524320 | tf_op jit(solution)/shard_map/ppermute | solution.py:23
  253.9 21.3 %inverse_factor.1 = f32[512,512]{1,0:T(8,128)S(1)} custom-call(f32[512,512]{1,0:T(8,128)S(1)} %pad_maximum_fusion.gram_ref), custom_call_target="tpu_custom_call" | custom-call | flops 5368709120 | bytes 2097152 | tf_op jit(solution)/shard_map/inverse_factor/pallas_call | solution.py:290
  289.9 15.3 %collective-permute-done.37 = bf16[2,128,3584]{2,1,0:T(8,128)(2,1)S(1)} collective-permute-done((bf16[2,128,3584]{2,1,0:T(8,128)(2,1)S(1)}, bf16[2,128,3584]{2,1,0:T(8,128)(2,1)S(1)}, u32[]{:S(2)}, u32[]{:S(2)}) %collective-permute-start.37) | collective-permute-done | bytes 1835040 | tf_op jit(solution)/shard_map/ppermute | solution.py:23
  309.2 11.2 %collective-permute-done.38 = bf16[1,128,3584]{2,1,0:T(8,128)(2,1)} collective-permute-done((bf16[1,128,3584]{2,1,0:T(8,128)(2,1)}, bf16[1,128,3584]{2,1,0:T(8,128)(2,1)}, u32[]{:S(2)}, u32[]{:S(2)}) %collective-permute-start.38) | collective-permute-done | bytes 917536 | tf_op jit(solution)/shard_map/ppermute | solution.py:23
  (169 shorter events, 131.0 us)
Async XLA Ops:
  14.3 26.3 %collective-permute-start.5 = (f32[4,256,256]{2,1,0:T(8,128)S(1)}, f32[4,256,256]{2,1,0:T(8,128)}, u32[]{:S(2)}, u32[]{:S(2)}) collective-permute-start(f32[4,256,256]{2,1,0:T(8,128)S(1)} %get-tuple-element.21), channel_id=1, source_target_pairs={{0,1},{1,0},{2,3},{3,2},{4,5},{5,4},{6,7},{7,6},{8,9},{9,8},{10,11... | collective-permute-start | bytes 3145736 | tf_op jit(solution)/shard_map/ppermute | solution.py:23
  41.7 9.8 %collective-permute-start.6 = (bf16[2,256,256]{2,1,0:T(8,128)(2,1)S(1)}, bf16[2,256,256]{2,1,0:T(8,128)(2,1)S(1)}, u32[]{:S(2)}, u32[]{:S(2)}) collective-permute-start(bf16[2,256,256]{2,1,0:T(8,128)(2,1)S(1)} %fusion.19), channel_id=1, source_target_pairs={{0,2},{1,5},{2,0},{3,7},{4,6},{5,1},{6,4},{7,3},{8,10},{9,13},{10,... | collective-permute-start | bytes 786440 | tf_op jit(solution)/shard_map/ppermute | solution.py:23
  45.0 15.6 %collective-permute-start.1 = (bf16[576,256]{1,0:T(8,128)(2,1)S(1)}, bf16[576,256]{1,0:T(8,128)(2,1)S(1)}, u32[]{:S(2)}, u32[]{:S(2)}) collective-permute-start(bf16[576,256]{1,0:T(8,128)(2,1)S(1)} %pad_maximum_fusion.9), channel_id=1, source_target_pairs={{0,2},{1,5},{2,0},{3,7},{4,6},{5,1},{6,4},{7,3},{8,10},{9,13},{10,... | collective-permute-start | bytes 884744 | tf_op jit(solution)/shard_map/ppermute | solution.py:23
  65.0 12.8 %collective-permute-start.2 = (bf16[320,256]{1,0:T(8,128)(2,1)S(1)}, bf16[320,256]{1,0:T(8,128)(2,1)S(1)}, u32[]{:S(2)}, u32[]{:S(2)}) collective-permute-start(bf16[320,256]{1,0:T(8,128)(2,1)S(1)} %pad_maximum_fusion.14), channel_id=1, source_target_pairs={{0,4},{1,3},{2,6},{3,1},{4,0},{5,7},{6,2},{7,5},{8,12},{9,11},{10,... | collective-permute-start | bytes 491528 | tf_op jit(solution)/shard_map/ppermute | solution.py:23
  69.0 20.6 %collective-permute-start.9 = (bf16[2,256,256]{2,1,0:T(8,128)(2,1)S(1)}, bf16[2,256,256]{2,1,0:T(8,128)(2,1)S(1)}, u32[]{:S(2)}, u32[]{:S(2)}) collective-permute-start(bf16[2,256,256]{2,1,0:T(8,128)(2,1)S(1)} %pad_maximum_fusion.10), channel_id=1, source_target_pairs={{0,2},{1,5},{2,0},{3,7},{4,6},{5,1},{6,4},{7,3},{8,10},{9,13},{10,... | collective-permute-start | bytes 786440 | tf_op jit(solution)/shard_map/ppermute | solution.py:23
  77.9 11.5 %collective-permute-start.21 = (bf16[1,256,256]{2,1,0:T(8,128)(2,1)S(1)}, bf16[1,256,256]{2,1,0:T(8,128)(2,1)S(1)}, u32[]{:S(2)}, u32[]{:S(2)}) collective-permute-start(bf16[1,256,256]{2,1,0:T(8,128)(2,1)S(1)} %fusion.38), channel_id=1, source_target_pairs={{0,4},{1,3},{2,6},{3,1},{4,0},{5,7},{6,2},{7,5},{8,12},{9,11},{10,... | collective-permute-start | bytes 393224 | tf_op jit(solution)/shard_map/ppermute | solution.py:23
  89.6 9.3 %collective-permute-start.10 = (bf16[4,256,256]{2,1,0:T(8,128)(2,1)S(1)}, bf16[4,256,256]{2,1,0:T(8,128)(2,1)S(1)}, u32[]{:S(2)}, u32[]{:S(2)}) collective-permute-start(bf16[4,256,256]{2,1,0:T(8,128)(2,1)S(1)} %pad_maximum_fusion.3.first_ref), channel_id=1, source_target_pairs={{0,1},{1,0},{2,3},{3,2},{4,5},{5,4},{6,7},{7,6},{8,9},{9,8},{10,11... | collective-permute-start | bytes 1572872 | tf_op jit(solution)/shard_map/ppermute | solution.py:23
  95.9 15.5 %collective-permute-start.23 = (bf16[4,256,256]{2,1,0:T(8,128)(2,1)S(1)}, bf16[4,256,256]{2,1,0:T(8,128)(2,1)S(1)}, u32[]{:S(2)}, u32[]{:S(2)}) collective-permute-start(bf16[4,256,256]{2,1,0:T(8,128)(2,1)S(1)} %pad_maximum_fusion.5.first_ref), channel_id=1, source_target_pairs={{0,1},{1,0},{2,3},{3,2},{4,5},{5,4},{6,7},{7,6},{8,9},{9,8},{10,11... | collective-permute-start | bytes 1572872 | tf_op jit(solution)/shard_map/ppermute | solution.py:23
  109.9 13.5 %collective-permute-start.11 = (bf16[2,256,896]{2,1,0:T(8,128)(2,1)S(1)}, bf16[2,256,896]{2,1,0:T(8,128)(2,1)S(1)}, u32[]{:S(2)}, u32[]{:S(2)}) collective-permute-start(bf16[2,256,896]{2,1,0:T(8,128)(2,1)S(1)} %get-tuple-element.23), channel_id=1, source_target_pairs={{0,8},{1,17},{2,10},{3,19},{4,12},{5,21},{6,14},{7,23},{8,0},{9,25... | collective-permute-start | bytes 2752520 | tf_op jit(solution)/shard_map/ppermute | solution.py:23
  117.4 20.7 %collective-permute-start.24 = (bf16[2,256,896]{2,1,0:T(8,128)(2,1)S(1)}, bf16[2,256,896]{2,1,0:T(8,128)(2,1)S(1)}, u32[]{:S(2)}, u32[]{:S(2)}) collective-permute-start(bf16[2,256,896]{2,1,0:T(8,128)(2,1)S(1)} %get-tuple-element.27), channel_id=1, source_target_pairs={{0,8},{1,17},{2,10},{3,19},{4,12},{5,21},{6,14},{7,23},{8,0},{9,25... | collective-permute-start | bytes 2752520 | tf_op jit(solution)/shard_map/ppermute | solution.py:23
  123.5 16.4 %collective-permute-start.12 = (bf16[1,256,896]{2,1,0:T(8,128)(2,1)S(1)}, bf16[1,256,896]{2,1,0:T(8,128)(2,1)S(1)}, u32[]{:S(2)}, u32[]{:S(2)}) collective-permute-start(bf16[1,256,896]{2,1,0:T(8,128)(2,1)S(1)} %add_convert_fusion.3), channel_id=1, source_target_pairs={{0,16},{1,9},{2,18},{3,11},{4,20},{5,13},{6,22},{7,15},{8,24},{9,1... | collective-permute-start | bytes 1376264 | tf_op jit(solution)/shard_map/ppermute | solution.py:23
  138.3 8.5 %collective-permute-start.25 = (bf16[1,256,896]{2,1,0:T(8,128)(2,1)S(1)}, bf16[1,256,896]{2,1,0:T(8,128)(2,1)S(1)}, u32[]{:S(2)}, u32[]{:S(2)}) collective-permute-start(bf16[1,256,896]{2,1,0:T(8,128)(2,1)S(1)} %add_convert_fusion.1), channel_id=1, source_target_pairs={{0,16},{1,9},{2,18},{3,11},{4,20},{5,13},{6,22},{7,15},{8,24},{9,1... | collective-permute-start | bytes 1376264 | tf_op jit(solution)/shard_map/ppermute | solution.py:23
  140.0 12.5 %collective-permute-start.13 = (bf16[1,256,896]{2,1,0:T(8,128)(2,1)S(1)}, bf16[1,256,896]{2,1,0:T(8,128)(2,1)S(1)}, u32[]{:S(2)}, u32[]{:S(2)}) collective-permute-start(bf16[1,256,896]{2,1,0:T(8,128)(2,1)S(1)} %add_convert_fusion.2), channel_id=1, source_target_pairs={{0,16},{1,9},{2,18},{3,11},{4,20},{5,13},{6,22},{7,15},{8,24},{9,1... | collective-permute-start | bytes 1376264 | tf_op jit(solution)/shard_map/ppermute | solution.py:23
  147.0 15.4 %collective-permute-start.26 = (bf16[1,256,896]{2,1,0:T(8,128)(2,1)S(1)}, bf16[1,256,896]{2,1,0:T(8,128)(2,1)S(1)}, u32[]{:S(2)}, u32[]{:S(2)}) collective-permute-start(bf16[1,256,896]{2,1,0:T(8,128)(2,1)S(1)} %add_convert_fusion), channel_id=1, source_target_pairs={{0,16},{1,9},{2,18},{3,11},{4,20},{5,13},{6,22},{7,15},{8,24},{9,1... | collective-permute-start | bytes 1376264 | tf_op jit(solution)/shard_map/ppermute | solution.py:23
  152.7 13.5 %collective-permute-start.14 = (bf16[2,256,896]{2,1,0:T(8,128)(2,1)S(1)}, bf16[2,256,896]{2,1,0:T(8,128)(2,1)S(1)}, u32[]{:S(2)}, u32[]{:S(2)}) collective-permute-start(bf16[2,256,896]{2,1,0:T(8,128)(2,1)S(1)} %pad_maximum_fusion.1.first_ref), channel_id=1, source_target_pairs={{0,8},{1,17},{2,10},{3,19},{4,12},{5,21},{6,14},{7,23},{8,0},{9,25... | collective-permute-start | bytes 2752520 | tf_op jit(solution)/shard_map/ppermute | solution.py:23
  162.5 13.5 %collective-permute-start.27 = (bf16[2,256,896]{2,1,0:T(8,128)(2,1)S(1)}, bf16[2,256,896]{2,1,0:T(8,128)(2,1)S(1)}, u32[]{:S(2)}, u32[]{:S(2)}) collective-permute-start(bf16[2,256,896]{2,1,0:T(8,128)(2,1)S(1)} %pad_maximum_fusion.2.first_ref), channel_id=1, source_target_pairs={{0,8},{1,17},{2,10},{3,19},{4,12},{5,21},{6,14},{7,23},{8,0},{9,25... | collective-permute-start | bytes 2752520 | tf_op jit(solution)/shard_map/ppermute | solution.py:23
  171.8 10.1 %collective-permute-start.15 = (bf16[4,256,256]{2,1,0:T(8,128)(2,1)S(1)}, bf16[4,256,256]{2,1,0:T(8,128)(2,1)S(1)}, u32[]{:S(2)}, u32[]{:S(2)}) collective-permute-start(bf16[4,256,256]{2,1,0:T(8,128)(2,1)S(1)} %get-tuple-element.25), channel_id=1, source_target_pairs={{0,1},{1,0},{2,3},{3,2},{4,5},{5,4},{6,7},{7,6},{8,9},{9,8},{10,11... | collective-permute-start | bytes 1572872 | tf_op jit(solution)/shard_map/ppermute | solution.py:23
  182.0 12.3 %collective-permute-start.16 = (bf16[2,256,256]{2,1,0:T(8,128)(2,1)S(1)}, bf16[2,256,256]{2,1,0:T(8,128)(2,1)S(1)}, u32[]{:S(2)}, u32[]{:S(2)}) collective-permute-start(bf16[2,256,256]{2,1,0:T(8,128)(2,1)S(1)} %add_convert_fusion.5), channel_id=1, source_target_pairs={{0,2},{1,5},{2,0},{3,7},{4,6},{5,1},{6,4},{7,3},{8,10},{9,13},{10,... | collective-permute-start | bytes 786440 | tf_op jit(solution)/shard_map/ppermute | solution.py:23
  185.7 12.3 %collective-permute-start.29 = (bf16[2,256,256]{2,1,0:T(8,128)(2,1)S(1)}, bf16[2,256,256]{2,1,0:T(8,128)(2,1)S(1)}, u32[]{:S(2)}, u32[]{:S(2)}) collective-permute-start(bf16[2,256,256]{2,1,0:T(8,128)(2,1)S(1)} %add_convert_fusion.4), channel_id=1, source_target_pairs={{0,2},{1,5},{2,0},{3,7},{4,6},{5,1},{6,4},{7,3},{8,10},{9,13},{10,... | collective-permute-start | bytes 786440 | tf_op jit(solution)/shard_map/ppermute | solution.py:23
  211.0 12.4 %collective-permute-start.32 = (bf16[2,256,256]{2,1,0:T(8,128)(2,1)S(1)}, bf16[2,256,256]{2,1,0:T(8,128)(2,1)S(1)}, u32[]{:S(2)}, u32[]{:S(2)}) collective-permute-start(bf16[2,256,256]{2,1,0:T(8,128)(2,1)S(1)} %pad_maximum_fusion.13), channel_id=1, source_target_pairs={{0,2},{1,5},{2,0},{3,7},{4,6},{5,1},{6,4},{7,3},{8,10},{9,13},{10,... | collective-permute-start | bytes 786440 | tf_op jit(solution)/shard_map/ppermute | solution.py:23
  231.9 9.2 %collective-permute-start.34 = (f32[256,512]{1,0:T(8,128)S(1)}, f32[256,512]{1,0:T(8,128)S(1)}, u32[]{:S(2)}, u32[]{:S(2)}) collective-permute-start(f32[256,512]{1,0:T(8,128)S(1)} %convolution_add_fusion.2), channel_id=1, source_target_pairs={{0,8},{1,17},{2,10},{3,19},{4,12},{5,21},{6,14},{7,23},{8,0},{9,25... | collective-permute-start | bytes 1572872 | tf_op jit(solution)/shard_map/ppermute | solution.py:23
  241.2 9.2 %collective-permute-start.35 = (f32[256,512]{1,0:T(8,128)S(1)}, f32[256,512]{1,0:T(8,128)S(1)}, u32[]{:S(2)}, u32[]{:S(2)}) collective-permute-start(f32[256,512]{1,0:T(8,128)S(1)} %add.227), channel_id=1, source_target_pairs={{0,16},{1,9},{2,18},{3,11},{4,20},{5,13},{6,22},{7,15},{8,24},{9,1... | collective-permute-start | bytes 1572872 | tf_op jit(solution)/shard_map/ppermute | solution.py:23
  281.9 23.3 %collective-permute-start.37 = (bf16[2,128,3584]{2,1,0:T(8,128)(2,1)S(1)}, bf16[2,128,3584]{2,1,0:T(8,128)(2,1)S(1)}, u32[]{:S(2)}, u32[]{:S(2)}) collective-permute-start(bf16[2,128,3584]{2,1,0:T(8,128)(2,1)S(1)} %bitcast.75), channel_id=1, source_target_pairs={{0,8},{1,17},{2,10},{3,19},{4,12},{5,21},{6,14},{7,23},{8,0},{9,25... | collective-permute-start | bytes 5505032 | tf_op jit(solution)/shard_map/ppermute | solution.py:23
  306.7 13.7 %collective-permute-start.38 = (bf16[1,128,3584]{2,1,0:T(8,128)(2,1)}, bf16[1,128,3584]{2,1,0:T(8,128)(2,1)}, u32[]{:S(2)}, u32[]{:S(2)}) collective-permute-start(bf16[1,128,3584]{2,1,0:T(8,128)(2,1)} %fusion.6), channel_id=1, source_target_pairs={{0,16},{1,9},{2,18},{3,11},{4,20},{5,13},{6,22},{7,15},{8,24},{9,1... | collective-permute-start | bytes 2752520 | tf_op jit(solution)/shard_map/ppermute | solution.py:23
  (37 other events, 246.8 us)

commit v6 on v5

--- a/solution.py
+++ b/solution.py
@@ -72,10 +72,13 @@
         for t in range(len(self.orders[0])):
             came = self.step(t, send)
             if rider is not None:
-                height = rider.shape[0]
-                *parts, blocks = jnp.split(came, [height] if t == 0 else [height, 2 * height])
-                rider = rider + sum(part.astype(F32) for part in parts)
-                came = blocks.reshape(terms[0].shape)
+                if t == 0:
+                    rider = rider + self.step(t, rider)
+                else:
+                    height = rider.shape[0]
+                    *parts, blocks = jnp.split(came, [height, 2 * height])
+                    rider = rider + sum(part.astype(F32) for part in parts)
+                    came = blocks.reshape(terms[0].shape)
             terms.append(came)
             half = terms[0].shape[0] // 2
             add = lambda part: sum(term[part].astype(F32) for term in terms)
@@ -124,7 +127,7 @@
     return value
 
 
-def token_gram_kernel(valid_ref, grads_ref, after_ref, weight_ref, gram_ref, scale_ref):
+def token_gram_kernel(valid_ref, grads_ref, after_ref, gram_ref, scale_ref):
     seq = pl.program_id(0)
     length = grads_ref.shape[1]
     tokens = lax.broadcasted_iota(jnp.int32, (length, 1), 0)
@@ -146,7 +149,7 @@
     scale_ref[0] = jnp.broadcast_to(scale, (length, 128))
 
 
-def row_mass_kernel(acts_ref, gram_ref, scale_ref, weight_ref, mass_ref):
+def row_mass_kernel(acts_ref, gram_ref, scale_ref, mass_ref):
     length = acts_ref.shape[1]
     total = jnp.zeros((1, acts_ref.shape[2]), F32)
     for seq in range(acts_ref.shape[0]):
@@ -157,7 +160,7 @@
     mass_ref[...] = total
 
 
-def local_mass(activations, out_grads, valid_len, after, weight):
+def local_mass(activations, out_grads, valid_len, after):
     seqs, length, width = activations.shape
     cols = out_grads.shape[2]
     whole = lambda seq, valid: (seq, 0, 0)
@@ -173,7 +176,6 @@
             in_specs=[
                 pl.BlockSpec((1, length, cols), whole),
                 pl.BlockSpec(memory_space=pl.ANY),
-                pl.BlockSpec(memory_space=pltpu.VMEM),
             ],
             out_specs=(
                 pl.BlockSpec((1, 2 * length, length), whole),
@@ -187,7 +189,7 @@
             transcendentals=0,
         ),
         name="token_gram",
-    )(valid_len, out_grads, after, weight)
+    )(valid_len, out_grads, after)
     tile = math.gcd(width, 1024)
     fixed = lambda i: (0, 0, 0)
     mass = pl.pallas_call(
@@ -198,7 +200,6 @@
             pl.BlockSpec((seqs, length, tile), lambda i: (0, 0, i)),
             pl.BlockSpec((seqs, 2 * length, length), fixed),
             pl.BlockSpec((seqs, length, 128), fixed),
-            pl.BlockSpec(memory_space=pltpu.VMEM),
         ],
         out_specs=pl.BlockSpec((1, tile), lambda i: (0, i)),
         compiler_params=pltpu.CompilerParams(vmem_limit_bytes=LIMIT),
@@ -208,7 +209,7 @@
             transcendentals=0,
         ),
         name="row_mass",
-    )(activations, gram, scale, weight)
+    )(activations, gram, scale)
     return mass.reshape(width)
 
 
@@ -312,20 +313,14 @@
 
 
 def gather_rows(order_ref, sum_ref, send_ref, keep_ref, turned):
-    half, height = keep_ref.shape[:2]
-    above = send_ref.shape[0] - half * height
+    half = send_ref.shape[0]
     block = sum_ref.shape[0] // (2 * half)
     for i in range(2 * half):
         here = pl.ds(pl.multiple_of(order_ref[i] * block, block), block)
         value = sum_ref[here, :]
         value = value.T if turned else value
-        if i >= half:
-            keep_ref[i - half] = value
-        elif len(send_ref.shape) == 3:
-            send_ref[i] = value.astype(send_ref.dtype)
-        else:
-            start = above + i * height
-            send_ref[start : start + height] = value
+        target = send_ref if i < half else keep_ref
+        target[i % half] = value.astype(target.dtype)
 
 
 def two_halves(size, shape, send_type):
@@ -352,8 +347,9 @@
     )(*indices, weight, *arrays)
 
 
-def rows_plain_kernel(part, width, turned, order_ref, weight_ref, right_ref, *refs):
-    *rider_ref, send_ref, keep_ref, sum_ref = refs
+def rows_plain_kernel(
+    part, width, turned, order_ref, weight_ref, right_ref, send_ref, keep_ref, sum_ref
+):
     depth = weight_ref.shape[1]
     chunk = 512 if depth % 512 == 0 else depth
 
@@ -367,18 +363,13 @@
     def _(i):
         sum_ref[...] += term(pl.multiple_of(i * chunk, chunk))
 
-    if rider_ref:
-        send_ref[: rider_ref[0].shape[0]] = rider_ref[0][...]
     gather_rows(order_ref, sum_ref, send_ref, keep_ref, turned)
 
 
-def rows_times(weight, right, part, width, rows, turned, rider=()):
+def rows_times(weight, right, part, width, rows, turned):
     height = weight.shape[0]
     block = height // rows.size
     shapes = two_halves(rows.size, (width, block) if turned else (block, width), F32)
-    for load in rider:
-        dims = (load.shape[0] + rows.size // 2 * width, block)
-        shapes = (jax.ShapeDtypeStruct(dims, F32), shapes[1])
     return product_call(
         functools.partial(rows_plain_kernel, part, width, turned),
         "rows_times",
@@ -387,7 +378,7 @@
         weight,
         width,
         (rows.sending_first(),),
-        (right, *rider),
+        (right,),
     )
 
 
@@ -535,10 +526,9 @@
     own_rows = rows_here // col_count
     over_col, over_row = Halving("col"), Halving("row")
 
-    raw = rows_times(weight, sketch, 0, half, over_col, True)
-    mass = local_mass(activations, out_grads, valid_len, raw[1], weight)
+    raw, later = (rows_times(weight, sketch, part, half, over_col, True) for part in range(2))
+    mass = local_mass(activations, out_grads, valid_len, later[1])
     mass = mass.reshape(-1, own_rows)
-    later = rows_times(weight, sketch, 1, half, over_col, True, (mass,))
     raw = over_col.scatter_sum(*raw)
     later, fisher = over_col.scatter_sum(*later, mass)
     fisher = sum_everywhere(fisher, col=False).reshape(width)

time: 324 us -> 325 us (level)
  waiting for transfers between devices: 153 us -> 163 us
  local copies, waits for them, and re-layouts: 24.9 us -> 16.9 us
  starting transfers between devices: 46.5 us -> 42.1 us
    ppermute x39 -> x40, waiting for transfers between devices: 153 us -> 163 us  [swap(): return lax.ppermute(block, AXES, pairs)]
    unnamed x45 -> x39, local copies, waits for them, and re-layouts: 24.2 us -> 16.2 us
    ppermute x39 -> x40, starting transfers between devices: 46.5 us -> 42.1 us  [swap(): return lax.ppermute(block, AXES, pairs)]
  transfers between devices with their start and end apart: 39 -> 40, of which waited for: 29 -> 30; matrix products, arithmetic and copies ran while one was open for 3% -> 4% of each run, Pallas kernels for 14% -> 14%
where the time goes in v6:
time: 325 us
  waiting for transfers between devices  163 us (50%)
  Pallas kernels  79.2 us (24%)
  starting transfers between devices  42.1 us (13%)
  local copies, waits for them, and re-layouts  16.9 us (5%)
  other arithmetic  14.8 us (5%)
  matrix products  7.31 us (2%)
    ppermute x40, waiting for transfers between devices, swap(): return lax.ppermute(block, AXES, pairs)  163 us
    ppermute x40, starting transfers between devices, swap(): return lax.ppermute(block, AXES, pairs)  42.1 us
    pallas_call x6, Pallas kernels, product_call(): pl.pallas_call(kernel, out_shape=out_shape, in_specs=[smem] * len(indices...  37.3 us
    pallas_call x1, Pallas kernels, inverse_factor(): pl.pallas_call(inverse_factor_kernel, out_shape=jax.ShapeDtypeStruct((siz...  21.3 us
    unnamed x39, local copies, waits for them, and re-layouts  16.2 us
    pallas_call x2, Pallas kernels, rank_times(): pl.pallas_call(rank_kernel, out_shape=jax.ShapeDtypeStruct((basis.shape[0...  9.91 us
    pallas_call x1, Pallas kernels, local_mass(): pl.pallas_call(row_mass_kernel, out_shape=jax.ShapeDtypeStruct((1, width)...  7.31 us
    dot_general x8, matrix products, dot(): lax.dot_general(left, right, (dims, ((), ())), preferred_element_type=F32)  7.31 us
  transfers between devices with their start and end apart: 40, of which 30 were waited for; matrix products, arithmetic and copies ran while one was open for 4% of the time, Pallas kernels for 14%

profile of v6, /device:TPU:0, one launch (start us, length us, event | category | flops | bytes accessed | tf_op | source)
XLA Modules:
  0.0 324.8 jit_solution(1985222784214524287)
XLA Ops:
  0.7 5.2 %copy-done = bf16[2048,3584]{1,0:T(8,128)(2,1)S(1)} copy-done((bf16[2048,3584]{1,0:T(8,128)(2,1)S(1)}, bf16[2048,3584]{1,0:T(8,128)(2,1)}, u32[]{:S(2)}) %copy-start) | copy-done | bytes 14680088
  8.0 7.1 %rows_times.3 = (f32[4,256,256]{2,1,0:T(8,128)}, f32[4,256,256]{2,1,0:T(8,128)S(1)}) custom-call(s32[8]{0:T(128)S(1)} %stack.36.order_ref.rows_ref, bf16[2048,3584]{1,0:T(8,128)(2,1)S(1)} %copy-done, bf16[3584,512]{1,0:T(8,128)(2,1)S(1)} %copy-done.2), custom_call_target="tpu_custom_call" | custom-call | flops 3758096384 | bytes 16515072 | tf_op jit(solution)/shard_map/rows_times/pallas_call | solution.py:334
  15.5 7.1 %rows_times.2 = (f32[4,256,256]{2,1,0:T(8,128)}, f32[4,256,256]{2,1,0:T(8,128)S(1)}) custom-call(s32[8]{0:T(128)S(1)} %stack.36.order_ref.rows_ref, bf16[2048,3584]{1,0:T(8,128)(2,1)S(1)} %copy-done, bf16[3584,512]{1,0:T(8,128)(2,1)S(1)} %copy-done.2), custom_call_target="tpu_custom_call" | custom-call | flops 3758096384 | bytes 16515072 | tf_op jit(solution)/shard_map/rows_times/pallas_call | solution.py:334
  25.3 7.3 %row_mass.1 = f32[1,8192]{1,0:T(1,128)S(1)} custom-call(bf16[2,256,8192]{2,1,0:T(8,128)(2,1)S(1)} %bitcast.72, bf16[2,512,256]{2,1,0:T(8,128)(2,1)S(1)} %get-tuple-element.17.gram_ref, f32[2,256,128]{2,1,0:T(8,128)S(1)} %get-tuple-element.18.scale_ref), custom_call_target="tpu_custom_call" | custom-call | flops 4294967296 | bytes 8388608 | tf_op jit(solution)/shard_map/row_mass/pallas_call | solution.py:195
  40.6 5.5 %collective-permute-done.7 = bf16[2,256,256]{2,1,0:T(8,128)(2,1)S(1)} collective-permute-done((bf16[2,256,256]{2,1,0:T(8,128)(2,1)S(1)}, bf16[2,256,256]{2,1,0:T(8,128)(2,1)S(1)}, u32[]{:S(2)}, u32[]{:S(2)}) %collective-permute-start.7) | collective-permute-done | bytes 262176 | tf_op jit(solution)/shard_map/ppermute | solution.py:23
  66.1 6.5 %collective-permute-done.3 = bf16[320,256]{1,0:T(8,128)(2,1)S(1)} collective-permute-done((bf16[320,256]{1,0:T(8,128)(2,1)S(1)}, bf16[320,256]{1,0:T(8,128)(2,1)S(1)}, u32[]{:S(2)}, u32[]{:S(2)}) %collective-permute-start.3) | collective-permute-done | bytes 163872 | tf_op jit(solution)/shard_map/ppermute | solution.py:23
  73.9 10.6 %collective-permute-done.22 = bf16[1,256,256]{2,1,0:T(8,128)(2,1)S(1)} collective-permute-done((bf16[1,256,256]{2,1,0:T(8,128)(2,1)S(1)}, bf16[1,256,256]{2,1,0:T(8,128)(2,1)S(1)}, u32[]{:S(2)}, u32[]{:S(2)}) %collective-permute-start.22) | collective-permute-done | bytes 131104 | tf_op jit(solution)/shard_map/ppermute | solution.py:23
  99.1 5.8 %cols_times_joined.2 = (bf16[2,256,896]{2,1,0:T(8,128)(2,1)S(1)}, f32[2,256,896]{2,1,0:T(8,128)S(1)}) custom-call(s32[4]{0:T(128)S(1)} %pad_add_fusion.cols_ref, s32[8]{0:T(128)S(1)} %stack.36.order_ref.rows_ref, bf16[2048,3584]{1,0:T(8,128)(2,1)S(1)} %copy-done.1, f32[1,2048]{1,0:T(1,128)S(1)} %bitcast.69, ...), custom_call_target="tpu_custom_call" | custom-call | flops 3758096384 | bytes 16515072 | tf_op jit(solution)/shard_map/cols_times_joined/pallas_call | solution.py:334
  106.0 6.0 %cols_times_joined.3 = (bf16[2,256,896]{2,1,0:T(8,128)(2,1)S(1)}, f32[2,256,896]{2,1,0:T(8,128)S(1)}) custom-call(s32[4]{0:T(128)S(1)} %pad_add_fusion.cols_ref, s32[8]{0:T(128)S(1)} %stack.36.order_ref.rows_ref, bf16[2048,3584]{1,0:T(8,128)(2,1)S(1)} %copy-done.1, f32[1,2048]{1,0:T(1,128)S(1)} %bitcast.70, ...), custom_call_target="tpu_custom_call" | custom-call | flops 3758096384 | bytes 16515072 | tf_op jit(solution)/shard_map/cols_times_joined/pallas_call | solution.py:334
  113.1 5.3 %collective-permute-done.12 = bf16[2,256,896]{2,1,0:T(8,128)(2,1)S(1)} collective-permute-done((bf16[2,256,896]{2,1,0:T(8,128)(2,1)S(1)}, bf16[2,256,896]{2,1,0:T(8,128)(2,1)S(1)}, u32[]{:S(2)}, u32[]{:S(2)}) %collective-permute-start.12) | collective-permute-done | bytes 917536 | tf_op jit(solution)/shard_map/ppermute | solution.py:23
  119.7 13.5 %collective-permute-done.25 = bf16[2,256,896]{2,1,0:T(8,128)(2,1)S(1)} collective-permute-done((bf16[2,256,896]{2,1,0:T(8,128)(2,1)S(1)}, bf16[2,256,896]{2,1,0:T(8,128)(2,1)S(1)}, u32[]{:S(2)}, u32[]{:S(2)}) %collective-permute-start.25) | collective-permute-done | bytes 917536 | tf_op jit(solution)/shard_map/ppermute | solution.py:23
  135.6 6.2 %collective-permute-done.26 = bf16[1,256,896]{2,1,0:T(8,128)(2,1)S(1)} collective-permute-done((bf16[1,256,896]{2,1,0:T(8,128)(2,1)S(1)}, bf16[1,256,896]{2,1,0:T(8,128)(2,1)S(1)}, u32[]{:S(2)}, u32[]{:S(2)}) %collective-permute-start.26) | collective-permute-done | bytes 458784 | tf_op jit(solution)/shard_map/ppermute | solution.py:23
  148.8 8.7 %collective-permute-done.27 = bf16[1,256,896]{2,1,0:T(8,128)(2,1)S(1)} collective-permute-done((bf16[1,256,896]{2,1,0:T(8,128)(2,1)S(1)}, bf16[1,256,896]{2,1,0:T(8,128)(2,1)S(1)}, u32[]{:S(2)}, u32[]{:S(2)}) %collective-permute-start.27) | collective-permute-done | bytes 458784 | tf_op jit(solution)/shard_map/ppermute | solution.py:23
  161.1 5.7 %rows_times_joined.2 = (bf16[4,256,256]{2,1,0:T(8,128)(2,1)S(1)}, f32[4,256,256]{2,1,0:T(8,128)S(1)}) custom-call(s32[8]{0:T(128)S(1)} %stack.36.order_ref.rows_ref, s32[4]{0:T(128)S(1)} %pad_add_fusion.cols_ref, bf16[2048,3584]{1,0:T(8,128)(2,1)S(1)} %copy-done.1, bf16[2,256,896]{2,1,0:T(8,128)(2,1)S(1)} %pad_maximum_fusion.1.first_ref, ...), custom_call_target="tpu_custom_call" | custom-call | flops 3758096384 | bytes 16515072 | tf_op jit(solution)/shard_map/rows_times_joined/pallas_call | solution.py:334
  171.0 5.7 %rows_times_joined.3 = (bf16[4,256,256]{2,1,0:T(8,128)(2,1)S(1)}, f32[4,256,256]{2,1,0:T(8,128)S(1)}) custom-call(s32[8]{0:T(128)S(1)} %stack.36.order_ref.rows_ref, s32[4]{0:T(128)S(1)} %pad_add_fusion.cols_ref, bf16[2048,3584]{1,0:T(8,128)(2,1)S(1)} %copy-done.1, bf16[2,256,896]{2,1,0:T(8,128)(2,1)S(1)} %pad_maximum_fusion.2.first_ref, ...), custom_call_target="tpu_custom_call" | custom-call | flops 3758096384 | bytes 16515072 | tf_op jit(solution)/shard_map/rows_times_joined/pallas_call | solution.py:334
  182.6 6.9 %collective-permute-done.17 = bf16[2,256,256]{2,1,0:T(8,128)(2,1)S(1)} collective-permute-done((bf16[2,256,256]{2,1,0:T(8,128)(2,1)S(1)}, bf16[2,256,256]{2,1,0:T(8,128)(2,1)S(1)}, u32[]{:S(2)}, u32[]{:S(2)}) %collective-permute-start.17) | collective-permute-done | bytes 262176 | tf_op jit(solution)/shard_map/ppermute | solution.py:23
  190.2 5.3 %collective-permute-done.30 = bf16[2,256,256]{2,1,0:T(8,128)(2,1)S(1)} collective-permute-done((bf16[2,256,256]{2,1,0:T(8,128)(2,1)S(1)}, bf16[2,256,256]{2,1,0:T(8,128)(2,1)S(1)}, u32[]{:S(2)}, u32[]{:S(2)}) %collective-permute-start.30) | collective-permute-done | bytes 262176 | tf_op jit(solution)/shard_map/ppermute | solution.py:23
  205.7 6.8 %collective-permute-start.20 = (bf16[2,256,256]{2,1,0:T(8,128)(2,1)S(1)}, bf16[2,256,256]{2,1,0:T(8,128)(2,1)S(1)}, u32[]{:S(2)}, u32[]{:S(2)}) collective-permute-start(bf16[2,256,256]{2,1,0:T(8,128)(2,1)S(1)} %pad_maximum_fusion.11), channel_id=1, source_target_pairs={{0,2},{1,5},{2,0},{3,7},{4,6},{5,1},{6,4},{7,3},{8,10},{9,13},{10,... | collective-permute-start | bytes 786440 | tf_op jit(solution)/shard_map/ppermute | solution.py:23
  216.1 6.0 %collective-permute-done.20 = bf16[2,256,256]{2,1,0:T(8,128)(2,1)S(1)} collective-permute-done((bf16[2,256,256]{2,1,0:T(8,128)(2,1)S(1)}, bf16[2,256,256]{2,1,0:T(8,128)(2,1)S(1)}, u32[]{:S(2)}, u32[]{:S(2)}) %collective-permute-start.20) | collective-permute-done | bytes 262176 | tf_op jit(solution)/shard_map/ppermute | solution.py:23
  233.5 9.2 %collective-permute-done.35 = f32[256,512]{1,0:T(8,128)S(1)} collective-permute-done((f32[256,512]{1,0:T(8,128)S(1)}, f32[256,512]{1,0:T(8,128)S(1)}, u32[]{:S(2)}, u32[]{:S(2)}) %collective-permute-start.35) | collective-permute-done | bytes 524320 | tf_op jit(solution)/shard_map/ppermute | solution.py:23
  242.8 9.2 %collective-permute-done.36 = f32[256,512]{1,0:T(8,128)S(1)} collective-permute-done((f32[256,512]{1,0:T(8,128)S(1)}, f32[256,512]{1,0:T(8,128)S(1)}, u32[]{:S(2)}, u32[]{:S(2)}) %collective-permute-start.36) | collective-permute-done | bytes 524320 | tf_op jit(solution)/shard_map/ppermute | solution.py:23
  255.5 21.3 %inverse_factor.1 = f32[512,512]{1,0:T(8,128)S(1)} custom-call(f32[512,512]{1,0:T(8,128)S(1)} %pad_maximum_fusion.gram_ref), custom_call_target="tpu_custom_call" | custom-call | flops 5368709120 | bytes 2097152 | tf_op jit(solution)/shard_map/inverse_factor/pallas_call | solution.py:291
  290.0 16.7 %collective-permute-done.38 = bf16[2,128,3584]{2,1,0:T(8,128)(2,1)S(1)} collective-permute-done((bf16[2,128,3584]{2,1,0:T(8,128)(2,1)S(1)}, bf16[2,128,3584]{2,1,0:T(8,128)(2,1)S(1)}, u32[]{:S(2)}, u32[]{:S(2)}) %collective-permute-start.38) | collective-permute-done | bytes 1835040 | tf_op jit(solution)/shard_map/ppermute | solution.py:23
  309.9 12.1 %collective-permute-done.39 = bf16[1,128,3584]{2,1,0:T(8,128)(2,1)} collective-permute-done((bf16[1,128,3584]{2,1,0:T(8,128)(2,1)}, bf16[1,128,3584]{2,1,0:T(8,128)(2,1)}, u32[]{:S(2)}, u32[]{:S(2)}) %collective-permute-start.39) | collective-permute-done | bytes 917536 | tf_op jit(solution)/shard_map/ppermute | solution.py:23
  (164 shorter events, 123.1 us)
Async XLA Ops:
  15.0 20.2 %collective-permute-start.6 = (f32[4,256,256]{2,1,0:T(8,128)}, f32[4,256,256]{2,1,0:T(8,128)}, u32[]{:S(2)}, u32[]{:S(2)}) collective-permute-start(f32[4,256,256]{2,1,0:T(8,128)} %get-tuple-element.21), channel_id=1, source_target_pairs={{0,1},{1,0},{2,3},{3,2},{4,5},{5,4},{6,7},{7,6},{8,9},{9,8},{10,11... | collective-permute-start | bytes 3145736 | tf_op jit(solution)/shard_map/ppermute | solution.py:23
  22.5 16.8 %collective-permute-start.1 = (f32[4,256,256]{2,1,0:T(8,128)}, f32[4,256,256]{2,1,0:T(8,128)}, u32[]{:S(2)}, u32[]{:S(2)}) collective-permute-start(f32[4,256,256]{2,1,0:T(8,128)} %get-tuple-element.19), channel_id=1, source_target_pairs={{0,1},{1,0},{2,3},{3,2},{4,5},{5,4},{6,7},{7,6},{8,9},{9,8},{10,11... | collective-permute-start | bytes 3145736 | tf_op jit(solution)/shard_map/ppermute | solution.py:23
  36.4 9.8 %collective-permute-start.7 = (bf16[2,256,256]{2,1,0:T(8,128)(2,1)S(1)}, bf16[2,256,256]{2,1,0:T(8,128)(2,1)S(1)}, u32[]{:S(2)}, u32[]{:S(2)}) collective-permute-start(bf16[2,256,256]{2,1,0:T(8,128)(2,1)S(1)} %fusion.19), channel_id=1, source_target_pairs={{0,2},{1,5},{2,0},{3,7},{4,6},{5,1},{6,4},{7,3},{8,10},{9,13},{10,... | collective-permute-start | bytes 786440 | tf_op jit(solution)/shard_map/ppermute | solution.py:23
  40.5 14.7 %collective-permute-start.2 = (bf16[576,256]{1,0:T(8,128)(2,1)S(1)}, bf16[576,256]{1,0:T(8,128)(2,1)S(1)}, u32[]{:S(2)}, u32[]{:S(2)}) collective-permute-start(bf16[576,256]{1,0:T(8,128)(2,1)S(1)} %pad_maximum_fusion.9), channel_id=1, source_target_pairs={{0,2},{1,5},{2,0},{3,7},{4,6},{5,1},{6,4},{7,3},{8,10},{9,13},{10,... | collective-permute-start | bytes 884744 | tf_op jit(solution)/shard_map/ppermute | solution.py:23
  59.5 13.2 %collective-permute-start.3 = (bf16[320,256]{1,0:T(8,128)(2,1)S(1)}, bf16[320,256]{1,0:T(8,128)(2,1)S(1)}, u32[]{:S(2)}, u32[]{:S(2)}) collective-permute-start(bf16[320,256]{1,0:T(8,128)(2,1)S(1)} %pad_maximum_fusion.14), channel_id=1, source_target_pairs={{0,4},{1,3},{2,6},{3,1},{4,0},{5,7},{6,2},{7,5},{8,12},{9,11},{10,... | collective-permute-start | bytes 491528 | tf_op jit(solution)/shard_map/ppermute | solution.py:23
  63.7 20.9 %collective-permute-start.10 = (bf16[2,256,256]{2,1,0:T(8,128)(2,1)S(1)}, bf16[2,256,256]{2,1,0:T(8,128)(2,1)S(1)}, u32[]{:S(2)}, u32[]{:S(2)}) collective-permute-start(bf16[2,256,256]{2,1,0:T(8,128)(2,1)S(1)} %pad_maximum_fusion.10), channel_id=1, source_target_pairs={{0,2},{1,5},{2,0},{3,7},{4,6},{5,1},{6,4},{7,3},{8,10},{9,13},{10,... | collective-permute-start | bytes 786440 | tf_op jit(solution)/shard_map/ppermute | solution.py:23
  73.6 10.8 %collective-permute-start.22 = (bf16[1,256,256]{2,1,0:T(8,128)(2,1)S(1)}, bf16[1,256,256]{2,1,0:T(8,128)(2,1)S(1)}, u32[]{:S(2)}, u32[]{:S(2)}) collective-permute-start(bf16[1,256,256]{2,1,0:T(8,128)(2,1)S(1)} %fusion.39), channel_id=1, source_target_pairs={{0,4},{1,3},{2,6},{3,1},{4,0},{5,7},{6,2},{7,5},{8,12},{9,11},{10,... | collective-permute-start | bytes 393224 | tf_op jit(solution)/shard_map/ppermute | solution.py:23
  84.7 9.3 %collective-permute-start.11 = (bf16[4,256,256]{2,1,0:T(8,128)(2,1)S(1)}, bf16[4,256,256]{2,1,0:T(8,128)(2,1)S(1)}, u32[]{:S(2)}, u32[]{:S(2)}) collective-permute-start(bf16[4,256,256]{2,1,0:T(8,128)(2,1)S(1)} %pad_maximum_fusion.3.first_ref), channel_id=1, source_target_pairs={{0,1},{1,0},{2,3},{3,2},{4,5},{5,4},{6,7},{7,6},{8,9},{9,8},{10,11... | collective-permute-start | bytes 1572872 | tf_op jit(solution)/shard_map/ppermute | solution.py:23
  91.0 15.0 %collective-permute-start.24 = (bf16[4,256,256]{2,1,0:T(8,128)(2,1)S(1)}, bf16[4,256,256]{2,1,0:T(8,128)(2,1)S(1)}, u32[]{:S(2)}, u32[]{:S(2)}) collective-permute-start(bf16[4,256,256]{2,1,0:T(8,128)(2,1)S(1)} %pad_maximum_fusion.5.first_ref), channel_id=1, source_target_pairs={{0,1},{1,0},{2,3},{3,2},{4,5},{5,4},{6,7},{7,6},{8,9},{9,8},{10,11... | collective-permute-start | bytes 1572872 | tf_op jit(solution)/shard_map/ppermute | solution.py:23
  104.9 13.5 %collective-permute-start.12 = (bf16[2,256,896]{2,1,0:T(8,128)(2,1)S(1)}, bf16[2,256,896]{2,1,0:T(8,128)(2,1)S(1)}, u32[]{:S(2)}, u32[]{:S(2)}) collective-permute-start(bf16[2,256,896]{2,1,0:T(8,128)(2,1)S(1)} %get-tuple-element.23), channel_id=1, source_target_pairs={{0,8},{1,17},{2,10},{3,19},{4,12},{5,21},{6,14},{7,23},{8,0},{9,25... | collective-permute-start | bytes 2752520 | tf_op jit(solution)/shard_map/ppermute | solution.py:23
  112.0 21.2 %collective-permute-start.25 = (bf16[2,256,896]{2,1,0:T(8,128)(2,1)S(1)}, bf16[2,256,896]{2,1,0:T(8,128)(2,1)S(1)}, u32[]{:S(2)}, u32[]{:S(2)}) collective-permute-start(bf16[2,256,896]{2,1,0:T(8,128)(2,1)S(1)} %get-tuple-element.27), channel_id=1, source_target_pairs={{0,8},{1,17},{2,10},{3,19},{4,12},{5,21},{6,14},{7,23},{8,0},{9,25... | collective-permute-start | bytes 2752520 | tf_op jit(solution)/shard_map/ppermute | solution.py:23
  118.5 15.9 %collective-permute-start.13 = (bf16[1,256,896]{2,1,0:T(8,128)(2,1)S(1)}, bf16[1,256,896]{2,1,0:T(8,128)(2,1)S(1)}, u32[]{:S(2)}, u32[]{:S(2)}) collective-permute-start(bf16[1,256,896]{2,1,0:T(8,128)(2,1)S(1)} %add_convert_fusion.3), channel_id=1, source_target_pairs={{0,16},{1,9},{2,18},{3,11},{4,20},{5,13},{6,22},{7,15},{8,24},{9,1... | collective-permute-start | bytes 1376264 | tf_op jit(solution)/shard_map/ppermute | solution.py:23
  134.6 13.0 %collective-permute-start.14 = (bf16[1,256,896]{2,1,0:T(8,128)(2,1)S(1)}, bf16[1,256,896]{2,1,0:T(8,128)(2,1)S(1)}, u32[]{:S(2)}, u32[]{:S(2)}) collective-permute-start(bf16[1,256,896]{2,1,0:T(8,128)(2,1)S(1)} %add_convert_fusion.2), channel_id=1, source_target_pairs={{0,16},{1,9},{2,18},{3,11},{4,20},{5,13},{6,22},{7,15},{8,24},{9,1... | collective-permute-start | bytes 1376264 | tf_op jit(solution)/shard_map/ppermute | solution.py:23
  142.0 15.4 %collective-permute-start.27 = (bf16[1,256,896]{2,1,0:T(8,128)(2,1)S(1)}, bf16[1,256,896]{2,1,0:T(8,128)(2,1)S(1)}, u32[]{:S(2)}, u32[]{:S(2)}) collective-permute-start(bf16[1,256,896]{2,1,0:T(8,128)(2,1)S(1)} %add_convert_fusion), channel_id=1, source_target_pairs={{0,16},{1,9},{2,18},{3,11},{4,20},{5,13},{6,22},{7,15},{8,24},{9,1... | collective-permute-start | bytes 1376264 | tf_op jit(solution)/shard_map/ppermute | solution.py:23
  147.7 13.5 %collective-permute-start.15 = (bf16[2,256,896]{2,1,0:T(8,128)(2,1)S(1)}, bf16[2,256,896]{2,1,0:T(8,128)(2,1)S(1)}, u32[]{:S(2)}, u32[]{:S(2)}) collective-permute-start(bf16[2,256,896]{2,1,0:T(8,128)(2,1)S(1)} %pad_maximum_fusion.1.first_ref), channel_id=1, source_target_pairs={{0,8},{1,17},{2,10},{3,19},{4,12},{5,21},{6,14},{7,23},{8,0},{9,25... | collective-permute-start | bytes 2752520 | tf_op jit(solution)/shard_map/ppermute | solution.py:23
  157.5 13.5 %collective-permute-start.28 = (bf16[2,256,896]{2,1,0:T(8,128)(2,1)S(1)}, bf16[2,256,896]{2,1,0:T(8,128)(2,1)S(1)}, u32[]{:S(2)}, u32[]{:S(2)}) collective-permute-start(bf16[2,256,896]{2,1,0:T(8,128)(2,1)S(1)} %pad_maximum_fusion.2.first_ref), channel_id=1, source_target_pairs={{0,8},{1,17},{2,10},{3,19},{4,12},{5,21},{6,14},{7,23},{8,0},{9,25... | collective-permute-start | bytes 2752520 | tf_op jit(solution)/shard_map/ppermute | solution.py:23
  166.9 10.1 %collective-permute-start.16 = (bf16[4,256,256]{2,1,0:T(8,128)(2,1)S(1)}, bf16[4,256,256]{2,1,0:T(8,128)(2,1)S(1)}, u32[]{:S(2)}, u32[]{:S(2)}) collective-permute-start(bf16[4,256,256]{2,1,0:T(8,128)(2,1)S(1)} %get-tuple-element.25), channel_id=1, source_target_pairs={{0,1},{1,0},{2,3},{3,2},{4,5},{5,4},{6,7},{7,6},{8,9},{9,8},{10,11... | collective-permute-start | bytes 1572872 | tf_op jit(solution)/shard_map/ppermute | solution.py:23
  177.0 12.4 %collective-permute-start.17 = (bf16[2,256,256]{2,1,0:T(8,128)(2,1)S(1)}, bf16[2,256,256]{2,1,0:T(8,128)(2,1)S(1)}, u32[]{:S(2)}, u32[]{:S(2)}) collective-permute-start(bf16[2,256,256]{2,1,0:T(8,128)(2,1)S(1)} %add_convert_fusion.5), channel_id=1, source_target_pairs={{0,2},{1,5},{2,0},{3,7},{4,6},{5,1},{6,4},{7,3},{8,10},{9,13},{10,... | collective-permute-start | bytes 786440 | tf_op jit(solution)/shard_map/ppermute | solution.py:23
  180.7 14.8 %collective-permute-start.30 = (bf16[2,256,256]{2,1,0:T(8,128)(2,1)S(1)}, bf16[2,256,256]{2,1,0:T(8,128)(2,1)S(1)}, u32[]{:S(2)}, u32[]{:S(2)}) collective-permute-start(bf16[2,256,256]{2,1,0:T(8,128)(2,1)S(1)} %add_convert_fusion.4), channel_id=1, source_target_pairs={{0,2},{1,5},{2,0},{3,7},{4,6},{5,1},{6,4},{7,3},{8,10},{9,13},{10,... | collective-permute-start | bytes 786440 | tf_op jit(solution)/shard_map/ppermute | solution.py:23
  202.7 13.4 %collective-permute-start.32 = (bf16[1,256,256]{2,1,0:T(8,128)(2,1)S(1)}, bf16[1,256,256]{2,1,0:T(8,128)(2,1)S(1)}, u32[]{:S(2)}, u32[]{:S(2)}) collective-permute-start(bf16[1,256,256]{2,1,0:T(8,128)(2,1)S(1)} %add_convert_fusion.6), channel_id=1, source_target_pairs={{0,4},{1,3},{2,6},{3,1},{4,0},{5,7},{6,2},{7,5},{8,12},{9,11},{10,... | collective-permute-start | bytes 393224 | tf_op jit(solution)/shard_map/ppermute | solution.py:23
  205.7 16.5 %collective-permute-start.20 = (bf16[2,256,256]{2,1,0:T(8,128)(2,1)S(1)}, bf16[2,256,256]{2,1,0:T(8,128)(2,1)S(1)}, u32[]{:S(2)}, u32[]{:S(2)}) collective-permute-start(bf16[2,256,256]{2,1,0:T(8,128)(2,1)S(1)} %pad_maximum_fusion.11), channel_id=1, source_target_pairs={{0,2},{1,5},{2,0},{3,7},{4,6},{5,1},{6,4},{7,3},{8,10},{9,13},{10,... | collective-permute-start | bytes 786440 | tf_op jit(solution)/shard_map/ppermute | solution.py:23
  233.4 9.2 %collective-permute-start.35 = (f32[256,512]{1,0:T(8,128)S(1)}, f32[256,512]{1,0:T(8,128)S(1)}, u32[]{:S(2)}, u32[]{:S(2)}) collective-permute-start(f32[256,512]{1,0:T(8,128)S(1)} %convolution_add_fusion.2), channel_id=1, source_target_pairs={{0,8},{1,17},{2,10},{3,19},{4,12},{5,21},{6,14},{7,23},{8,0},{9,25... | collective-permute-start | bytes 1572872 | tf_op jit(solution)/shard_map/ppermute | solution.py:23
  283.5 23.3 %collective-permute-start.38 = (bf16[2,128,3584]{2,1,0:T(8,128)(2,1)S(1)}, bf16[2,128,3584]{2,1,0:T(8,128)(2,1)S(1)}, u32[]{:S(2)}, u32[]{:S(2)}) collective-permute-start(bf16[2,128,3584]{2,1,0:T(8,128)(2,1)S(1)} %bitcast.68), channel_id=1, source_target_pairs={{0,8},{1,17},{2,10},{3,19},{4,12},{5,21},{6,14},{7,23},{8,0},{9,25... | collective-permute-start | bytes 5505032 | tf_op jit(solution)/shard_map/ppermute | solution.py:23
  308.3 13.7 %collective-permute-start.39 = (bf16[1,128,3584]{2,1,0:T(8,128)(2,1)}, bf16[1,128,3584]{2,1,0:T(8,128)(2,1)}, u32[]{:S(2)}, u32[]{:S(2)}) collective-permute-start(bf16[1,128,3584]{2,1,0:T(8,128)(2,1)} %fusion.6), channel_id=1, source_target_pairs={{0,16},{1,9},{2,18},{3,11},{4,20},{5,13},{6,22},{7,15},{8,24},{9,1... | collective-permute-start | bytes 2752520 | tf_op jit(solution)/shard_map/ppermute | solution.py:23
  (35 other events, 266.9 us)

commit v7 on v6

--- a/solution.py
+++ b/solution.py
@@ -536,14 +536,18 @@
     square_scale = lax.dynamic_slice_in_dim(fisher, row * rows_here, rows_here) / mean
     own_square = lax.dynamic_slice_in_dim(square_scale, col * own_rows, own_rows)
 
-    def second_of(raw):
-        first = over_col.gather(raw.astype(BF16))
-        parts = cols_times_joined(weight, square_scale, first, over_col, over_row)
+    def second_of(first, scale):
+        first = over_col.gather(first.astype(BF16))
+        parts = cols_times_joined(weight, scale, first, over_col, over_row)
         projected = over_row.gather(over_row.scatter_sum(*parts).astype(BF16))
         parts = rows_times_joined(weight, projected, over_col, over_row)
         return over_col.gather(over_col.scatter_sum(*parts).astype(BF16))
 
-    second = settle(second_of(raw), second_of(later), over_col)
+    second = settle(
+        second_of(raw, square_scale),
+        second_of(own_square * later, jnp.ones_like(square_scale)),
+        over_col,
+    )
 
     even = (col & 1) == 0
     mine = lax.dynamic_slice_in_dim(second, (col & 1) * half, half, 1).astype(F32)

time: 325 us -> 321 us (0.988)
  waiting for transfers between devices: 163 us -> 153 us
  starting transfers between devices: 42.1 us -> 49.3 us
    ppermute x40, waiting for transfers between devices: 163 us -> 153 us  [swap(): return lax.ppermute(block, AXES, pairs)]
    ppermute x40, starting transfers between devices: 42.1 us -> 49.3 us  [swap(): return lax.ppermute(block, AXES, pairs)]
    unnamed x39 -> x31, local copies, waits for them, and re-layouts: 16.2 us -> 16.1 us
  transfers between devices with their start and end apart: 40 -> 40, of which waited for: 30 -> 29; matrix products, arithmetic and copies ran while one was open for 4% -> 4% of each run, Pallas kernels for 14% -> 14%
where the time goes in v7:
time: 321 us; the launch traced here: 320 us
  waiting for transfers between devices  153 us (48%)
  Pallas kernels  79.2 us (25%)
  starting transfers between devices  49.3 us (15%)
  local copies, waits for them, and re-layouts  16.9 us (5%)
  other arithmetic  12.5 us (4%)
  matrix products  7.31 us (2%)
    ppermute x40, waiting for transfers between devices, swap(): return lax.ppermute(block, AXES, pairs)  153 us
    ppermute x40, starting transfers between devices, swap(): return lax.ppermute(block, AXES, pairs)  49.3 us
    pallas_call x6, Pallas kernels, product_call(): pl.pallas_call(kernel, out_shape=out_shape, in_specs=[smem] * len(indices...  37.3 us
    pallas_call x1, Pallas kernels, inverse_factor(): pl.pallas_call(inverse_factor_kernel, out_shape=jax.ShapeDtypeStruct((siz...  21.3 us
    unnamed x31, local copies, waits for them, and re-layouts  16.1 us
    pallas_call x2, Pallas kernels, rank_times(): pl.pallas_call(rank_kernel, out_shape=jax.ShapeDtypeStruct((basis.shape[0...  9.91 us
    dot_general x8, matrix products, dot(): lax.dot_general(left, right, (dims, ((), ())), preferred_element_type=F32)  7.31 us
    pallas_call x1, Pallas kernels, local_mass(): pl.pallas_call(row_mass_kernel, out_shape=jax.ShapeDtypeStruct((1, width)...  7.31 us
  transfers between devices with their start and end apart: 40, of which 29 were waited for; matrix products, arithmetic and copies ran while one was open for 4% of the time, Pallas kernels for 14%

profile of v7, /device:TPU:0, one launch (start us, length us, event | category | flops | bytes accessed | tf_op | source)
XLA Modules:
  0.0 320.3 jit_solution(7733669933304078192)
XLA Ops:
  0.7 5.2 %copy-done = bf16[2048,3584]{1,0:T(8,128)(2,1)S(1)} copy-done((bf16[2048,3584]{1,0:T(8,128)(2,1)S(1)}, bf16[2048,3584]{1,0:T(8,128)(2,1)}, u32[]{:S(2)}) %copy-start) | copy-done | bytes 14680088
  8.0 7.1 %rows_times.3 = (f32[4,256,256]{2,1,0:T(8,128)}, f32[4,256,256]{2,1,0:T(8,128)S(1)}) custom-call(s32[8]{0:T(128)S(1)} %stack.36.order_ref.rows_ref, bf16[2048,3584]{1,0:T(8,128)(2,1)S(1)} %copy-done, bf16[3584,512]{1,0:T(8,128)(2,1)S(1)} %copy-done.2), custom_call_target="tpu_custom_call" | custom-call | flops 3758096384 | bytes 16515072 | tf_op jit(solution)/shard_map/rows_times/pallas_call | solution.py:334
  15.5 7.0 %rows_times.2 = (f32[4,256,256]{2,1,0:T(8,128)}, f32[4,256,256]{2,1,0:T(8,128)S(1)}) custom-call(s32[8]{0:T(128)S(1)} %stack.36.order_ref.rows_ref, bf16[2048,3584]{1,0:T(8,128)(2,1)S(1)} %copy-done, bf16[3584,512]{1,0:T(8,128)(2,1)S(1)} %copy-done.2), custom_call_target="tpu_custom_call" | custom-call | flops 3758096384 | bytes 16515072 | tf_op jit(solution)/shard_map/rows_times/pallas_call | solution.py:334
  25.3 7.3 %row_mass.1 = f32[1,8192]{1,0:T(1,128)S(1)} custom-call(bf16[2,256,8192]{2,1,0:T(8,128)(2,1)S(1)} %bitcast.73, bf16[2,512,256]{2,1,0:T(8,128)(2,1)S(1)} %get-tuple-element.17.gram_ref, f32[2,256,128]{2,1,0:T(8,128)S(1)} %get-tuple-element.18.scale_ref), custom_call_target="tpu_custom_call" | custom-call | flops 4294967296 | bytes 8388608 | tf_op jit(solution)/shard_map/row_mass/pallas_call | solution.py:195
  40.7 5.5 %collective-permute-done.7 = bf16[2,256,256]{2,1,0:T(8,128)(2,1)S(1)} collective-permute-done((bf16[2,256,256]{2,1,0:T(8,128)(2,1)S(1)}, bf16[2,256,256]{2,1,0:T(8,128)(2,1)S(1)}, u32[]{:S(2)}, u32[]{:S(2)}) %collective-permute-start.7) | collective-permute-done | bytes 262176 | tf_op jit(solution)/shard_map/ppermute | solution.py:23
  77.2 8.2 %collective-permute-done.22 = bf16[1,256,256]{2,1,0:T(8,128)(2,1)S(1)} collective-permute-done((bf16[1,256,256]{2,1,0:T(8,128)(2,1)S(1)}, bf16[1,256,256]{2,1,0:T(8,128)(2,1)S(1)}, u32[]{:S(2)}, u32[]{:S(2)}) %collective-permute-start.22) | collective-permute-done | bytes 131104 | tf_op jit(solution)/shard_map/ppermute | solution.py:23
  86.5 5.4 %collective-permute-done.23 = bf16[2,256,256]{2,1,0:T(8,128)(2,1)S(1)} collective-permute-done((bf16[2,256,256]{2,1,0:T(8,128)(2,1)S(1)}, bf16[2,256,256]{2,1,0:T(8,128)(2,1)S(1)}, u32[]{:S(2)}, u32[]{:S(2)}) %collective-permute-start.23) | collective-permute-done | bytes 262176 | tf_op jit(solution)/shard_map/ppermute | solution.py:23
  97.3 5.8 %cols_times_joined.2 = (bf16[2,256,896]{2,1,0:T(8,128)(2,1)S(1)}, f32[2,256,896]{2,1,0:T(8,128)S(1)}) custom-call(s32[4]{0:T(128)S(1)} %pad_add_fusion.cols_ref, s32[8]{0:T(128)S(1)} %stack.36.order_ref.rows_ref, bf16[2048,3584]{1,0:T(8,128)(2,1)S(1)} %copy-done.1, f32[1,2048]{1,0:T(1,128)S(1)} %bitcast.71, ...), custom_call_target="tpu_custom_call" | custom-call | flops 3758096384 | bytes 16515072 | tf_op jit(solution)/shard_map/cols_times_joined/pallas_call | solution.py:334
  104.9 6.0 %cols_times_joined.3 = (bf16[2,256,896]{2,1,0:T(8,128)(2,1)S(1)}, f32[2,256,896]{2,1,0:T(8,128)S(1)}) custom-call(s32[4]{0:T(128)S(1)} %pad_add_fusion.cols_ref, s32[8]{0:T(128)S(1)} %stack.36.order_ref.rows_ref, bf16[2048,3584]{1,0:T(8,128)(2,1)S(1)} %copy-done.1, f32[1,2048]{1,0:T(1,128)S(1)} %broadcast_in_dim_broadcast_in_dim.3.scale_ref, ...), custom_call_target="tpu_custom_call" | custom-call | flops 3758096384 | bytes 16515072 | tf_op jit(solution)/shard_map/cols_times_joined/pallas_call | solution.py:334
  111.3 5.3 %collective-permute-done.12 = bf16[2,256,896]{2,1,0:T(8,128)(2,1)S(1)} collective-permute-done((bf16[2,256,896]{2,1,0:T(8,128)(2,1)S(1)}, bf16[2,256,896]{2,1,0:T(8,128)(2,1)S(1)}, u32[]{:S(2)}, u32[]{:S(2)}) %collective-permute-start.12) | collective-permute-done | bytes 917536 | tf_op jit(solution)/shard_map/ppermute | solution.py:23
  119.3 12.0 %collective-permute-done.25 = bf16[2,256,896]{2,1,0:T(8,128)(2,1)S(1)} collective-permute-done((bf16[2,256,896]{2,1,0:T(8,128)(2,1)S(1)}, bf16[2,256,896]{2,1,0:T(8,128)(2,1)S(1)}, u32[]{:S(2)}, u32[]{:S(2)}) %collective-permute-start.25) | collective-permute-done | bytes 917536 | tf_op jit(solution)/shard_map/ppermute | solution.py:23
  134.3 6.2 %collective-permute-done.26 = bf16[1,256,896]{2,1,0:T(8,128)(2,1)S(1)} collective-permute-done((bf16[1,256,896]{2,1,0:T(8,128)(2,1)S(1)}, bf16[1,256,896]{2,1,0:T(8,128)(2,1)S(1)}, u32[]{:S(2)}, u32[]{:S(2)}) %collective-permute-start.26) | collective-permute-done | bytes 458784 | tf_op jit(solution)/shard_map/ppermute | solution.py:23
  147.4 5.7 %collective-permute-done.27 = bf16[1,256,896]{2,1,0:T(8,128)(2,1)S(1)} collective-permute-done((bf16[1,256,896]{2,1,0:T(8,128)(2,1)S(1)}, bf16[1,256,896]{2,1,0:T(8,128)(2,1)S(1)}, u32[]{:S(2)}, u32[]{:S(2)}) %collective-permute-start.27) | collective-permute-done | bytes 458784 | tf_op jit(solution)/shard_map/ppermute | solution.py:23
  158.9 5.7 %rows_times_joined.2 = (bf16[4,256,256]{2,1,0:T(8,128)(2,1)S(1)}, f32[4,256,256]{2,1,0:T(8,128)S(1)}) custom-call(s32[8]{0:T(128)S(1)} %stack.36.order_ref.rows_ref, s32[4]{0:T(128)S(1)} %pad_add_fusion.cols_ref, bf16[2048,3584]{1,0:T(8,128)(2,1)S(1)} %copy-done.1, bf16[2,256,896]{2,1,0:T(8,128)(2,1)S(1)} %pad_maximum_fusion.1.first_ref, ...), custom_call_target="tpu_custom_call" | custom-call | flops 3758096384 | bytes 16515072 | tf_op jit(solution)/shard_map/rows_times_joined/pallas_call | solution.py:334
  168.8 5.7 %rows_times_joined.3 = (bf16[4,256,256]{2,1,0:T(8,128)(2,1)S(1)}, f32[4,256,256]{2,1,0:T(8,128)S(1)}) custom-call(s32[8]{0:T(128)S(1)} %stack.36.order_ref.rows_ref, s32[4]{0:T(128)S(1)} %pad_add_fusion.cols_ref, bf16[2048,3584]{1,0:T(8,128)(2,1)S(1)} %copy-done.1, bf16[2,256,896]{2,1,0:T(8,128)(2,1)S(1)} %pad_maximum_fusion.2.first_ref, ...), custom_call_target="tpu_custom_call" | custom-call | flops 3758096384 | bytes 16515072 | tf_op jit(solution)/shard_map/rows_times_joined/pallas_call | solution.py:334
  177.9 6.9 %collective-permute-done.17 = bf16[2,256,256]{2,1,0:T(8,128)(2,1)S(1)} collective-permute-done((bf16[2,256,256]{2,1,0:T(8,128)(2,1)S(1)}, bf16[2,256,256]{2,1,0:T(8,128)(2,1)S(1)}, u32[]{:S(2)}, u32[]{:S(2)}) %collective-permute-start.17) | collective-permute-done | bytes 262176 | tf_op jit(solution)/shard_map/ppermute | solution.py:23
  186.7 6.6 %collective-permute-done.30 = bf16[2,256,256]{2,1,0:T(8,128)(2,1)S(1)} collective-permute-done((bf16[2,256,256]{2,1,0:T(8,128)(2,1)S(1)}, bf16[2,256,256]{2,1,0:T(8,128)(2,1)S(1)}, u32[]{:S(2)}, u32[]{:S(2)}) %collective-permute-start.30) | collective-permute-done | bytes 262176 | tf_op jit(solution)/shard_map/ppermute | solution.py:23
  200.9 10.0 %collective-permute-done.19 = bf16[1,256,256]{2,1,0:T(8,128)(2,1)S(1)} collective-permute-done((bf16[1,256,256]{2,1,0:T(8,128)(2,1)S(1)}, bf16[1,256,256]{2,1,0:T(8,128)(2,1)S(1)}, u32[]{:S(2)}, u32[]{:S(2)}) %collective-permute-start.19) | collective-permute-done | bytes 131104 | tf_op jit(solution)/shard_map/ppermute | solution.py:23
  213.9 6.4 %collective-permute-done.20 = bf16[2,256,256]{2,1,0:T(8,128)(2,1)S(1)} collective-permute-done((bf16[2,256,256]{2,1,0:T(8,128)(2,1)S(1)}, bf16[2,256,256]{2,1,0:T(8,128)(2,1)S(1)}, u32[]{:S(2)}, u32[]{:S(2)}) %collective-permute-start.20) | collective-permute-done | bytes 262176 | tf_op jit(solution)/shard_map/ppermute | solution.py:23
  233.1 7.7 %collective-permute-done.35 = f32[256,512]{1,0:T(8,128)S(1)} collective-permute-done((f32[256,512]{1,0:T(8,128)S(1)}, f32[256,512]{1,0:T(8,128)S(1)}, u32[]{:S(2)}, u32[]{:S(2)}) %collective-permute-start.35) | collective-permute-done | bytes 524320 | tf_op jit(solution)/shard_map/ppermute | solution.py:23
  242.6 7.6 %collective-permute-done.36 = f32[256,512]{1,0:T(8,128)S(1)} collective-permute-done((f32[256,512]{1,0:T(8,128)S(1)}, f32[256,512]{1,0:T(8,128)S(1)}, u32[]{:S(2)}, u32[]{:S(2)}) %collective-permute-start.36) | collective-permute-done | bytes 524320 | tf_op jit(solution)/shard_map/ppermute | solution.py:23
  253.6 21.3 %inverse_factor.1 = f32[512,512]{1,0:T(8,128)S(1)} custom-call(f32[512,512]{1,0:T(8,128)S(1)} %pad_maximum_fusion.gram_ref), custom_call_target="tpu_custom_call" | custom-call | flops 5368709120 | bytes 2097152 | tf_op jit(solution)/shard_map/inverse_factor/pallas_call | solution.py:291
  289.6 15.3 %collective-permute-done.38 = bf16[2,128,3584]{2,1,0:T(8,128)(2,1)S(1)} collective-permute-done((bf16[2,128,3584]{2,1,0:T(8,128)(2,1)S(1)}, bf16[2,128,3584]{2,1,0:T(8,128)(2,1)S(1)}, u32[]{:S(2)}, u32[]{:S(2)}) %collective-permute-start.38) | collective-permute-done | bytes 1835040 | tf_op jit(solution)/shard_map/ppermute | solution.py:23
  308.3 10.3 %collective-permute-done.39 = bf16[1,128,3584]{2,1,0:T(8,128)(2,1)S(1)} collective-permute-done((bf16[1,128,3584]{2,1,0:T(8,128)(2,1)S(1)}, bf16[1,128,3584]{2,1,0:T(8,128)(2,1)S(1)}, u32[]{:S(2)}, u32[]{:S(2)}) %collective-permute-start.39) | collective-permute-done | bytes 917536 | tf_op jit(solution)/shard_map/ppermute | solution.py:23
  (157 shorter events, 128.2 us)
Async XLA Ops:
  15.0 20.3 %collective-permute-start.6 = (f32[4,256,256]{2,1,0:T(8,128)}, f32[4,256,256]{2,1,0:T(8,128)}, u32[]{:S(2)}, u32[]{:S(2)}) collective-permute-start(f32[4,256,256]{2,1,0:T(8,128)} %get-tuple-element.21), channel_id=1, source_target_pairs={{0,1},{1,0},{2,3},{3,2},{4,5},{5,4},{6,7},{7,6},{8,9},{9,8},{10,11... | collective-permute-start | bytes 3145736 | tf_op jit(solution)/shard_map/ppermute | solution.py:23
  22.5 16.9 %collective-permute-start.1 = (f32[4,256,256]{2,1,0:T(8,128)}, f32[4,256,256]{2,1,0:T(8,128)}, u32[]{:S(2)}, u32[]{:S(2)}) collective-permute-start(f32[4,256,256]{2,1,0:T(8,128)} %get-tuple-element.19), channel_id=1, source_target_pairs={{0,1},{1,0},{2,3},{3,2},{4,5},{5,4},{6,7},{7,6},{8,9},{9,8},{10,11... | collective-permute-start | bytes 3145736 | tf_op jit(solution)/shard_map/ppermute | solution.py:23
  36.5 9.7 %collective-permute-start.7 = (bf16[2,256,256]{2,1,0:T(8,128)(2,1)S(1)}, bf16[2,256,256]{2,1,0:T(8,128)(2,1)S(1)}, u32[]{:S(2)}, u32[]{:S(2)}) collective-permute-start(bf16[2,256,256]{2,1,0:T(8,128)(2,1)S(1)} %fusion.19), channel_id=1, source_target_pairs={{0,2},{1,5},{2,0},{3,7},{4,6},{5,1},{6,4},{7,3},{8,10},{9,13},{10,... | collective-permute-start | bytes 786440 | tf_op jit(solution)/shard_map/ppermute | solution.py:23
  40.6 14.7 %collective-permute-start.2 = (bf16[576,256]{1,0:T(8,128)(2,1)S(1)}, bf16[576,256]{1,0:T(8,128)(2,1)S(1)}, u32[]{:S(2)}, u32[]{:S(2)}) collective-permute-start(bf16[576,256]{1,0:T(8,128)(2,1)S(1)} %pad_maximum_fusion.9), channel_id=1, source_target_pairs={{0,2},{1,5},{2,0},{3,7},{4,6},{5,1},{6,4},{7,3},{8,10},{9,13},{10,... | collective-permute-start | bytes 884744 | tf_op jit(solution)/shard_map/ppermute | solution.py:23
  47.2 10.5 %collective-permute-start.8 = (bf16[1,256,256]{2,1,0:T(8,128)(2,1)S(1)}, bf16[1,256,256]{2,1,0:T(8,128)(2,1)S(1)}, u32[]{:S(2)}, u32[]{:S(2)}) collective-permute-start(bf16[1,256,256]{2,1,0:T(8,128)(2,1)S(1)} %fusion.31), channel_id=1, source_target_pairs={{0,4},{1,3},{2,6},{3,1},{4,0},{5,7},{6,2},{7,5},{8,12},{9,11},{10,... | collective-permute-start | bytes 393224 | tf_op jit(solution)/shard_map/ppermute | solution.py:23
  58.7 12.0 %collective-permute-start.9 = (bf16[1,256,256]{2,1,0:T(8,128)(2,1)S(1)}, bf16[1,256,256]{2,1,0:T(8,128)(2,1)S(1)}, u32[]{:S(2)}, u32[]{:S(2)}) collective-permute-start(bf16[1,256,256]{2,1,0:T(8,128)(2,1)S(1)} %fusion.34), channel_id=1, source_target_pairs={{0,4},{1,3},{2,6},{3,1},{4,0},{5,7},{6,2},{7,5},{8,12},{9,11},{10,... | collective-permute-start | bytes 393224 | tf_op jit(solution)/shard_map/ppermute | solution.py:23
  70.7 15.7 %collective-permute-start.10 = (bf16[2,256,256]{2,1,0:T(8,128)(2,1)S(1)}, bf16[2,256,256]{2,1,0:T(8,128)(2,1)S(1)}, u32[]{:S(2)}, u32[]{:S(2)}) collective-permute-start(bf16[2,256,256]{2,1,0:T(8,128)(2,1)S(1)} %pad_maximum_fusion.10), channel_id=1, source_target_pairs={{0,2},{1,5},{2,0},{3,7},{4,6},{5,1},{6,4},{7,3},{8,10},{9,13},{10,... | collective-permute-start | bytes 786440 | tf_op jit(solution)/shard_map/ppermute | solution.py:23
  75.0 10.5 %collective-permute-start.22 = (bf16[1,256,256]{2,1,0:T(8,128)(2,1)S(1)}, bf16[1,256,256]{2,1,0:T(8,128)(2,1)S(1)}, u32[]{:S(2)}, u32[]{:S(2)}) collective-permute-start(bf16[1,256,256]{2,1,0:T(8,128)(2,1)S(1)} %fusion.40), channel_id=1, source_target_pairs={{0,4},{1,3},{2,6},{3,1},{4,0},{5,7},{6,2},{7,5},{8,12},{9,11},{10,... | collective-permute-start | bytes 393224 | tf_op jit(solution)/shard_map/ppermute | solution.py:23
  91.9 13.0 %collective-permute-start.24 = (bf16[4,256,256]{2,1,0:T(8,128)(2,1)S(1)}, bf16[4,256,256]{2,1,0:T(8,128)(2,1)S(1)}, u32[]{:S(2)}, u32[]{:S(2)}) collective-permute-start(bf16[4,256,256]{2,1,0:T(8,128)(2,1)S(1)} %pad_maximum_fusion.5.first_ref), channel_id=1, source_target_pairs={{0,1},{1,0},{2,3},{3,2},{4,5},{5,4},{6,7},{7,6},{8,9},{9,8},{10,11... | collective-permute-start | bytes 1572872 | tf_op jit(solution)/shard_map/ppermute | solution.py:23
  103.1 13.5 %collective-permute-start.12 = (bf16[2,256,896]{2,1,0:T(8,128)(2,1)S(1)}, bf16[2,256,896]{2,1,0:T(8,128)(2,1)S(1)}, u32[]{:S(2)}, u32[]{:S(2)}) collective-permute-start(bf16[2,256,896]{2,1,0:T(8,128)(2,1)S(1)} %get-tuple-element.23), channel_id=1, source_target_pairs={{0,8},{1,17},{2,10},{3,19},{4,12},{5,21},{6,14},{7,23},{8,0},{9,25... | collective-permute-start | bytes 2752520 | tf_op jit(solution)/shard_map/ppermute | solution.py:23
  110.9 20.4 %collective-permute-start.25 = (bf16[2,256,896]{2,1,0:T(8,128)(2,1)S(1)}, bf16[2,256,896]{2,1,0:T(8,128)(2,1)S(1)}, u32[]{:S(2)}, u32[]{:S(2)}) collective-permute-start(bf16[2,256,896]{2,1,0:T(8,128)(2,1)S(1)} %get-tuple-element.27), channel_id=1, source_target_pairs={{0,8},{1,17},{2,10},{3,19},{4,12},{5,21},{6,14},{7,23},{8,0},{9,25... | collective-permute-start | bytes 2752520 | tf_op jit(solution)/shard_map/ppermute | solution.py:23
  116.7 17.3 %collective-permute-start.13 = (bf16[1,256,896]{2,1,0:T(8,128)(2,1)S(1)}, bf16[1,256,896]{2,1,0:T(8,128)(2,1)S(1)}, u32[]{:S(2)}, u32[]{:S(2)}) collective-permute-start(bf16[1,256,896]{2,1,0:T(8,128)(2,1)S(1)} %add_convert_fusion.3), channel_id=1, source_target_pairs={{0,16},{1,9},{2,18},{3,11},{4,20},{5,13},{6,22},{7,15},{8,24},{9,1... | collective-permute-start | bytes 1376264 | tf_op jit(solution)/shard_map/ppermute | solution.py:23
  134.2 11.2 %collective-permute-start.14 = (bf16[1,256,896]{2,1,0:T(8,128)(2,1)S(1)}, bf16[1,256,896]{2,1,0:T(8,128)(2,1)S(1)}, u32[]{:S(2)}, u32[]{:S(2)}) collective-permute-start(bf16[1,256,896]{2,1,0:T(8,128)(2,1)S(1)} %add_convert_fusion.2), channel_id=1, source_target_pairs={{0,16},{1,9},{2,18},{3,11},{4,20},{5,13},{6,22},{7,15},{8,24},{9,1... | collective-permute-start | bytes 1376264 | tf_op jit(solution)/shard_map/ppermute | solution.py:23
  140.6 12.5 %collective-permute-start.27 = (bf16[1,256,896]{2,1,0:T(8,128)(2,1)S(1)}, bf16[1,256,896]{2,1,0:T(8,128)(2,1)S(1)}, u32[]{:S(2)}, u32[]{:S(2)}) collective-permute-start(bf16[1,256,896]{2,1,0:T(8,128)(2,1)S(1)} %add_convert_fusion), channel_id=1, source_target_pairs={{0,16},{1,9},{2,18},{3,11},{4,20},{5,13},{6,22},{7,15},{8,24},{9,1... | collective-permute-start | bytes 1376264 | tf_op jit(solution)/shard_map/ppermute | solution.py:23
  145.5 13.5 %collective-permute-start.15 = (bf16[2,256,896]{2,1,0:T(8,128)(2,1)S(1)}, bf16[2,256,896]{2,1,0:T(8,128)(2,1)S(1)}, u32[]{:S(2)}, u32[]{:S(2)}) collective-permute-start(bf16[2,256,896]{2,1,0:T(8,128)(2,1)S(1)} %pad_maximum_fusion.1.first_ref), channel_id=1, source_target_pairs={{0,8},{1,17},{2,10},{3,19},{4,12},{5,21},{6,14},{7,23},{8,0},{9,25... | collective-permute-start | bytes 2752520 | tf_op jit(solution)/shard_map/ppermute | solution.py:23
  153.3 15.5 %collective-permute-start.28 = (bf16[2,256,896]{2,1,0:T(8,128)(2,1)S(1)}, bf16[2,256,896]{2,1,0:T(8,128)(2,1)S(1)}, u32[]{:S(2)}, u32[]{:S(2)}) collective-permute-start(bf16[2,256,896]{2,1,0:T(8,128)(2,1)S(1)} %pad_maximum_fusion.2.first_ref), channel_id=1, source_target_pairs={{0,8},{1,17},{2,10},{3,19},{4,12},{5,21},{6,14},{7,23},{8,0},{9,25... | collective-permute-start | bytes 2752520 | tf_op jit(solution)/shard_map/ppermute | solution.py:23
  164.7 10.9 %collective-permute-start.16 = (bf16[4,256,256]{2,1,0:T(8,128)(2,1)S(1)}, bf16[4,256,256]{2,1,0:T(8,128)(2,1)S(1)}, u32[]{:S(2)}, u32[]{:S(2)}) collective-permute-start(bf16[4,256,256]{2,1,0:T(8,128)(2,1)S(1)} %get-tuple-element.25), channel_id=1, source_target_pairs={{0,1},{1,0},{2,3},{3,2},{4,5},{5,4},{6,7},{7,6},{8,9},{9,8},{10,11... | collective-permute-start | bytes 1572872 | tf_op jit(solution)/shard_map/ppermute | solution.py:23
  177.2 16.1 %collective-permute-start.30 = (bf16[2,256,256]{2,1,0:T(8,128)(2,1)S(1)}, bf16[2,256,256]{2,1,0:T(8,128)(2,1)S(1)}, u32[]{:S(2)}, u32[]{:S(2)}) collective-permute-start(bf16[2,256,256]{2,1,0:T(8,128)(2,1)S(1)} %add_convert_fusion.4), channel_id=1, source_target_pairs={{0,2},{1,5},{2,0},{3,7},{4,6},{5,1},{6,4},{7,3},{8,10},{9,13},{10,... | collective-permute-start | bytes 786440 | tf_op jit(solution)/shard_map/ppermute | solution.py:23
  193.7 17.1 %collective-permute-start.19 = (bf16[1,256,256]{2,1,0:T(8,128)(2,1)S(1)}, bf16[1,256,256]{2,1,0:T(8,128)(2,1)S(1)}, u32[]{:S(2)}, u32[]{:S(2)}) collective-permute-start(bf16[1,256,256]{2,1,0:T(8,128)(2,1)S(1)} %add_convert_fusion.8), channel_id=1, source_target_pairs={{0,4},{1,3},{2,6},{3,1},{4,0},{5,7},{6,2},{7,5},{8,12},{9,11},{10,... | collective-permute-start | bytes 393224 | tf_op jit(solution)/shard_map/ppermute | solution.py:23
  200.4 13.2 %collective-permute-start.32 = (bf16[1,256,256]{2,1,0:T(8,128)(2,1)S(1)}, bf16[1,256,256]{2,1,0:T(8,128)(2,1)S(1)}, u32[]{:S(2)}, u32[]{:S(2)}) collective-permute-start(bf16[1,256,256]{2,1,0:T(8,128)(2,1)S(1)} %add_convert_fusion.6), channel_id=1, source_target_pairs={{0,4},{1,3},{2,6},{3,1},{4,0},{5,7},{6,2},{7,5},{8,12},{9,11},{10,... | collective-permute-start | bytes 393224 | tf_op jit(solution)/shard_map/ppermute | solution.py:23
  210.9 9.4 %collective-permute-start.20 = (bf16[2,256,256]{2,1,0:T(8,128)(2,1)S(1)}, bf16[2,256,256]{2,1,0:T(8,128)(2,1)S(1)}, u32[]{:S(2)}, u32[]{:S(2)}) collective-permute-start(bf16[2,256,256]{2,1,0:T(8,128)(2,1)S(1)} %pad_maximum_fusion.11), channel_id=1, source_target_pairs={{0,2},{1,5},{2,0},{3,7},{4,6},{5,1},{6,4},{7,3},{8,10},{9,13},{10,... | collective-permute-start | bytes 786440 | tf_op jit(solution)/shard_map/ppermute | solution.py:23
  213.7 9.4 %collective-permute-start.33 = (bf16[2,256,256]{2,1,0:T(8,128)(2,1)S(1)}, bf16[2,256,256]{2,1,0:T(8,128)(2,1)S(1)}, u32[]{:S(2)}, u32[]{:S(2)}) collective-permute-start(bf16[2,256,256]{2,1,0:T(8,128)(2,1)S(1)} %pad_maximum_fusion.13), channel_id=1, source_target_pairs={{0,2},{1,5},{2,0},{3,7},{4,6},{5,1},{6,4},{7,3},{8,10},{9,13},{10,... | collective-permute-start | bytes 786440 | tf_op jit(solution)/shard_map/ppermute | solution.py:23
  281.6 23.3 %collective-permute-start.38 = (bf16[2,128,3584]{2,1,0:T(8,128)(2,1)S(1)}, bf16[2,128,3584]{2,1,0:T(8,128)(2,1)S(1)}, u32[]{:S(2)}, u32[]{:S(2)}) collective-permute-start(bf16[2,128,3584]{2,1,0:T(8,128)(2,1)S(1)} %bitcast.70), channel_id=1, source_target_pairs={{0,8},{1,17},{2,10},{3,19},{4,12},{5,21},{6,14},{7,23},{8,0},{9,25... | collective-permute-start | bytes 5505032 | tf_op jit(solution)/shard_map/ppermute | solution.py:23
  305.2 13.5 %collective-permute-start.39 = (bf16[1,128,3584]{2,1,0:T(8,128)(2,1)S(1)}, bf16[1,128,3584]{2,1,0:T(8,128)(2,1)S(1)}, u32[]{:S(2)}, u32[]{:S(2)}) collective-permute-start(bf16[1,128,3584]{2,1,0:T(8,128)(2,1)S(1)} %fusion.6), channel_id=1, source_target_pairs={{0,16},{1,9},{2,18},{3,11},{4,20},{5,13},{6,22},{7,15},{8,24},{9,1... | collective-permute-start | bytes 2752520 | tf_op jit(solution)/shard_map/ppermute | solution.py:23
  (31 other events, 221.2 us)

commit v8 on v7

--- a/solution.py
+++ b/solution.py
@@ -302,7 +302,7 @@
     )(gram)
 
 
-LIMIT = 16 << 20
+LIMIT = 10 << 20
 
 
 def dot(left, right, dims=((1,), (0,))):

time: 321 us -> 323 us (level)
  starting transfers between devices: 49.3 us -> 43 us
  local copies, waits for them, and re-layouts: 16.9 us -> 22.1 us
    ppermute x40, starting transfers between devices: 49.3 us -> 43 us  [swap(): return lax.ppermute(block, AXES, pairs)]
    unnamed x31 -> x41, local copies, waits for them, and re-layouts: 16.1 us -> 21.3 us
    ppermute x40, waiting for transfers between devices: 153 us -> 156 us  [swap(): return lax.ppermute(block, AXES, pairs)]
where the time goes in v8:
time: 323 us; the launch traced here: 322 us
  waiting for transfers between devices  156 us (48%)
  Pallas kernels  79.2 us (25%)
  starting transfers between devices  43 us (13%)
  local copies, waits for them, and re-layouts  22.1 us (7%)
  other arithmetic  12.5 us (4%)
  matrix products  7.31 us (2%)
    ppermute x40, waiting for transfers between devices, swap(): return lax.ppermute(block, AXES, pairs)  156 us
    ppermute x40, starting transfers between devices, swap(): return lax.ppermute(block, AXES, pairs)  43 us
    pallas_call x6, Pallas kernels, product_call(): pl.pallas_call(kernel, out_shape=out_shape, in_specs=[smem] * len(indices...  37.3 us
    pallas_call x1, Pallas kernels, inverse_factor(): pl.pallas_call(inverse_factor_kernel, out_shape=jax.ShapeDtypeStruct((siz...  21.3 us
    unnamed x41, local copies, waits for them, and re-layouts  21.3 us
    pallas_call x2, Pallas kernels, rank_times(): pl.pallas_call(rank_kernel, out_shape=jax.ShapeDtypeStruct((basis.shape[0...  9.91 us
    dot_general x8, matrix products, dot(): lax.dot_general(left, right, (dims, ((), ())), preferred_element_type=F32)  7.31 us
    pallas_call x1, Pallas kernels, local_mass(): pl.pallas_call(row_mass_kernel, out_shape=jax.ShapeDtypeStruct((1, width)...  7.31 us
  transfers between devices with their start and end apart: 40, of which 29 were waited for; matrix products, arithmetic and copies ran while one was open for 4% of the time, Pallas kernels for 14%

profile of v8, /device:TPU:0, one launch (start us, length us, event | category | flops | bytes accessed | tf_op | source)
XLA Modules:
  0.0 322.5 jit_solution(3289205651697911535)
XLA Ops:
  0.7 5.2 %copy-done = bf16[2048,3584]{1,0:T(8,128)(2,1)S(1)} copy-done((bf16[2048,3584]{1,0:T(8,128)(2,1)S(1)}, bf16[2048,3584]{1,0:T(8,128)(2,1)}, u32[]{:S(2)}) %copy-start) | copy-done | bytes 14680088
  8.0 7.0 %rows_times.3 = (f32[4,256,256]{2,1,0:T(8,128)}, f32[4,256,256]{2,1,0:T(8,128)S(1)}) custom-call(s32[8]{0:T(128)S(1)} %stack.36.order_ref.rows_ref, bf16[2048,3584]{1,0:T(8,128)(2,1)S(1)} %copy-done, bf16[3584,512]{1,0:T(8,128)(2,1)S(1)} %copy-done.3), custom_call_target="tpu_custom_call" | custom-call | flops 3758096384 | bytes 16515072 | tf_op jit(solution)/shard_map/rows_times/pallas_call | solution.py:334
  15.5 7.1 %rows_times.2 = (f32[4,256,256]{2,1,0:T(8,128)}, f32[4,256,256]{2,1,0:T(8,128)S(1)}) custom-call(s32[8]{0:T(128)S(1)} %stack.36.order_ref.rows_ref, bf16[2048,3584]{1,0:T(8,128)(2,1)S(1)} %copy-done, bf16[3584,512]{1,0:T(8,128)(2,1)S(1)} %copy-done.3), custom_call_target="tpu_custom_call" | custom-call | flops 3758096384 | bytes 16515072 | tf_op jit(solution)/shard_map/rows_times/pallas_call | solution.py:334
  25.3 7.3 %row_mass.1 = f32[1,8192]{1,0:T(1,128)S(1)} custom-call(bf16[2,256,8192]{2,1,0:T(8,128)(2,1)S(1)} %bitcast.75, bf16[2,512,256]{2,1,0:T(8,128)(2,1)S(1)} %get-tuple-element.17.gram_ref, f32[2,256,128]{2,1,0:T(8,128)S(1)} %get-tuple-element.18.scale_ref), custom_call_target="tpu_custom_call" | custom-call | flops 4294967296 | bytes 8388608 | tf_op jit(solution)/shard_map/row_mass/pallas_call | solution.py:195
  40.6 5.5 %collective-permute-done.7 = bf16[2,256,256]{2,1,0:T(8,128)(2,1)S(1)} collective-permute-done((bf16[2,256,256]{2,1,0:T(8,128)(2,1)S(1)}, bf16[2,256,256]{2,1,0:T(8,128)(2,1)S(1)}, u32[]{:S(2)}, u32[]{:S(2)}) %collective-permute-start.7) | collective-permute-done | bytes 262176 | tf_op jit(solution)/shard_map/ppermute | solution.py:23
  77.1 8.2 %collective-permute-done.22 = bf16[1,256,256]{2,1,0:T(8,128)(2,1)S(1)} collective-permute-done((bf16[1,256,256]{2,1,0:T(8,128)(2,1)S(1)}, bf16[1,256,256]{2,1,0:T(8,128)(2,1)S(1)}, u32[]{:S(2)}, u32[]{:S(2)}) %collective-permute-start.22) | collective-permute-done | bytes 131104 | tf_op jit(solution)/shard_map/ppermute | solution.py:23
  86.5 5.3 %collective-permute-done.23 = bf16[2,256,256]{2,1,0:T(8,128)(2,1)S(1)} collective-permute-done((bf16[2,256,256]{2,1,0:T(8,128)(2,1)S(1)}, bf16[2,256,256]{2,1,0:T(8,128)(2,1)S(1)}, u32[]{:S(2)}, u32[]{:S(2)}) %collective-permute-start.23) | collective-permute-done | bytes 262176 | tf_op jit(solution)/shard_map/ppermute | solution.py:23
  92.1 5.2 %copy-done.1 = bf16[2048,3584]{1,0:T(8,128)(2,1)S(1)} copy-done((bf16[2048,3584]{1,0:T(8,128)(2,1)S(1)}, bf16[2048,3584]{1,0:T(8,128)(2,1)}, u32[]{:S(2)}) %copy-start.1) | copy-done | bytes 14680088
  97.2 5.8 %cols_times_joined.2 = (bf16[2,256,896]{2,1,0:T(8,128)(2,1)S(1)}, f32[2,256,896]{2,1,0:T(8,128)S(1)}) custom-call(s32[4]{0:T(128)S(1)} %pad_add_fusion.cols_ref, s32[8]{0:T(128)S(1)} %stack.36.order_ref.rows_ref, bf16[2048,3584]{1,0:T(8,128)(2,1)S(1)} %copy-done.1, f32[1,2048]{1,0:T(1,128)S(1)} %bitcast.73, ...), custom_call_target="tpu_custom_call" | custom-call | flops 3758096384 | bytes 16515072 | tf_op jit(solution)/shard_map/cols_times_joined/pallas_call | solution.py:334
  110.1 6.0 %cols_times_joined.3 = (bf16[2,256,896]{2,1,0:T(8,128)(2,1)S(1)}, f32[2,256,896]{2,1,0:T(8,128)S(1)}) custom-call(s32[4]{0:T(128)S(1)} %pad_add_fusion.cols_ref, s32[8]{0:T(128)S(1)} %stack.36.order_ref.rows_ref, bf16[2048,3584]{1,0:T(8,128)(2,1)S(1)} %copy-done.2, f32[1,2048]{1,0:T(1,128)S(1)} %broadcast_in_dim_broadcast_in_dim.3.scale_ref, ...), custom_call_target="tpu_custom_call" | custom-call | flops 3758096384 | bytes 16515072 | tf_op jit(solution)/shard_map/cols_times_joined/pallas_call | solution.py:334
  119.3 15.2 %collective-permute-done.25 = bf16[2,256,896]{2,1,0:T(8,128)(2,1)S(1)} collective-permute-done((bf16[2,256,896]{2,1,0:T(8,128)(2,1)S(1)}, bf16[2,256,896]{2,1,0:T(8,128)(2,1)S(1)}, u32[]{:S(2)}, u32[]{:S(2)}) %collective-permute-start.25) | collective-permute-done | bytes 917536 | tf_op jit(solution)/shard_map/ppermute | solution.py:23
  136.9 6.2 %collective-permute-done.26 = bf16[1,256,896]{2,1,0:T(8,128)(2,1)S(1)} collective-permute-done((bf16[1,256,896]{2,1,0:T(8,128)(2,1)S(1)}, bf16[1,256,896]{2,1,0:T(8,128)(2,1)S(1)}, u32[]{:S(2)}, u32[]{:S(2)}) %collective-permute-start.26) | collective-permute-done | bytes 458784 | tf_op jit(solution)/shard_map/ppermute | solution.py:23
  149.0 7.9 %collective-permute-done.27 = bf16[1,256,896]{2,1,0:T(8,128)(2,1)S(1)} collective-permute-done((bf16[1,256,896]{2,1,0:T(8,128)(2,1)S(1)}, bf16[1,256,896]{2,1,0:T(8,128)(2,1)S(1)}, u32[]{:S(2)}, u32[]{:S(2)}) %collective-permute-start.27) | collective-permute-done | bytes 458784 | tf_op jit(solution)/shard_map/ppermute | solution.py:23
  162.0 5.7 %rows_times_joined.2 = (bf16[4,256,256]{2,1,0:T(8,128)(2,1)S(1)}, f32[4,256,256]{2,1,0:T(8,128)S(1)}) custom-call(s32[8]{0:T(128)S(1)} %stack.36.order_ref.rows_ref, s32[4]{0:T(128)S(1)} %pad_add_fusion.cols_ref, bf16[2048,3584]{1,0:T(8,128)(2,1)S(1)} %bitcast.68, bf16[2,256,896]{2,1,0:T(8,128)(2,1)S(1)} %pad_maximum_fusion.1.first_ref, ...), custom_call_target="tpu_custom_call" | custom-call | flops 3758096384 | bytes 16515072 | tf_op jit(solution)/shard_map/rows_times_joined/pallas_call | solution.py:334
  171.8 5.7 %rows_times_joined.3 = (bf16[4,256,256]{2,1,0:T(8,128)(2,1)S(1)}, f32[4,256,256]{2,1,0:T(8,128)S(1)}) custom-call(s32[8]{0:T(128)S(1)} %stack.36.order_ref.rows_ref, s32[4]{0:T(128)S(1)} %pad_add_fusion.cols_ref, bf16[2048,3584]{1,0:T(8,128)(2,1)S(1)} %bitcast.68, bf16[2,256,896]{2,1,0:T(8,128)(2,1)S(1)} %pad_maximum_fusion.2.first_ref, ...), custom_call_target="tpu_custom_call" | custom-call | flops 3758096384 | bytes 16515072 | tf_op jit(solution)/shard_map/rows_times_joined/pallas_call | solution.py:334
  180.5 7.0 %collective-permute-done.17 = bf16[2,256,256]{2,1,0:T(8,128)(2,1)S(1)} collective-permute-done((bf16[2,256,256]{2,1,0:T(8,128)(2,1)S(1)}, bf16[2,256,256]{2,1,0:T(8,128)(2,1)S(1)}, u32[]{:S(2)}, u32[]{:S(2)}) %collective-permute-start.17) | collective-permute-done | bytes 262176 | tf_op jit(solution)/shard_map/ppermute | solution.py:23
  188.2 7.8 %collective-permute-done.30 = bf16[2,256,256]{2,1,0:T(8,128)(2,1)S(1)} collective-permute-done((bf16[2,256,256]{2,1,0:T(8,128)(2,1)S(1)}, bf16[2,256,256]{2,1,0:T(8,128)(2,1)S(1)}, u32[]{:S(2)}, u32[]{:S(2)}) %collective-permute-start.30) | collective-permute-done | bytes 262176 | tf_op jit(solution)/shard_map/ppermute | solution.py:23
  203.5 10.3 %collective-permute-done.19 = bf16[1,256,256]{2,1,0:T(8,128)(2,1)S(1)} collective-permute-done((bf16[1,256,256]{2,1,0:T(8,128)(2,1)S(1)}, bf16[1,256,256]{2,1,0:T(8,128)(2,1)S(1)}, u32[]{:S(2)}, u32[]{:S(2)}) %collective-permute-start.19) | collective-permute-done | bytes 131104 | tf_op jit(solution)/shard_map/ppermute | solution.py:23
  216.7 5.8 %collective-permute-done.20 = bf16[2,256,256]{2,1,0:T(8,128)(2,1)S(1)} collective-permute-done((bf16[2,256,256]{2,1,0:T(8,128)(2,1)S(1)}, bf16[2,256,256]{2,1,0:T(8,128)(2,1)S(1)}, u32[]{:S(2)}, u32[]{:S(2)}) %collective-permute-start.20) | collective-permute-done | bytes 262176 | tf_op jit(solution)/shard_map/ppermute | solution.py:23
  235.0 8.0 %collective-permute-done.35 = f32[256,512]{1,0:T(8,128)S(1)} collective-permute-done((f32[256,512]{1,0:T(8,128)S(1)}, f32[256,512]{1,0:T(8,128)S(1)}, u32[]{:S(2)}, u32[]{:S(2)}) %collective-permute-start.35) | collective-permute-done | bytes 524320 | tf_op jit(solution)/shard_map/ppermute | solution.py:23
  245.3 7.2 %collective-permute-done.36 = f32[256,512]{1,0:T(8,128)S(1)} collective-permute-done((f32[256,512]{1,0:T(8,128)S(1)}, f32[256,512]{1,0:T(8,128)S(1)}, u32[]{:S(2)}, u32[]{:S(2)}) %collective-permute-start.36) | collective-permute-done | bytes 524320 | tf_op jit(solution)/shard_map/ppermute | solution.py:23
  255.9 21.3 %inverse_factor.1 = f32[512,512]{1,0:T(8,128)S(1)} custom-call(f32[512,512]{1,0:T(8,128)S(1)} %pad_maximum_fusion.gram_ref), custom_call_target="tpu_custom_call" | custom-call | flops 5368709120 | bytes 2097152 | tf_op jit(solution)/shard_map/inverse_factor/pallas_call | solution.py:291
  291.5 15.6 %collective-permute-done.38 = bf16[2,128,3584]{2,1,0:T(8,128)(2,1)S(1)} collective-permute-done((bf16[2,128,3584]{2,1,0:T(8,128)(2,1)S(1)}, bf16[2,128,3584]{2,1,0:T(8,128)(2,1)S(1)}, u32[]{:S(2)}, u32[]{:S(2)}) %collective-permute-start.38) | collective-permute-done | bytes 1835040 | tf_op jit(solution)/shard_map/ppermute | solution.py:23
  311.0 9.9 %collective-permute-done.39 = bf16[1,128,3584]{2,1,0:T(8,128)(2,1)S(1)} collective-permute-done((bf16[1,128,3584]{2,1,0:T(8,128)(2,1)S(1)}, bf16[1,128,3584]{2,1,0:T(8,128)(2,1)S(1)}, u32[]{:S(2)}, u32[]{:S(2)}) %collective-permute-start.39) | collective-permute-done | bytes 917536 | tf_op jit(solution)/shard_map/ppermute | solution.py:23
  (168 shorter events, 124.3 us)
Async XLA Ops:
  15.0 20.3 %collective-permute-start.6 = (f32[4,256,256]{2,1,0:T(8,128)}, f32[4,256,256]{2,1,0:T(8,128)}, u32[]{:S(2)}, u32[]{:S(2)}) collective-permute-start(f32[4,256,256]{2,1,0:T(8,128)} %get-tuple-element.21), channel_id=1, source_target_pairs={{0,1},{1,0},{2,3},{3,2},{4,5},{5,4},{6,7},{7,6},{8,9},{9,8},{10,11... | collective-permute-start | bytes 3145736 | tf_op jit(solution)/shard_map/ppermute | solution.py:23
  22.5 16.9 %collective-permute-start.1 = (f32[4,256,256]{2,1,0:T(8,128)}, f32[4,256,256]{2,1,0:T(8,128)}, u32[]{:S(2)}, u32[]{:S(2)}) collective-permute-start(f32[4,256,256]{2,1,0:T(8,128)} %get-tuple-element.19), channel_id=1, source_target_pairs={{0,1},{1,0},{2,3},{3,2},{4,5},{5,4},{6,7},{7,6},{8,9},{9,8},{10,11... | collective-permute-start | bytes 3145736 | tf_op jit(solution)/shard_map/ppermute | solution.py:23
  36.4 9.8 %collective-permute-start.7 = (bf16[2,256,256]{2,1,0:T(8,128)(2,1)S(1)}, bf16[2,256,256]{2,1,0:T(8,128)(2,1)S(1)}, u32[]{:S(2)}, u32[]{:S(2)}) collective-permute-start(bf16[2,256,256]{2,1,0:T(8,128)(2,1)S(1)} %fusion.19), channel_id=1, source_target_pairs={{0,2},{1,5},{2,0},{3,7},{4,6},{5,1},{6,4},{7,3},{8,10},{9,13},{10,... | collective-permute-start | bytes 786440 | tf_op jit(solution)/shard_map/ppermute | solution.py:23
  40.6 14.7 %collective-permute-start.2 = (bf16[576,256]{1,0:T(8,128)(2,1)S(1)}, bf16[576,256]{1,0:T(8,128)(2,1)S(1)}, u32[]{:S(2)}, u32[]{:S(2)}) collective-permute-start(bf16[576,256]{1,0:T(8,128)(2,1)S(1)} %pad_maximum_fusion.9), channel_id=1, source_target_pairs={{0,2},{1,5},{2,0},{3,7},{4,6},{5,1},{6,4},{7,3},{8,10},{9,13},{10,... | collective-permute-start | bytes 884744 | tf_op jit(solution)/shard_map/ppermute | solution.py:23
  47.2 10.5 %collective-permute-start.8 = (bf16[1,256,256]{2,1,0:T(8,128)(2,1)S(1)}, bf16[1,256,256]{2,1,0:T(8,128)(2,1)S(1)}, u32[]{:S(2)}, u32[]{:S(2)}) collective-permute-start(bf16[1,256,256]{2,1,0:T(8,128)(2,1)S(1)} %fusion.31), channel_id=1, source_target_pairs={{0,4},{1,3},{2,6},{3,1},{4,0},{5,7},{6,2},{7,5},{8,12},{9,11},{10,... | collective-permute-start | bytes 393224 | tf_op jit(solution)/shard_map/ppermute | solution.py:23
  58.7 11.9 %collective-permute-start.9 = (bf16[1,256,256]{2,1,0:T(8,128)(2,1)S(1)}, bf16[1,256,256]{2,1,0:T(8,128)(2,1)S(1)}, u32[]{:S(2)}, u32[]{:S(2)}) collective-permute-start(bf16[1,256,256]{2,1,0:T(8,128)(2,1)S(1)} %fusion.34), channel_id=1, source_target_pairs={{0,4},{1,3},{2,6},{3,1},{4,0},{5,7},{6,2},{7,5},{8,12},{9,11},{10,... | collective-permute-start | bytes 393224 | tf_op jit(solution)/shard_map/ppermute | solution.py:23
  70.7 15.7 %collective-permute-start.10 = (bf16[2,256,256]{2,1,0:T(8,128)(2,1)S(1)}, bf16[2,256,256]{2,1,0:T(8,128)(2,1)S(1)}, u32[]{:S(2)}, u32[]{:S(2)}) collective-permute-start(bf16[2,256,256]{2,1,0:T(8,128)(2,1)S(1)} %pad_maximum_fusion.10), channel_id=1, source_target_pairs={{0,2},{1,5},{2,0},{3,7},{4,6},{5,1},{6,4},{7,3},{8,10},{9,13},{10,... | collective-permute-start | bytes 786440 | tf_op jit(solution)/shard_map/ppermute | solution.py:23
  74.9 10.4 %collective-permute-start.22 = (bf16[1,256,256]{2,1,0:T(8,128)(2,1)S(1)}, bf16[1,256,256]{2,1,0:T(8,128)(2,1)S(1)}, u32[]{:S(2)}, u32[]{:S(2)}) collective-permute-start(bf16[1,256,256]{2,1,0:T(8,128)(2,1)S(1)} %fusion.40), channel_id=1, source_target_pairs={{0,4},{1,3},{2,6},{3,1},{4,0},{5,7},{6,2},{7,5},{8,12},{9,11},{10,... | collective-permute-start | bytes 393224 | tf_op jit(solution)/shard_map/ppermute | solution.py:23
  91.9 13.0 %collective-permute-start.24 = (bf16[4,256,256]{2,1,0:T(8,128)(2,1)S(1)}, bf16[4,256,256]{2,1,0:T(8,128)(2,1)S(1)}, u32[]{:S(2)}, u32[]{:S(2)}) collective-permute-start(bf16[4,256,256]{2,1,0:T(8,128)(2,1)S(1)} %pad_maximum_fusion.5.first_ref), channel_id=1, source_target_pairs={{0,1},{1,0},{2,3},{3,2},{4,5},{5,4},{6,7},{7,6},{8,9},{9,8},{10,11... | collective-permute-start | bytes 1572872 | tf_op jit(solution)/shard_map/ppermute | solution.py:23
  103.0 13.5 %collective-permute-start.12 = (bf16[2,256,896]{2,1,0:T(8,128)(2,1)S(1)}, bf16[2,256,896]{2,1,0:T(8,128)(2,1)S(1)}, u32[]{:S(2)}, u32[]{:S(2)}) collective-permute-start(bf16[2,256,896]{2,1,0:T(8,128)(2,1)S(1)} %get-tuple-element.23), channel_id=1, source_target_pairs={{0,8},{1,17},{2,10},{3,19},{4,12},{5,21},{6,14},{7,23},{8,0},{9,25... | collective-permute-start | bytes 2752520 | tf_op jit(solution)/shard_map/ppermute | solution.py:23
  116.1 18.4 %collective-permute-start.25 = (bf16[2,256,896]{2,1,0:T(8,128)(2,1)S(1)}, bf16[2,256,896]{2,1,0:T(8,128)(2,1)S(1)}, u32[]{:S(2)}, u32[]{:S(2)}) collective-permute-start(bf16[2,256,896]{2,1,0:T(8,128)(2,1)S(1)} %get-tuple-element.27), channel_id=1, source_target_pairs={{0,8},{1,17},{2,10},{3,19},{4,12},{5,21},{6,14},{7,23},{8,0},{9,25... | collective-permute-start | bytes 2752520 | tf_op jit(solution)/shard_map/ppermute | solution.py:23
  116.6 20.0 %collective-permute-start.13 = (bf16[1,256,896]{2,1,0:T(8,128)(2,1)S(1)}, bf16[1,256,896]{2,1,0:T(8,128)(2,1)S(1)}, u32[]{:S(2)}, u32[]{:S(2)}) collective-permute-start(bf16[1,256,896]{2,1,0:T(8,128)(2,1)S(1)} %add_convert_fusion.3), channel_id=1, source_target_pairs={{0,16},{1,9},{2,18},{3,11},{4,20},{5,13},{6,22},{7,15},{8,24},{9,1... | collective-permute-start | bytes 1376264 | tf_op jit(solution)/shard_map/ppermute | solution.py:23
  136.8 11.2 %collective-permute-start.14 = (bf16[1,256,896]{2,1,0:T(8,128)(2,1)S(1)}, bf16[1,256,896]{2,1,0:T(8,128)(2,1)S(1)}, u32[]{:S(2)}, u32[]{:S(2)}) collective-permute-start(bf16[1,256,896]{2,1,0:T(8,128)(2,1)S(1)} %add_convert_fusion.2), channel_id=1, source_target_pairs={{0,16},{1,9},{2,18},{3,11},{4,20},{5,13},{6,22},{7,15},{8,24},{9,1... | collective-permute-start | bytes 1376264 | tf_op jit(solution)/shard_map/ppermute | solution.py:23
  143.3 13.6 %collective-permute-start.27 = (bf16[1,256,896]{2,1,0:T(8,128)(2,1)S(1)}, bf16[1,256,896]{2,1,0:T(8,128)(2,1)S(1)}, u32[]{:S(2)}, u32[]{:S(2)}) collective-permute-start(bf16[1,256,896]{2,1,0:T(8,128)(2,1)S(1)} %add_convert_fusion), channel_id=1, source_target_pairs={{0,16},{1,9},{2,18},{3,11},{4,20},{5,13},{6,22},{7,15},{8,24},{9,1... | collective-permute-start | bytes 1376264 | tf_op jit(solution)/shard_map/ppermute | solution.py:23
  148.1 13.8 %collective-permute-start.15 = (bf16[2,256,896]{2,1,0:T(8,128)(2,1)S(1)}, bf16[2,256,896]{2,1,0:T(8,128)(2,1)S(1)}, u32[]{:S(2)}, u32[]{:S(2)}) collective-permute-start(bf16[2,256,896]{2,1,0:T(8,128)(2,1)S(1)} %pad_maximum_fusion.1.first_ref), channel_id=1, source_target_pairs={{0,8},{1,17},{2,10},{3,19},{4,12},{5,21},{6,14},{7,23},{8,0},{9,25... | collective-permute-start | bytes 2752520 | tf_op jit(solution)/shard_map/ppermute | solution.py:23
  157.0 14.7 %collective-permute-start.28 = (bf16[2,256,896]{2,1,0:T(8,128)(2,1)S(1)}, bf16[2,256,896]{2,1,0:T(8,128)(2,1)S(1)}, u32[]{:S(2)}, u32[]{:S(2)}) collective-permute-start(bf16[2,256,896]{2,1,0:T(8,128)(2,1)S(1)} %pad_maximum_fusion.2.first_ref), channel_id=1, source_target_pairs={{0,8},{1,17},{2,10},{3,19},{4,12},{5,21},{6,14},{7,23},{8,0},{9,25... | collective-permute-start | bytes 2752520 | tf_op jit(solution)/shard_map/ppermute | solution.py:23
  167.7 10.5 %collective-permute-start.16 = (bf16[4,256,256]{2,1,0:T(8,128)(2,1)S(1)}, bf16[4,256,256]{2,1,0:T(8,128)(2,1)S(1)}, u32[]{:S(2)}, u32[]{:S(2)}) collective-permute-start(bf16[4,256,256]{2,1,0:T(8,128)(2,1)S(1)} %get-tuple-element.25), channel_id=1, source_target_pairs={{0,1},{1,0},{2,3},{3,2},{4,5},{5,4},{6,7},{7,6},{8,9},{9,8},{10,11... | collective-permute-start | bytes 1572872 | tf_op jit(solution)/shard_map/ppermute | solution.py:23
  179.8 16.2 %collective-permute-start.30 = (bf16[2,256,256]{2,1,0:T(8,128)(2,1)S(1)}, bf16[2,256,256]{2,1,0:T(8,128)(2,1)S(1)}, u32[]{:S(2)}, u32[]{:S(2)}) collective-permute-start(bf16[2,256,256]{2,1,0:T(8,128)(2,1)S(1)} %add_convert_fusion.4), channel_id=1, source_target_pairs={{0,2},{1,5},{2,0},{3,7},{4,6},{5,1},{6,4},{7,3},{8,10},{9,13},{10,... | collective-permute-start | bytes 786440 | tf_op jit(solution)/shard_map/ppermute | solution.py:23
  196.2 17.6 %collective-permute-start.19 = (bf16[1,256,256]{2,1,0:T(8,128)(2,1)S(1)}, bf16[1,256,256]{2,1,0:T(8,128)(2,1)S(1)}, u32[]{:S(2)}, u32[]{:S(2)}) collective-permute-start(bf16[1,256,256]{2,1,0:T(8,128)(2,1)S(1)} %add_convert_fusion.8), channel_id=1, source_target_pairs={{0,4},{1,3},{2,6},{3,1},{4,0},{5,7},{6,2},{7,5},{8,12},{9,11},{10,... | collective-permute-start | bytes 393224 | tf_op jit(solution)/shard_map/ppermute | solution.py:23
  203.1 13.5 %collective-permute-start.32 = (bf16[1,256,256]{2,1,0:T(8,128)(2,1)S(1)}, bf16[1,256,256]{2,1,0:T(8,128)(2,1)S(1)}, u32[]{:S(2)}, u32[]{:S(2)}) collective-permute-start(bf16[1,256,256]{2,1,0:T(8,128)(2,1)S(1)} %add_convert_fusion.6), channel_id=1, source_target_pairs={{0,4},{1,3},{2,6},{3,1},{4,0},{5,7},{6,2},{7,5},{8,12},{9,11},{10,... | collective-permute-start | bytes 393224 | tf_op jit(solution)/shard_map/ppermute | solution.py:23
  233.8 9.2 %collective-permute-start.35 = (f32[256,512]{1,0:T(8,128)S(1)}, f32[256,512]{1,0:T(8,128)S(1)}, u32[]{:S(2)}, u32[]{:S(2)}) collective-permute-start(f32[256,512]{1,0:T(8,128)S(1)} %convolution_add_fusion.2), channel_id=1, source_target_pairs={{0,8},{1,17},{2,10},{3,19},{4,12},{5,21},{6,14},{7,23},{8,0},{9,25... | collective-permute-start | bytes 1572872 | tf_op jit(solution)/shard_map/ppermute | solution.py:23
  243.1 9.3 %collective-permute-start.36 = (f32[256,512]{1,0:T(8,128)S(1)}, f32[256,512]{1,0:T(8,128)S(1)}, u32[]{:S(2)}, u32[]{:S(2)}) collective-permute-start(f32[256,512]{1,0:T(8,128)S(1)} %add.231), channel_id=1, source_target_pairs={{0,16},{1,9},{2,18},{3,11},{4,20},{5,13},{6,22},{7,15},{8,24},{9,1... | collective-permute-start | bytes 1572872 | tf_op jit(solution)/shard_map/ppermute | solution.py:23
  283.9 23.3 %collective-permute-start.38 = (bf16[2,128,3584]{2,1,0:T(8,128)(2,1)S(1)}, bf16[2,128,3584]{2,1,0:T(8,128)(2,1)S(1)}, u32[]{:S(2)}, u32[]{:S(2)}) collective-permute-start(bf16[2,128,3584]{2,1,0:T(8,128)(2,1)S(1)} %bitcast.72), channel_id=1, source_target_pairs={{0,8},{1,17},{2,10},{3,19},{4,12},{5,21},{6,14},{7,23},{8,0},{9,25... | collective-permute-start | bytes 5505032 | tf_op jit(solution)/shard_map/ppermute | solution.py:23
  307.4 13.5 %collective-permute-start.39 = (bf16[1,128,3584]{2,1,0:T(8,128)(2,1)S(1)}, bf16[1,128,3584]{2,1,0:T(8,128)(2,1)S(1)}, u32[]{:S(2)}, u32[]{:S(2)}) collective-permute-start(bf16[1,128,3584]{2,1,0:T(8,128)(2,1)S(1)} %fusion.6), channel_id=1, source_target_pairs={{0,16},{1,9},{2,18},{3,11},{4,20},{5,13},{6,22},{7,15},{8,24},{9,1... | collective-permute-start | bytes 2752520 | tf_op jit(solution)/shard_map/ppermute | solution.py:23
  (36 other events, 407.0 us)
